TPU v7x, 32 devices: a whole 2x2x4 slice. The times are simulated.
32 devices in a mesh: group: 4 (over y, x), det: 4 (over z), tm: 2 (over core).
Axes of the slice: x: 2, y: 2, z: 4, core: 2. Of those that a mesh axis runs over, the one named last changes fastest.
Arguments:
- map_solution: float32 [3, 4, 64, 128], P(None, 'det', ('group', 'tm')), may hold values from -6 to 6
- map_residual: float32 [3, 4, 64, 128], P(None, 'det', ('group', 'tm')), may hold values from -6 to 6
- map_direction: float32 [3, 4, 64, 128], P(None, 'det', ('group', 'tm')), may hold values from -6 to 6
- hits: int32 [256, 256], P(('group', 'det'), 'tm'), may hold values from 0 to 192, as said below
- stokes_int: int32 [2, 256, 32768], P(None, ('group', 'det'), 'tm'), may hold values from -2047 to 2047
- inv_noise: float32 [256, 512], P(('group', 'det')), may hold values from 0.2 to 2
Outputs:
- new_solution: float32 [3, 4, 64, 128], P(None, 'det', ('group', 'tm'))
- new_residual: float32 [3, 4, 64, 128], P(None, 'det', ('group', 'tm'))
- new_direction: float32 [3, 4, 64, 128], P(None, 'det', ('group', 'tm'))
Inputs may be any that keep to these rules, and one draw needn't show every extreme that they name: `hits`: A value below 192 names a pixel block in the sky tile of the detector's det index or in one of its two neighbours along det, as the steps say; the value 192 marks a flagged block.
All inputs are finite; a program needn't handle non-finite values.
Results may differ from a plain program's by a relative error of at most 0.0003.
Values sent between devices are 32-bit elements; how exact they have to be, the bound alone decides.
No kernel may reach another device: no remote copies, remote signals or barrier semaphores. Data moves between devices by JAX's collectives and lax.ppermute only.
A program may use at most 64 MiB of HBM per device.

v0:
```python
import functools
import math

import jax
import jax.numpy as jnp
import numpy as np
from jax import lax
from jax.experimental import pallas as pl
from jax.experimental.pallas import tpu as pltpu
from jax.sharding import PartitionSpec as P

WIN = 1024
LANES = 128
SEG = WIN // 2
HALF = SEG // 2
PER_SEG = SEG // LANES
BF = jnp.bfloat16
F32 = jnp.float32


def split(value):
    high = value.astype(BF)
    return high, (value - high.astype(F32)).astype(BF)


def np_split(value):
    value = np.asarray(value, np.float32)
    high = value.astype(jnp.bfloat16)
    return high, (value - high.astype(np.float32)).astype(jnp.bfloat16)


def trig_table(samples, frequencies, length, with_ends):
    n = np.arange(samples)[:, None]
    cos_f = np.asarray(frequencies)
    sin_f = np.asarray([f for f in frequencies if not (with_ends and f in (0, length // 2))])
    angle = 2.0 * math.pi / length
    cos_t = np.cos(angle * ((n * cos_f[None, :]) % length))
    sin_t = np.sin(angle * ((n * sin_f[None, :]) % length))
    scale = np.full(len(cos_f), math.sqrt(2.0 / samples))
    if with_ends:
        scale[(cos_f == 0) | (cos_f == length // 2)] = math.sqrt(1.0 / samples)
    return np.concatenate([cos_t * scale, sin_t * math.sqrt(2.0 / samples)], axis=1), np.concatenate([cos_f, sin_f])


def tables():
    ee, ee_f = trig_table(HALF, np.arange(0, SEG + 1, 4), WIN, True)
    eo, eo_f = trig_table(HALF, np.arange(2, SEG, 4), WIN, False)
    od, od_f = trig_table(SEG, np.arange(1, SEG, 2), WIN, False)
    return (ee, ee_f), (eo, eo_f), (od, od_f)


def dot(a, b):
    return lax.dot_general(a, b, (((1,), (0,)), ((), ())), preferred_element_type=F32)


def dot_t(a, b):
    return lax.dot_general(a, b, (((1,), (1,)), ((), ())), preferred_element_type=F32)


def dot3(op, value, high, low):
    vh, vl = split(value)
    return op(vh, high) + (op(vl, high) + op(vh, low))


def main_kernel(
    groups, times, low, own, high, hits, stokes, left, right, wee, weo, wod,
    g1h, g1l, g2h, g2l, sh, sl, out, mh, ml, onehot, x, f,
):
    rows, blocks = hits.shape
    tile_blocks = own.shape[1]
    local = 3 * tile_blocks
    depth = mh.shape[0]
    segs = blocks // PER_SEG
    chunk_segs = 4
    chunk_blocks = chunk_segs * PER_SEG
    chunk = chunk_blocks * rows
    scale = 1.0 / 2048.0

    if depth > local:
        mh[pl.ds(local, depth - local), :] = jnp.zeros((depth - local, 3 * LANES), BF)
        ml[pl.ds(local, depth - local), :] = jnp.zeros((depth - local, 3 * LANES), BF)
    for t, ref in enumerate((low, own, high)):
        for c in range(3):
            part_h, part_l = split(ref[c])
            mh[pl.ds(t * tile_blocks, tile_blocks), pl.ds(c * LANES, LANES)] = part_h
            ml[pl.ds(t * tile_blocks, tile_blocks), pl.ds(c * LANES, LANES)] = part_l

    ids = lax.broadcasted_iota(jnp.int32, (rows, depth), 1)

    def rows_of(column):
        return jnp.where(jnp.broadcast_to(column, (rows, depth)) == ids, 1.0, 0.0).astype(BF)

    def scan(picked, j, q_int, u_int):
        part = picked[j * rows:(j + 1) * rows]
        q = q_int.astype(F32) * scale
        u = u_int.astype(F32) * scale
        return part[:, :LANES] + q * part[:, LANES:2 * LANES] + u * part[:, 2 * LANES:]

    for side, at in ((left, 0), (right, (segs + 1) * rows)):
        flags = side[:, 2 * SEG:] - 1
        ones = jnp.concatenate([rows_of(flags[:, j:j + 1]) for j in range(PER_SEG)], axis=0)
        picked = dot(ones, mh[...]) + dot(ones, ml[...])
        for j in range(PER_SEG):
            x[pl.ds(at, rows), pl.ds(j * LANES, LANES)] = scan(
                picked, j, side[:, j * LANES:(j + 1) * LANES],
                side[:, SEG + j * LANES:SEG + (j + 1) * LANES],
            )

    def scan_chunk(i, carry):
        turned = pltpu.roll(hits[...], blocks - i * chunk_blocks, 1)
        ones = jnp.concatenate([rows_of(turned[:, j:j + 1]) for j in range(chunk_blocks)], axis=0)
        onehot[pl.ds(pl.multiple_of(i * chunk, chunk), chunk), :] = ones
        picked = dot(ones, mh[...]) + dot(ones, ml[...])
        for j in range(chunk_blocks):
            lanes = pl.ds(pl.multiple_of(i * chunk_blocks * LANES, LANES) + j * LANES, LANES)
            at = pl.multiple_of((i * chunk_segs + 1 + j // PER_SEG) * rows, rows)
            x[pl.ds(at, rows), pl.ds((j % PER_SEG) * LANES, LANES)] = scan(
                picked, j, stokes[0, :, lanes], stokes[1, :, lanes]
            )
        return carry

    lax.fori_loop(0, segs // chunk_segs, scan_chunk, 0)

    part_segs = 16
    part = part_segs * rows

    def weighted(coeffs, weights):
        return (coeffs.reshape(part_segs, rows, -1) * weights[...][None]).reshape(part, -1)

    def filter_part(i, carry):
        at = pl.multiple_of(i * part, part)
        middle = x[pl.ds(at + rows, part), :]
        around = 0.5 * (x[pl.ds(at, part), :] + x[pl.ds(at + 2 * rows, part), :])
        even = middle + around
        odd = middle - around
        coeffs = weighted(dot3(dot, even[:, :HALF] + even[:, HALF:], g1h[...], g1l[...]), wee)
        first = dot3(dot_t, coeffs, g1h[...], g1l[...])
        coeffs = weighted(dot3(dot, even[:, :HALF] - even[:, HALF:], g2h[...], g2l[...]), weo)
        second = dot3(dot_t, coeffs, g2h[...], g2l[...])
        coeffs = weighted(dot3(dot, odd, sh[...], sl[...]), wod)
        third = dot3(dot_t, coeffs, sh[...], sl[...])
        f[pl.ds(at, part), :HALF] = first + second + third[:, :HALF]
        f[pl.ds(at, part), HALF:] = first - second + third[:, HALF:]
        return carry

    lax.fori_loop(0, segs // part_segs, filter_part, 0)

    def bin_chunk(i, total):
        values = []
        for j in range(chunk_blocks):
            lanes = pl.ds(pl.multiple_of(i * chunk_blocks * LANES, LANES) + j * LANES, LANES)
            at = pl.multiple_of((i * chunk_segs + j // PER_SEG) * rows, rows)
            value = f[pl.ds(at, rows), pl.ds((j % PER_SEG) * LANES, LANES)]
            q = stokes[0, :, lanes].astype(F32) * scale
            u = stokes[1, :, lanes].astype(F32) * scale
            values.append(jnp.concatenate([value, q * value, u * value], axis=1))
        vh, vl = split(jnp.concatenate(values, axis=0))
        ones = onehot[pl.ds(pl.multiple_of(i * chunk, chunk), chunk), :]
        over = (((0,), (0,)), ((), ()))
        return total + (
            lax.dot_general(ones, vh, over, preferred_element_type=F32)
            + lax.dot_general(ones, vl, over, preferred_element_type=F32)
        )

    total = lax.fori_loop(0, segs // chunk_segs, bin_chunk, jnp.zeros((depth, 3 * LANES), F32))
    width = tile_blocks // (groups * times)
    for t in range(3):
        for g in range(groups):
            for k in range(times):
                start = t * tile_blocks + (g * times + k) * width
                out[k, t, g] = total[start:start + width]


def scan_filter_bin(low, own, high, hits, stokes, left, right, inv_noise, groups, times):
    rows, samples = stokes.shape[1:]
    blocks = samples // LANES
    tile_blocks = own.shape[1]
    depth = -(-3 * tile_blocks // 256) * 256
    (ee, ee_f), (eo, eo_f), (od, od_f) = tables()
    g1h, g1l = np_split(ee)
    g2h, g2l = np_split(eo)
    sh, sl = np_split(od)
    last = inv_noise.shape[1] - 1
    wee = 0.5 * jnp.concatenate([inv_noise[:, 0::4], inv_noise[:, last:], inv_noise[:, 4::4]], axis=1)
    weo = 0.5 * jnp.concatenate([inv_noise[:, 2::4], inv_noise[:, 2::4]], axis=1)
    wod = jnp.concatenate([inv_noise[:, 1::2], inv_noise[:, 1::2]], axis=1)
    width = tile_blocks // (groups * times)
    vmem = pl.BlockSpec(memory_space=pltpu.VMEM)
    return pl.pallas_call(
        functools.partial(main_kernel, groups, times),
        out_shape=jax.ShapeDtypeStruct((times, 3, groups, width, 3 * LANES), F32),
        in_specs=[vmem] * 16,
        out_specs=vmem,
        scratch_shapes=[
            pltpu.VMEM((depth, 3 * LANES), BF),
            pltpu.VMEM((depth, 3 * LANES), BF),
            pltpu.VMEM((rows * blocks, depth), BF),
            pltpu.VMEM(((blocks // PER_SEG + 2) * rows, SEG), F32),
            pltpu.VMEM((blocks // PER_SEG * rows, SEG), F32),
        ],
        compiler_params=pltpu.CompilerParams(vmem_limit_bytes=48 * 2**20),
    )(low, own, high, hits, stokes, left, right, wee, weo, wod, g1h, g1l, g2h, g2l, sh, sl)


def turned(axis, by):
    count = lax.axis_size(axis)
    return [(i, (i + by) % count) for i in range(count)]


def scatter_sum(parts, axis):
    count = lax.axis_size(axis)
    me = lax.axis_index(axis)
    total = lax.dynamic_index_in_dim(parts, me, 0, keepdims=False)
    for by in range(1, count):
        sent = lax.dynamic_index_in_dim(parts, (me + by) % count, 0, keepdims=False)
        total = total + lax.ppermute(sent, axis, turned(axis, by))
    return total


def direct_sum(value, axis):
    total = value
    for by in range(1, lax.axis_size(axis)):
        total = total + lax.ppermute(value, axis, turned(axis, by))
    return total


def edge(stokes_int, hits, end):
    if end:
        stokes, flags = stokes_int[:, :, -SEG:], hits[:, -PER_SEG:]
    else:
        stokes, flags = stokes_int[:, :, :SEG], hits[:, :PER_SEG]
    flags = jnp.pad(flags + 1, ((0, 0), (0, LANES - PER_SEG)))
    return jnp.concatenate([stokes[0], stokes[1], flags], axis=1)


def shards(map_solution, map_residual, map_direction, hits, stokes_int, inv_noise):
    times = lax.axis_size("tm")
    groups = lax.axis_size("group")
    forward = [(i, i + 1) for i in range(times - 1)]
    left = lax.ppermute(edge(stokes_int, hits, True), "tm", forward)
    right = lax.ppermute(edge(stokes_int, hits, False), "tm", [(b, a) for a, b in forward])
    tile = lax.all_gather(map_direction, ("group", "tm"), axis=2, tiled=True)[:, 0]
    low = lax.ppermute(tile, "det", turned("det", 1))
    high = lax.ppermute(tile, "det", turned("det", -1))
    binned = scan_filter_bin(low, tile, high, hits, stokes_int, left, right, inv_noise, groups, times)
    half = scatter_sum(binned, "tm")
    image = (
        half[1]
        + lax.ppermute(half[2], "det", turned("det", 1))
        + lax.ppermute(half[0], "det", turned("det", -1))
    )
    image = scatter_sum(image, "group")
    map_image = jnp.stack([image[:, c * LANES:(c + 1) * LANES] for c in range(3)])[:, None]
    sums = jnp.stack([
        jnp.sum(map_residual * map_residual),
        jnp.sum(map_direction * map_image),
        jnp.sum(map_residual * map_image),
        jnp.sum(map_image * map_image),
    ])
    for axis in ("tm", "group", "det"):
        sums = direct_sum(sums, axis)
    old_norm, curvature, cross_term, image_norm = sums
    step_size = old_norm / curvature
    new_residual = map_residual - step_size * map_image
    new_norm = old_norm - 2.0 * step_size * cross_term + step_size * step_size * image_norm
    new_solution = map_solution + step_size * map_direction
    new_direction = new_residual + new_norm / old_norm * map_direction
    return (new_solution, new_residual, new_direction)


def solution(mesh):
    map_placed = P(None, "det", ("group", "tm"), None)
    placed = (
        map_placed,
        map_placed,
        map_placed,
        P(("group", "det"), "tm"),
        P(None, ("group", "det"), "tm"),
        P(("group", "det"), None),
    )
    return jax.shard_map(
        shards,
        mesh=mesh,
        in_specs=placed,
        out_specs=(map_placed, map_placed, map_placed),
        check_vma=False,
    )
```

profile of v0, /device:TPU:0, one launch (start us, length us, event | category | flops | bytes accessed | tf_op | source)
XLA Modules:
  0.0 85.5 jit_solution(15969444431581231761)
XLA Ops:
  0.6 10.8 %all_gather.3 = f32[3,1,64,128]{3,2,0,1:T(8,128)S(1)} all-gather(f32[3,1,8,128]{3,2,0,1:T(8,128)} %bitcast.70), channel_id=1, replica_groups=mesh['group'=4,'det'=4,'tm'=2] {'group','tm'}, dimensions={2}, use_global_device_ids=true | all-gather | bytes 110592 | tf_op jit(solution)/shard_map/all_gather | solution.py:242
  11.4 1.6 %collective-permute-start = (f32[3,64,128]{2,1,0:T(8,128)S(1)}, f32[3,64,128]{2,1,0:T(8,128)S(1)}, u32[]{:S(2)}, u32[]{:S(2)}) collective-permute-start(f32[3,64,128]{2,1,0:T(8,128)S(1)} %bitcast.67), channel_id=1, source_target_pairs={{0,2},{2,4},{4,6},{6,0},{1,3},{3,5},{5,7},{7,1},{8,10},{10,12},{12... | collective-permute-start | bytes 294920 | tf_op jit(solution)/shard_map/ppermute | solution.py:243
  13.0 2.2 %collective-permute-start.1 = (f32[3,64,128]{2,1,0:T(8,128)S(1)}, f32[3,64,128]{2,1,0:T(8,128)S(1)}, u32[]{:S(2)}, u32[]{:S(2)}) collective-permute-start(f32[3,64,128]{2,1,0:T(8,128)S(1)} %bitcast.68), channel_id=1, source_target_pairs={{0,6},{2,0},{4,2},{6,4},{1,7},{3,1},{5,3},{7,5},{8,14},{10,8},{12,... | collective-permute-start | bytes 294920 | tf_op jit(solution)/shard_map/ppermute | solution.py:244
  16.9 1.8 %collective-permute-start.2 = (s32[16,1152]{1,0:T(8,128)S(1)}, s32[16,1152]{1,0:T(8,128)S(1)}, u32[]{:S(2)}, u32[]{:S(2)}) collective-permute-start(s32[16,1152]{1,0:T(8,128)S(1)} %pad_add_fusion.1), channel_id=1, source_target_pairs={{0,1},{2,3},{4,5},{6,7},{8,9},{10,11},{12,13},{14,15},{16,17},{18,... | collective-permute-start | bytes 221192 | tf_op jit(solution)/shard_map/ppermute | solution.py:240
  18.7 1.3 %collective-permute-start.3 = (s32[16,1152]{1,0:T(8,128)S(1)}, s32[16,1152]{1,0:T(8,128)S(1)}, u32[]{:S(2)}, u32[]{:S(2)}) collective-permute-start(s32[16,1152]{1,0:T(8,128)S(1)} %pad_add_fusion), channel_id=1, source_target_pairs={{1,0},{3,2},{5,4},{7,6},{9,8},{11,10},{13,12},{15,14},{17,16},{19,... | collective-permute-start | bytes 221192 | tf_op jit(solution)/shard_map/ppermute | solution.py:241
  24.1 1.4 %slice.69 = f32[16,256]{1,0:T(8,128)S(1)} slice(f32[16,512]{1,0:T(8,128)} %param.17), slice={[0:16:1], [1:512:2]} | slice | bytes 32768 | tf_op jit(solution)/shard_map/slice | solution.py:186
  25.6 1.6 %copy-done = s32[2,16,16384]{2,1,0:T(8,128)S(1)} copy-done((s32[2,16,16384]{2,1,0:T(8,128)S(1)}, s32[2,16,16384]{2,1,0:T(8,128)}, u32[]{:S(2)}) %copy-start) | copy-done | bytes 2097176
  33.6 9.8 %shard_map.139 = f32[2,3,4,8,384]{4,3,2,1,0:T(8,128)S(1)} custom-call(f32[3,64,128]{2,1,0:T(8,128)S(1)} %collective-permute-done.low, f32[3,64,128]{2,1,0:T(8,128)S(1)} %bitcast.69, f32[3,64,128]{2,1,0:T(8,128)S(1)} %collective-permute-done.1.high, s32[16,128]{1,0:T(8,128)S(1)} %copy-done.7, s32[2,16,16384]{2,1,0:T(8,128)S(1)} %copy-done, ...), custom_call_target="tpu_custom_call" | custom-call | tf_op jit(solution)/shard_map/pallas_call | solution.py:189
  43.5 1.2 %collective-permute-start.4 = (f32[3,4,8,384]{3,2,1,0:T(8,128)S(1)}, f32[3,4,8,384]{3,2,1,0:T(8,128)S(1)}, u32[]{:S(2)}, u32[]{:S(2)}) collective-permute-start(f32[3,4,8,384]{3,2,1,0:T(8,128)S(1)} %dynamic-slice_bitcast_fusion), channel_id=1, source_target_pairs={{0,1},{1,0},{2,3},{3,2},{4,5},{5,4},{6,7},{7,6},{8,9},{9,8},{10,11... | collective-permute-start | bytes 442376 | tf_op jit(solution)/shard_map/ppermute | solution.py:216
  45.7 1.8 %collective-permute-start.6 = (f32[4,8,384]{2,1,0:T(8,128)S(1)}, f32[4,8,384]{2,1,0:T(8,128)S(1)}, u32[]{:S(2)}, u32[]{:S(2)}) collective-permute-start(f32[4,8,384]{2,1,0:T(8,128)S(1)} %get-tuple-element.12), channel_id=1, source_target_pairs={{0,6},{2,0},{4,2},{6,4},{1,7},{3,1},{5,3},{7,5},{8,14},{10,8},{12,... | collective-permute-start | bytes 147464 | tf_op jit(solution)/shard_map/ppermute | solution.py:250
  47.8 2.1 %collective-permute-done.6 = f32[4,8,384]{2,1,0:T(8,128)S(1)} collective-permute-done((f32[4,8,384]{2,1,0:T(8,128)S(1)}, f32[4,8,384]{2,1,0:T(8,128)S(1)}, u32[]{:S(2)}, u32[]{:S(2)}) %collective-permute-start.6) | collective-permute-done | bytes 49184 | tf_op jit(solution)/shard_map/ppermute | solution.py:250
  49.9 3.5 %collective-permute-done.5 = f32[4,8,384]{2,1,0:T(8,128)S(1)} collective-permute-done((f32[4,8,384]{2,1,0:T(8,128)S(1)}, f32[4,8,384]{2,1,0:T(8,128)S(1)}, u32[]{:S(2)}, u32[]{:S(2)}) %collective-permute-start.5) | collective-permute-done | bytes 49184 | tf_op jit(solution)/shard_map/ppermute | solution.py:249
  53.4 1.4 %collective-permute-start.9 = (f32[8,384]{1,0:T(8,128)S(1)}, f32[8,384]{1,0:T(8,128)S(1)}, u32[]{:S(2)}, u32[]{:S(2)}) collective-permute-start(f32[8,384]{1,0:T(8,128)S(1)} %get-tuple-element.14), channel_id=1, source_target_pairs={{0,24},{8,0},{16,8},{24,16},{1,25},{9,1},{17,9},{25,17},{2,26},{10... | collective-permute-start | bytes 36872 | tf_op jit(solution)/shard_map/ppermute | solution.py:216
  54.8 1.5 %collective-permute-start.8 = (f32[8,384]{1,0:T(8,128)S(1)}, f32[8,384]{1,0:T(8,128)S(1)}, u32[]{:S(2)}, u32[]{:S(2)}) collective-permute-start(f32[8,384]{1,0:T(8,128)S(1)} %get-tuple-element.15), channel_id=1, source_target_pairs={{0,16},{8,24},{16,0},{24,8},{1,17},{9,25},{17,1},{25,9},{2,18},{10... | collective-permute-start | bytes 36872 | tf_op jit(solution)/shard_map/ppermute | solution.py:216
  58.5 2.4 %collective-permute-done.7 = f32[8,384]{1,0:T(8,128)S(1)} collective-permute-done((f32[8,384]{1,0:T(8,128)S(1)}, f32[8,384]{1,0:T(8,128)S(1)}, u32[]{:S(2)}, u32[]{:S(2)}) %collective-permute-start.7) | collective-permute-done | bytes 12320 | tf_op jit(solution)/shard_map/ppermute | solution.py:216
  62.1 2.7 %pad_maximum_fusion.2 = f32[4]{0:T(128)S(1)} fusion(f32[1]{0:T(128)} %bitcast.26, f32[1]{0:T(128)} %bitcast.22, f32[1]{0:T(128)} %bitcast.20, f32[1]{0:T(128)} %bitcast), kind=kLoop, calls=%fused_computation.40 | loop fusion | flops 12 | bytes 32 | tf_op jit(solution)/shard_map/stack | solution.py:254
  64.8 1.1 %collective-permute-done.10 = f32[4]{0:T(128)S(1)} collective-permute-done((f32[4]{0:T(128)S(1)}, f32[4]{0:T(128)S(1)}, u32[]{:S(2)}, u32[]{:S(2)}) %collective-permute-start.10) | collective-permute-done | bytes 48 | tf_op jit(solution)/shard_map/ppermute | solution.py:223
  65.9 2.7 %fusion.6 = f32[4]{0:T(128)S(1)} fusion(f32[4]{0:T(128)S(1)} %collective-permute-done.10, f32[1]{0:T(128)} %bitcast.26, f32[1]{0:T(128)} %bitcast.22, f32[1]{0:T(128)} %bitcast.20, f32[1]{0:T(128)} %bitcast), kind=kLoop, calls=%fused_computation.44 | loop fusion | flops 16 | bytes 48 | tf_op jit(solution)/shard_map/add | solution.py:223
  68.6 1.1 %collective-permute-start.12 = (f32[4]{0:T(128)S(1)}, f32[4]{0:T(128)S(1)}, u32[]{:S(2)}, u32[]{:S(2)}) collective-permute-start(f32[4]{0:T(128)S(1)} %fusion.6), channel_id=1, source_target_pairs={{0,16},{8,24},{16,0},{24,8},{1,17},{9,25},{17,1},{25,9},{2,18},{10... | collective-permute-start | bytes 56 | tf_op jit(solution)/shard_map/ppermute | solution.py:223
  69.8 1.4 %collective-permute-start.11 = (f32[4]{0:T(128)S(1)}, f32[4]{0:T(128)S(1)}, u32[]{:S(2)}, u32[]{:S(2)}) collective-permute-start(f32[4]{0:T(128)S(1)} %fusion.6), channel_id=1, source_target_pairs={{0,8},{8,16},{16,24},{24,0},{1,9},{9,17},{17,25},{25,1},{2,10},{10... | collective-permute-start | bytes 56 | tf_op jit(solution)/shard_map/ppermute | solution.py:223
  72.2 2.0 %collective-permute-done.11 = f32[4]{0:T(128)S(1)} collective-permute-done((f32[4]{0:T(128)S(1)}, f32[4]{0:T(128)S(1)}, u32[]{:S(2)}, u32[]{:S(2)}) %collective-permute-start.11) | collective-permute-done | bytes 48 | tf_op jit(solution)/shard_map/ppermute | solution.py:223
  74.8 1.4 %collective-permute-start.14 = (f32[4]{0:T(128)S(1)}, f32[4]{0:T(128)S(1)}, u32[]{:S(2)}, u32[]{:S(2)}) collective-permute-start(f32[4]{0:T(128)S(1)} %add_add_fusion.1), channel_id=1, source_target_pairs={{0,2},{2,4},{4,6},{6,0},{1,3},{3,5},{5,7},{7,1},{8,10},{10,12},{12... | collective-permute-start | bytes 56 | tf_op jit(solution)/shard_map/ppermute | solution.py:223
  76.2 1.5 %collective-permute-done.16 = f32[4]{0:T(128)S(1)} collective-permute-done((f32[4]{0:T(128)S(1)}, f32[4]{0:T(128)S(1)}, u32[]{:S(2)}, u32[]{:S(2)}) %collective-permute-start.16) | collective-permute-done | bytes 48 | tf_op jit(solution)/shard_map/ppermute | solution.py:223
  77.7 1.3 %collective-permute-done.15 = f32[4]{0:T(128)S(1)} collective-permute-done((f32[4]{0:T(128)S(1)}, f32[4]{0:T(128)S(1)}, u32[]{:S(2)}, u32[]{:S(2)}) %collective-permute-start.15) | collective-permute-done | bytes 48 | tf_op jit(solution)/shard_map/ppermute | solution.py:223
  (61 shorter events, 21.0 us)
Async XLA Ops:
  11.4 14.2 %collective-permute-start = (f32[3,64,128]{2,1,0:T(8,128)S(1)}, f32[3,64,128]{2,1,0:T(8,128)S(1)}, u32[]{:S(2)}, u32[]{:S(2)}) collective-permute-start(f32[3,64,128]{2,1,0:T(8,128)S(1)} %bitcast.67), channel_id=1, source_target_pairs={{0,2},{2,4},{4,6},{6,0},{1,3},{3,5},{5,7},{7,1},{8,10},{10,12},{12... | collective-permute-start | bytes 294920 | tf_op jit(solution)/shard_map/ppermute | solution.py:243
  13.0 12.6 %collective-permute-start.1 = (f32[3,64,128]{2,1,0:T(8,128)S(1)}, f32[3,64,128]{2,1,0:T(8,128)S(1)}, u32[]{:S(2)}, u32[]{:S(2)}) collective-permute-start(f32[3,64,128]{2,1,0:T(8,128)S(1)} %bitcast.68), channel_id=1, source_target_pairs={{0,6},{2,0},{4,2},{6,4},{1,7},{3,1},{5,3},{7,5},{8,14},{10,8},{12,... | collective-permute-start | bytes 294920 | tf_op jit(solution)/shard_map/ppermute | solution.py:244
  16.9 8.6 %collective-permute-start.2 = (s32[16,1152]{1,0:T(8,128)S(1)}, s32[16,1152]{1,0:T(8,128)S(1)}, u32[]{:S(2)}, u32[]{:S(2)}) collective-permute-start(s32[16,1152]{1,0:T(8,128)S(1)} %pad_add_fusion.1), channel_id=1, source_target_pairs={{0,1},{2,3},{4,5},{6,7},{8,9},{10,11},{12,13},{14,15},{16,17},{18,... | collective-permute-start | bytes 221192 | tf_op jit(solution)/shard_map/ppermute | solution.py:240
  18.7 6.8 %collective-permute-start.3 = (s32[16,1152]{1,0:T(8,128)S(1)}, s32[16,1152]{1,0:T(8,128)S(1)}, u32[]{:S(2)}, u32[]{:S(2)}) collective-permute-start(s32[16,1152]{1,0:T(8,128)S(1)} %pad_add_fusion), channel_id=1, source_target_pairs={{1,0},{3,2},{5,4},{7,6},{9,8},{11,10},{13,12},{15,14},{17,16},{19,... | collective-permute-start | bytes 221192 | tf_op jit(solution)/shard_map/ppermute | solution.py:241
  25.6 1.6 %copy-start = (s32[2,16,16384]{2,1,0:T(8,128)S(1)}, s32[2,16,16384]{2,1,0:T(8,128)}, u32[]{:S(2)}) copy-start(s32[2,16,16384]{2,1,0:T(8,128)} %stokes.1) | copy-start | bytes 6291460
  27.2 1.0 %copy-start.1 = (bf16[512,512]{1,0:T(8,128)(2,1)S(1)}, bf16[512,512]{1,0:T(8,128)(2,1)}, u32[]{:S(2)}) copy-start(bf16[512,512]{1,0:T(8,128)(2,1)} %constant.82.clone.sh) | copy-start | bytes 1572868
  28.2 1.0 %copy-start.2 = (bf16[512,512]{1,0:T(8,128)(2,1)S(1)}, bf16[512,512]{1,0:T(8,128)(2,1)}, u32[]{:S(2)}) copy-start(bf16[512,512]{1,0:T(8,128)(2,1)} %constant.83.clone.sl) | copy-start | bytes 1572868
  29.3 0.9 %copy-start.3 = (bf16[256,256]{1,0:T(8,128)(2,1)S(1)}, bf16[256,256]{1,0:T(8,128)(2,1)}, u32[]{:S(2)}) copy-start(bf16[256,256]{1,0:T(8,128)(2,1)} %constant.78.clone.g1h) | copy-start | bytes 393220
  33.6 23.2 %copy-start.9 = (f32[3,1,8,128]{3,2,1,0:T(8,128)S(1)}, f32[3,1,8,128]{3,2,1,0:T(8,128)}, u32[]{:S(2)}) copy-start(f32[3,1,8,128]{3,2,1,0:T(8,128)} %param.13) | copy-start | bytes 36868
  33.6 27.9 %copy-start.8 = (f32[3,1,8,128]{3,2,1,0:T(8,128)S(1)}, f32[3,1,8,128]{3,2,1,0:T(8,128)}, u32[]{:S(2)}) copy-start(f32[3,1,8,128]{3,2,1,0:T(8,128)} %param.14) | copy-start | bytes 36868
  33.6 51.3 %copy-start.10 = (f32[3,1,8,128]{3,2,1,0:T(8,128)S(1)}, f32[3,1,8,128]{3,2,1,0:T(8,128)}, u32[]{:S(2)}) copy-start(f32[3,1,8,128]{3,2,1,0:T(8,128)} %param.12) | copy-start | bytes 36868
  43.5 2.2 %collective-permute-start.4 = (f32[3,4,8,384]{3,2,1,0:T(8,128)S(1)}, f32[3,4,8,384]{3,2,1,0:T(8,128)S(1)}, u32[]{:S(2)}, u32[]{:S(2)}) collective-permute-start(f32[3,4,8,384]{3,2,1,0:T(8,128)S(1)} %dynamic-slice_bitcast_fusion), channel_id=1, source_target_pairs={{0,1},{1,0},{2,3},{3,2},{4,5},{5,4},{6,7},{7,6},{8,9},{9,8},{10,11... | collective-permute-start | bytes 442376 | tf_op jit(solution)/shard_map/ppermute | solution.py:216
  45.7 4.2 %collective-permute-start.6 = (f32[4,8,384]{2,1,0:T(8,128)S(1)}, f32[4,8,384]{2,1,0:T(8,128)S(1)}, u32[]{:S(2)}, u32[]{:S(2)}) collective-permute-start(f32[4,8,384]{2,1,0:T(8,128)S(1)} %get-tuple-element.12), channel_id=1, source_target_pairs={{0,6},{2,0},{4,2},{6,4},{1,7},{3,1},{5,3},{7,5},{8,14},{10,8},{12,... | collective-permute-start | bytes 147464 | tf_op jit(solution)/shard_map/ppermute | solution.py:250
  47.5 5.9 %collective-permute-start.5 = (f32[4,8,384]{2,1,0:T(8,128)S(1)}, f32[4,8,384]{2,1,0:T(8,128)S(1)}, u32[]{:S(2)}, u32[]{:S(2)}) collective-permute-start(f32[4,8,384]{2,1,0:T(8,128)S(1)} %get-tuple-element.11), channel_id=1, source_target_pairs={{0,2},{2,4},{4,6},{6,0},{1,3},{3,5},{5,7},{7,1},{8,10},{10,12},{12... | collective-permute-start | bytes 147464 | tf_op jit(solution)/shard_map/ppermute | solution.py:249
  53.4 4.1 %collective-permute-start.9 = (f32[8,384]{1,0:T(8,128)S(1)}, f32[8,384]{1,0:T(8,128)S(1)}, u32[]{:S(2)}, u32[]{:S(2)}) collective-permute-start(f32[8,384]{1,0:T(8,128)S(1)} %get-tuple-element.14), channel_id=1, source_target_pairs={{0,24},{8,0},{16,8},{24,16},{1,25},{9,1},{17,9},{25,17},{2,26},{10... | collective-permute-start | bytes 36872 | tf_op jit(solution)/shard_map/ppermute | solution.py:216
  54.8 3.7 %collective-permute-start.8 = (f32[8,384]{1,0:T(8,128)S(1)}, f32[8,384]{1,0:T(8,128)S(1)}, u32[]{:S(2)}, u32[]{:S(2)}) collective-permute-start(f32[8,384]{1,0:T(8,128)S(1)} %get-tuple-element.15), channel_id=1, source_target_pairs={{0,16},{8,24},{16,0},{24,8},{1,17},{9,25},{17,1},{25,9},{2,18},{10... | collective-permute-start | bytes 36872 | tf_op jit(solution)/shard_map/ppermute | solution.py:216
  56.3 4.6 %collective-permute-start.7 = (f32[8,384]{1,0:T(8,128)S(1)}, f32[8,384]{1,0:T(8,128)S(1)}, u32[]{:S(2)}, u32[]{:S(2)}) collective-permute-start(f32[8,384]{1,0:T(8,128)S(1)} %get-tuple-element.13), channel_id=1, source_target_pairs={{0,8},{8,16},{16,24},{24,0},{1,9},{9,17},{17,25},{25,1},{2,10},{10... | collective-permute-start | bytes 36872 | tf_op jit(solution)/shard_map/ppermute | solution.py:216
  64.8 1.1 %collective-permute-start.10 = (f32[4]{0:T(128)S(1)}, f32[4]{0:T(128)S(1)}, u32[]{:S(2)}, u32[]{:S(2)}) collective-permute-start(f32[4]{0:T(128)S(1)} %pad_maximum_fusion.2), channel_id=1, source_target_pairs={{0,1},{1,0},{2,3},{3,2},{4,5},{5,4},{6,7},{7,6},{8,9},{9,8},{10,11... | collective-permute-start | bytes 56 | tf_op jit(solution)/shard_map/ppermute | solution.py:223
  68.6 3.5 %collective-permute-start.13 = (f32[4]{0:T(128)S(1)}, f32[4]{0:T(128)S(1)}, u32[]{:S(2)}, u32[]{:S(2)}) collective-permute-start(f32[4]{0:T(128)S(1)} %fusion.6), channel_id=1, source_target_pairs={{0,24},{8,0},{16,8},{24,16},{1,25},{9,1},{17,9},{25,17},{2,26},{10... | collective-permute-start | bytes 56 | tf_op jit(solution)/shard_map/ppermute | solution.py:223
  68.6 3.6 %collective-permute-start.12 = (f32[4]{0:T(128)S(1)}, f32[4]{0:T(128)S(1)}, u32[]{:S(2)}, u32[]{:S(2)}) collective-permute-start(f32[4]{0:T(128)S(1)} %fusion.6), channel_id=1, source_target_pairs={{0,16},{8,24},{16,0},{24,8},{1,17},{9,25},{17,1},{25,9},{2,18},{10... | collective-permute-start | bytes 56 | tf_op jit(solution)/shard_map/ppermute | solution.py:223
  69.8 4.4 %collective-permute-start.11 = (f32[4]{0:T(128)S(1)}, f32[4]{0:T(128)S(1)}, u32[]{:S(2)}, u32[]{:S(2)}) collective-permute-start(f32[4]{0:T(128)S(1)} %fusion.6), channel_id=1, source_target_pairs={{0,8},{8,16},{16,24},{24,0},{1,9},{9,17},{17,25},{25,1},{2,10},{10... | collective-permute-start | bytes 56 | tf_op jit(solution)/shard_map/ppermute | solution.py:223
  74.2 3.5 %collective-permute-start.16 = (f32[4]{0:T(128)S(1)}, f32[4]{0:T(128)S(1)}, u32[]{:S(2)}, u32[]{:S(2)}) collective-permute-start(f32[4]{0:T(128)S(1)} %add_add_fusion.1), channel_id=1, source_target_pairs={{0,6},{2,0},{4,2},{6,4},{1,7},{3,1},{5,3},{7,5},{8,14},{10,8},{12,... | collective-permute-start | bytes 56 | tf_op jit(solution)/shard_map/ppermute | solution.py:223
  74.6 4.4 %collective-permute-start.15 = (f32[4]{0:T(128)S(1)}, f32[4]{0:T(128)S(1)}, u32[]{:S(2)}, u32[]{:S(2)}) collective-permute-start(f32[4]{0:T(128)S(1)} %add_add_fusion.1), channel_id=1, source_target_pairs={{0,4},{2,6},{4,0},{6,2},{1,5},{3,7},{5,1},{7,3},{8,12},{10,14},{12... | collective-permute-start | bytes 56 | tf_op jit(solution)/shard_map/ppermute | solution.py:223
  74.8 5.3 %collective-permute-start.14 = (f32[4]{0:T(128)S(1)}, f32[4]{0:T(128)S(1)}, u32[]{:S(2)}, u32[]{:S(2)}) collective-permute-start(f32[4]{0:T(128)S(1)} %add_add_fusion.1), channel_id=1, source_target_pairs={{0,2},{2,4},{4,6},{6,0},{1,3},{3,5},{5,7},{7,1},{8,10},{10,12},{12... | collective-permute-start | bytes 56 | tf_op jit(solution)/shard_map/ppermute | solution.py:223
  (4 other events, 3.4 us)
where the time goes:
time: 86.5 us; the launch traced here: 85.5 us
  starting transfers between devices  18.2 us (21%)
  waiting for transfers between devices  18 us (21%)
  local copies, waits for them, and re-layouts  14.9 us (17%)
  blocking collectives  10.8 us (12%)
  Pallas kernels  9.83 us (11%)
  other arithmetic  8.9 us (10%)
  between operations  4.92 us (6%)
    all_gather x1, blocking collectives, shards(): lax.all_gather(map_direction, ('group', 'tm'), axis=2, tiled=True)[:, 0]  10.8 us
    pallas_call x1, Pallas kernels, scan_filter_bin(): pl.pallas_call(functools.partial(main_kernel, groups, times), out_shape=j...  9.83 us
    ppermute x7, waiting for transfers between devices, direct_sum(): total = total + lax.ppermute(value, axis, turned(axis, by))  8.05 us
    unnamed x22, local copies, waits for them, and re-layouts  7.99 us
    ppermute x4, starting transfers between devices, scatter_sum(): total = total + lax.ppermute(sent, axis, turned(axis, by))  4.6 us
    ppermute x7, starting transfers between devices, direct_sum(): total = total + lax.ppermute(value, axis, turned(axis, by))  4.59 us
    ppermute x4, waiting for transfers between devices, scatter_sum(): total = total + lax.ppermute(sent, axis, turned(axis, by))  4.36 us
    ppermute x1, waiting for transfers between devices, shards(): lax.ppermute(half[2], 'det', turned('det', 1))  3.52 us
  transfers between devices with their start and end apart: 17, of which 12 were waited for; matrix products, arithmetic and copies ran while one was open for 9% of the time, Pallas kernels for 0%

commit v1 on v0

v1 whole, which is shorter than its diff:
```python
import functools
import math

import jax
import jax.numpy as jnp
import numpy as np
from jax import lax
from jax.experimental import pallas as pl
from jax.experimental.pallas import tpu as pltpu
from jax.sharding import PartitionSpec as P

WIN = 1024
LANES = 128
SEG = WIN // 2
HALF = SEG // 2
PER_SEG = SEG // LANES
BF = jnp.bfloat16
F32 = jnp.float32


def split(value):
    high = value.astype(BF)
    return high, (value - high.astype(F32)).astype(BF)


def np_split(value):
    value = np.asarray(value, np.float32)
    high = value.astype(jnp.bfloat16)
    return high, (value - high.astype(np.float32)).astype(jnp.bfloat16)


def trig_table(samples, frequencies, length, with_ends):
    n = np.arange(samples)[:, None]
    cos_f = np.asarray(frequencies)
    sin_f = np.asarray([f for f in frequencies if not (with_ends and f in (0, length // 2))])
    angle = 2.0 * math.pi / length
    cos_t = np.cos(angle * ((n * cos_f[None, :]) % length))
    sin_t = np.sin(angle * ((n * sin_f[None, :]) % length))
    scale = np.full(len(cos_f), math.sqrt(2.0 / samples))
    if with_ends:
        scale[(cos_f == 0) | (cos_f == length // 2)] = math.sqrt(1.0 / samples)
    return np.concatenate([cos_t * scale, sin_t * math.sqrt(2.0 / samples)], axis=1)


def tables():
    ee = trig_table(HALF, np.arange(0, SEG + 1, 4), WIN, True)
    eo = trig_table(HALF, np.arange(2, SEG, 4), WIN, False)
    odd = trig_table(SEG, np.arange(1, SEG, 2), WIN, False)
    return ee, eo, odd


def dot(a, b):
    return lax.dot_general(a, b, (((1,), (0,)), ((), ())), preferred_element_type=F32)


def dot_t(a, b):
    return lax.dot_general(a, b, (((1,), (1,)), ((), ())), preferred_element_type=F32)


def partner_perm(axis, by):
    count = lax.axis_size(axis)
    if count & (count - 1) == 0:
        return [(i, i ^ by) for i in range(count)]
    return [(i, (i + by) % count) for i in range(count)]


def source_of(axis, by):
    count = lax.axis_size(axis)
    me = lax.axis_index(axis)
    if count & (count - 1) == 0:
        return me ^ by
    return lax.rem(me + count - by, count)


def target_of(axis, by):
    count = lax.axis_size(axis)
    me = lax.axis_index(axis)
    if count & (count - 1) == 0:
        return me ^ by
    return lax.rem(me + by, count)


def tile_perm(exchange):
    count = lax.axis_size("det")
    if count % 2:
        return [(i, (i + 1 - 2 * exchange) % count) for i in range(count)]
    pairs = [(i, (i + 1) % count) for i in range(1 - exchange, count, 2)]
    return sorted(pairs + [(b, a) for a, b in pairs])


def tile_sides(exchange):
    if lax.axis_size("det") % 2:
        return 2 * exchange, 2 - 2 * exchange
    odd = lax.rem(lax.axis_index("det"), 2)
    side = 2 * odd if exchange == 0 else 2 - 2 * odd
    return side, side


def dot3(op, value, high, low):
    vh, vl = split(value)
    return op(vh, high) + (op(vl, high) + op(vh, low))


def edge_kernel(count, hits, stokes, residual, *refs):
    edges_out, residual_out, raw, sems = refs[:count], refs[count], refs[count + 1], refs[count + 2]
    rows, blocks = hits.shape
    samples = stokes.shape[2]
    first = [lax.axis_index("tm") == 1] if count == 1 else [True, False]
    copies = []
    for i in range(count):
        at = jnp.where(first[i], 0, samples - SEG)
        lanes = pl.ds(pl.multiple_of(at, SEG), SEG)
        copies.append(pltpu.make_async_copy(stokes.at[:, :, lanes], raw.at[i], sems.at[i]))
        copies[i].start()
    residual_out[...] = residual[:, 0]
    flags = hits[...].astype(F32) + 1.0
    last_flags = pltpu.roll(flags, PER_SEG, 1)
    for i in range(count):
        edges_out[i][2 * PER_SEG] = jnp.where(first[i], flags, last_flags)
    for i in range(count):
        copies[i].wait()
        for k in range(2):
            for j in range(PER_SEG):
                part = raw[i, k, :, j * LANES:(j + 1) * LANES]
                edges_out[i][k * PER_SEG + j] = part.astype(F32) * (1.0 / 2048.0)


def prep_kernel(
    payload, hits, inv_noise, stokes, tables_in,
    payload_out, weights, onehot, scales, tables_out, raw, sems,
):
    rows, blocks = hits.shape
    depth = onehot.shape[1]
    parts = raw.shape[0]
    width = stokes.shape[2] // parts
    copies = [
        pltpu.make_async_copy(stokes.at[:, :, pl.ds(i * width, width)], raw.at[i], sems.at[i])
        for i in range(parts)
    ]
    copies.append(pltpu.make_async_copy(tables_in, tables_out, sems.at[parts]))
    for copy in copies:
        copy.start()
    payload_out[...] = payload[...]
    ids = lax.broadcasted_iota(jnp.int32, (rows, depth), 1)
    step = 16

    def ones_of(i, carry):
        part = pltpu.roll(hits[...], blocks - i * step, 1)
        for j in range(step):
            column = jnp.broadcast_to(part[:, j:j + 1], (rows, depth))
            at = pl.multiple_of((i * step + j) * rows, rows)
            onehot[pl.ds(at, rows), :] = jnp.where(column == ids, 1.0, 0.0).astype(BF)
        return carry

    lax.fori_loop(0, blocks // step, ones_of, 0)

    freqs = inv_noise.shape[1]
    column = lax.broadcasted_iota(jnp.int32, (1, WIN), 1)
    quarter = HALF // 2
    wanted = jnp.where(
        column < HALF,
        jnp.where(column <= quarter, 4 * column, 4 * (column - quarter)),
        jnp.where(
            column < SEG,
            4 * lax.rem(column, quarter) + 2,
            2 * lax.rem(column, HALF) + 1,
        ),
    )
    wanted = jnp.broadcast_to(jnp.minimum(wanted, freqs - 1), (freqs, WIN))
    held = lax.broadcasted_iota(jnp.int32, (freqs, WIN), 0)
    chosen = jnp.where(wanted == held, 1.0, 0.0).astype(BF)
    both = dot(jnp.concatenate(split(inv_noise[...]), axis=0), chosen)
    scales[...] = both[:rows] + both[rows:]

    for i in range(parts):
        copies[i].wait()
        for k in range(2):
            weights[k, :, pl.ds(i * width, width)] = raw[i, k].astype(F32) * (1.0 / 2048.0)
    copies[parts].wait()


def main_kernel(
    arrived, others, weights, onehot, scales, tables_in, *refs,
):
    sides, (out, window, mh, ml, x, f, total) = refs[:-7], refs[-7:]
    groups = lax.axis_size("group")
    times = lax.axis_size("tm")
    width = arrived.shape[3]
    rows = weights.shape[1]
    blocks = weights.shape[2] // LANES
    tile_blocks = groups * times * width
    depth = mh.shape[0]
    segs = blocks // PER_SEG
    chunk_segs = 4
    chunk_blocks = chunk_segs * PER_SEG
    chunk = chunk_blocks * rows
    tiles = (1, tile_sides(0)[0], tile_sides(1)[0])

    window[...] = jnp.zeros(window.shape, F32)
    for k in range(times):
        for j in range(groups):
            at = (source_of("group", j) * times + source_of("tm", k)) * width
            for s in range(3):
                place = pl.ds(pl.multiple_of(tiles[s] * tile_blocks + at, 8), width)
                for c in range(3):
                    piece = arrived[j, s, c] if k == 0 else others[k - 1, j, s, c]
                    window[place, pl.ds(c * LANES, LANES)] = piece
    mh[...], ml[...] = split(window[...])

    ids = lax.broadcasted_iota(jnp.int32, (rows, depth), 1).astype(F32)

    def scan(picked, j, q, u):
        part = picked[j * rows:(j + 1) * rows]
        return part[:, :LANES] + q * part[:, LANES:2 * LANES] + u * part[:, 2 * LANES:]

    upper_at = (segs + 1) * rows
    for at in (0, upper_at):
        x[pl.ds(at, rows), :] = jnp.zeros((rows, SEG), F32)
    if len(sides) == 1:
        places = (jnp.where(lax.axis_index("tm") == 0, upper_at, 0),)
    else:
        places = (0, upper_at)
    for side, at in zip(sides, places):
        flags = side[2 * PER_SEG] - 1.0
        ones = jnp.concatenate(
            [
                jnp.where(jnp.broadcast_to(flags[:, j:j + 1], (rows, depth)) == ids, 1.0, 0.0)
                for j in range(PER_SEG)
            ],
            axis=0,
        ).astype(BF)
        picked = dot(ones, mh[...]) + dot(ones, ml[...])
        place = pl.ds(at if isinstance(at, int) else pl.multiple_of(at, rows), rows)
        for j in range(PER_SEG):
            x[place, pl.ds(j * LANES, LANES)] = scan(picked, j, side[j], side[PER_SEG + j])

    def scan_chunk(i, carry):
        ones = onehot[pl.ds(pl.multiple_of(i * chunk, chunk), chunk), :]
        picked = dot(ones, mh[...]) + dot(ones, ml[...])
        for j in range(chunk_blocks):
            lanes = pl.ds(pl.multiple_of(i * chunk_blocks * LANES, LANES) + j * LANES, LANES)
            at = pl.multiple_of((i * chunk_segs + 1 + j // PER_SEG) * rows, rows)
            x[pl.ds(at, rows), pl.ds((j % PER_SEG) * LANES, LANES)] = scan(
                picked, j, weights[0, :, lanes], weights[1, :, lanes]
            )
        return carry

    lax.fori_loop(0, segs // chunk_segs, scan_chunk, 0)

    sh = tables_in[:SEG, :]
    sl = tables_in[SEG:2 * SEG, :]
    g1h, g1l = tables_in[2 * SEG:2 * SEG + HALF, :HALF], tables_in[2 * SEG:2 * SEG + HALF, HALF:]
    g2h, g2l = tables_in[2 * SEG + HALF:, :HALF], tables_in[2 * SEG + HALF:, HALF:]
    part_segs = 16
    part = part_segs * rows

    def weighted(coeffs, scale):
        return (coeffs.reshape(part_segs, rows, -1) * scale[None]).reshape(part, -1)

    def filter_part(i, carry):
        at = pl.multiple_of(i * part, part)
        middle = x[pl.ds(at + rows, part), :]
        around = 0.5 * (x[pl.ds(at, part), :] + x[pl.ds(at + 2 * rows, part), :])
        even = middle + around
        odd = middle - around
        coeffs = dot3(dot, even[:, :HALF] + even[:, HALF:], g1h, g1l)
        first = dot3(dot_t, weighted(coeffs, 0.5 * scales[:, :HALF]), g1h, g1l)
        coeffs = dot3(dot, even[:, :HALF] - even[:, HALF:], g2h, g2l)
        second = dot3(dot_t, weighted(coeffs, 0.5 * scales[:, HALF:SEG]), g2h, g2l)
        coeffs = dot3(dot, odd, sh, sl)
        third = dot3(dot_t, weighted(coeffs, scales[:, SEG:]), sh, sl)
        f[pl.ds(at, part), :HALF] = first + second + third[:, :HALF]
        f[pl.ds(at, part), HALF:] = first - second + third[:, HALF:]
        return carry

    lax.fori_loop(0, segs // part_segs, filter_part, 0)

    total[...] = jnp.zeros(total.shape, F32)

    def bin_chunk(i, carry):
        values = []
        for j in range(chunk_blocks):
            lanes = pl.ds(pl.multiple_of(i * chunk_blocks * LANES, LANES) + j * LANES, LANES)
            at = pl.multiple_of((i * chunk_segs + j // PER_SEG) * rows, rows)
            value = f[pl.ds(at, rows), pl.ds((j % PER_SEG) * LANES, LANES)]
            values.append(
                jnp.concatenate(
                    [value, weights[0, :, lanes] * value, weights[1, :, lanes] * value], axis=1
                )
            )
        vh, vl = split(jnp.concatenate(values, axis=0))
        ones = onehot[pl.ds(pl.multiple_of(i * chunk, chunk), chunk), :]
        over = (((0,), (0,)), ((), ()))
        total[...] += (
            lax.dot_general(ones, vh, over, preferred_element_type=F32)
            + lax.dot_general(ones, vl, over, preferred_element_type=F32)
        )
        return carry

    lax.fori_loop(0, segs // chunk_segs, bin_chunk, 0)
    tiles = (1, tile_sides(0)[1], tile_sides(1)[1])
    for k in range(times):
        for s in range(3):
            for g in range(groups):
                at = tiles[s] * tile_blocks + (g * times + target_of("tm", k)) * width
                out[k, s, g] = total[pl.ds(pl.multiple_of(at, 8), width), :]


def sum_kernel(arrived, parts, image, sums):
    groups = arrived.shape[0]
    rows = [jnp.zeros((1, LANES), F32)] * 4
    for j in range(groups):
        g = source_of("group", j)
        pixels = parts[0, g]
        for k in range(1, groups):
            pixels = pixels + parts[k, g]
        for c in range(3):
            a = pixels[:, c * LANES:(c + 1) * LANES]
            d = arrived[j, 0, c]
            r = arrived[j, 3, c]
            if j == 0:
                image[c] = a
            for i, term in enumerate((r * r, d * a, r * a, a * a)):
                rows[i] = rows[i] + jnp.sum(term, axis=0, keepdims=True)
    sums[...] = jnp.concatenate(rows + [jnp.zeros((4, LANES), F32)], axis=0)


def step_kernel(sums, image, arrived, solution_in, new_solution, new_residual, new_direction):
    old_norm, curvature, cross_term, image_norm = [
        jnp.sum(sums[i:i + 1, :], axis=1, keepdims=True) for i in range(4)
    ]
    step_size = old_norm / curvature
    new_norm = old_norm - 2.0 * step_size * cross_term + step_size * step_size * image_norm
    ratio = new_norm / old_norm
    for c in range(3):
        d = arrived[0, 0, c]
        residual = arrived[0, 3, c] - step_size * image[c]
        new_solution[c, 0] = solution_in[c, 0] + step_size * d
        new_residual[c, 0] = residual
        new_direction[c, 0] = residual + ratio * d


def vmem_call(kernel, out_shape, args, scratch=(), limit=24):
    spec = pl.BlockSpec(memory_space=pltpu.VMEM)
    return pl.pallas_call(
        kernel,
        out_shape=out_shape,
        in_specs=[spec] * len(args),
        out_specs=jax.tree.map(lambda _: spec, out_shape),
        scratch_shapes=list(scratch),
        compiler_params=pltpu.CompilerParams(vmem_limit_bytes=limit * 2**20),
    )(*args)


def edges(hits, stokes_int, map_residual, count):
    rows, blocks = hits.shape
    edge = jax.ShapeDtypeStruct((2 * PER_SEG + 1, rows, blocks), F32)
    spec = pl.BlockSpec(memory_space=pltpu.VMEM)
    return pl.pallas_call(
        functools.partial(edge_kernel, count),
        out_shape=[edge] * count + [jax.ShapeDtypeStruct(map_residual[:, 0].shape, F32)],
        in_specs=[spec, pl.BlockSpec(memory_space=pl.ANY), spec],
        out_specs=[spec] * (count + 1),
        scratch_shapes=[
            pltpu.VMEM((count, 2, rows, SEG), jnp.int32),
            pltpu.SemaphoreType.DMA((count,)),
        ],
        compiler_params=pltpu.CompilerParams(vmem_limit_bytes=32 * 2**20),
        cost_estimate=pl.CostEstimate(flops=0, bytes_accessed=8 * 10**6, transcendentals=0),
    )(hits, stokes_int, map_residual)


def prepare(payload, hits, stokes_int, inv_noise, depth):
    rows, samples = stokes_int.shape[1:]
    blocks = samples // LANES
    (g1h, g1l), (g2h, g2l), (sh, sl) = [np_split(table) for table in tables()]
    fixed = np.concatenate(
        [sh, sl, np.concatenate([g1h, g1l], 1), np.concatenate([g2h, g2l], 1)], axis=0
    )
    parts = 4
    out_shape = [
        jax.ShapeDtypeStruct(payload.shape, F32),
        jax.ShapeDtypeStruct(stokes_int.shape, F32),
        jax.ShapeDtypeStruct((rows * blocks, depth), BF),
        jax.ShapeDtypeStruct((rows, WIN), F32),
        jax.ShapeDtypeStruct(fixed.shape, BF),
    ]
    spec = pl.BlockSpec(memory_space=pltpu.VMEM)
    far = pl.BlockSpec(memory_space=pl.ANY)
    return pl.pallas_call(
        prep_kernel,
        out_shape=out_shape,
        in_specs=[spec, spec, spec, far, far],
        out_specs=[spec] * len(out_shape),
        scratch_shapes=[
            pltpu.VMEM((parts, 2, rows, samples // parts), jnp.int32),
            pltpu.SemaphoreType.DMA((parts + 1,)),
        ],
        compiler_params=pltpu.CompilerParams(vmem_limit_bytes=32 * 2**20),
        cost_estimate=pl.CostEstimate(flops=0, bytes_accessed=12 * 10**6, transcendentals=0),
    )(payload, hits, inv_noise, stokes_int, fixed)


def exchanged(value, axis):
    return [value] + [
        lax.ppermute(value, axis, partner_perm(axis, by)) for by in range(1, lax.axis_size(axis))
    ]


def summed(value, axis):
    count = lax.axis_size(axis)
    if count & (count - 1):
        return sum(exchanged(value, axis))
    by = 1
    while by < count:
        value = value + lax.ppermute(value, axis, partner_perm(axis, by))
        by *= 2
    return value


def shards(map_solution, map_residual, map_direction, hits, stokes_int, inv_noise):
    groups = lax.axis_size("group")
    times = lax.axis_size("tm")
    width = map_direction.shape[2]
    local = 3 * groups * times * width
    depth = -(-local // 256) * 256
    rows = hits.shape[0]
    segs = hits.shape[1] // PER_SEG

    own = map_direction[:, 0]
    near = [lax.ppermute(own, "det", tile_perm(e)) for e in range(2)]
    *edge, residual = edges(hits, stokes_int, map_residual, 1 if times == 2 else 2)
    payload = jnp.stack([own] + near + [residual])
    from_group = exchanged(payload, "group")
    payload, weights, onehot, scales, fixed = prepare(payload, hits, stokes_int, inv_noise, depth)
    arrived = jnp.stack([payload] + from_group[1:])
    if times == 2:
        sent = jnp.concatenate([arrived.reshape(-1, width, LANES), edge[0].reshape(-1, width, LANES)])
        came = lax.ppermute(sent, "tm", partner_perm("tm", 1))
        others = came[:arrived.size // (width * LANES)].reshape((1,) + arrived.shape)
        sides = [came[arrived.size // (width * LANES):].reshape(edge[0].shape)]
    else:
        forward = [(i, i + 1) for i in range(times - 1)]
        backward = [(b, a) for a, b in forward]
        sides = [lax.ppermute(edge[1], "tm", forward), lax.ppermute(edge[0], "tm", backward)]
        others = jnp.stack(exchanged(arrived, "tm")[1:])

    binned = vmem_call(
        main_kernel,
        jax.ShapeDtypeStruct((times, 3, groups, width, 3 * LANES), F32),
        [arrived, others, weights, onehot, scales, fixed] + sides,
        [
            pltpu.VMEM((depth, 3 * LANES), F32),
            pltpu.VMEM((depth, 3 * LANES), BF),
            pltpu.VMEM((depth, 3 * LANES), BF),
            pltpu.VMEM(((segs + 2) * rows, SEG), F32),
            pltpu.VMEM((segs * rows, SEG), F32),
            pltpu.VMEM((depth, 3 * LANES), F32),
        ],
    )
    half = binned[0]
    for by in range(1, times):
        half = half + lax.ppermute(binned[by], "tm", partner_perm("tm", by))
    pixels = half[0]
    for e in range(2):
        pixels = pixels + lax.ppermute(half[1 + e], "det", tile_perm(e))
    parts = jnp.stack(exchanged(pixels, "group"))
    image, sums = vmem_call(
        sum_kernel,
        [
            jax.ShapeDtypeStruct((3, width, LANES), F32),
            jax.ShapeDtypeStruct((8, LANES), F32),
        ],
        [arrived, parts],
    )
    sums = summed(summed(sums, "tm"), "det")
    return vmem_call(
        step_kernel,
        [jax.ShapeDtypeStruct(map_solution.shape, F32)] * 3,
        [sums, image, arrived, map_solution],
    )


def solution(mesh):
    map_placed = P(None, "det", ("group", "tm"), None)
    placed = (
        map_placed,
        map_placed,
        map_placed,
        P(("group", "det"), "tm"),
        P(None, ("group", "det"), "tm"),
        P(("group", "det"), None),
    )
    return jax.shard_map(
        shards,
        mesh=mesh,
        in_specs=placed,
        out_specs=(map_placed, map_placed, map_placed),
        check_vma=False,
    )
```

time: 86.5 us -> 52.4 us (0.61)
  local copies, waits for them, and re-layouts: 14.9 us -> 3.52 us
  blocking collectives: 10.8 us -> 0 us
  other arithmetic: 8.9 us -> 0.09 us
  between operations: 4.92 us -> 0.76 us
  starting transfers between devices: 18.2 us -> 15.9 us
  Pallas kernels: 9.83 us -> 12 us
  waiting for transfers between devices: 18 us -> 19.7 us
    all_gather x1 -> x0, blocking collectives: 10.8 us -> none  [shards(): lax.all_gather(map_direction, ('group', 'tm'), axis=2, tiled=True)[:, 0]]
    slice x5 -> x2, local copies, waits for them, and re-layouts: 5.41 us -> 0.02 us  [the longest x1 0.01 us: shards(): came[:arrived.size // (width * LANES)].reshape((1,) + arrived.shape)]
    unnamed x22 -> x14, local copies, waits for them, and re-layouts: 7.99 us -> 3.48 us
    add x8 -> x5, other arithmetic: 4.21 us -> 0.04 us  [the longest x1 0.02 us: shards(): half = half + lax.ppermute(binned[by], 'tm', partner_perm('tm', by))]
    another operation x1 -> x3, other arithmetic: 2.7 us -> 0.03 us  [the longest x1 0.01 us: shards(): parts = jnp.stack(exchanged(pixels, 'group'))]
    ppermute x17 -> x15, starting transfers between devices: 18.2 us -> 15.9 us  [the longest x6 7.04 us: exchanged(): lax.ppermute(value, axis, partner_perm(axis, by))]
    pallas_call x1 -> x5, Pallas kernels: 9.83 us -> 12 us  [the longest x3 9.65 us: vmem_call(): pl.pallas_call(kernel, out_shape=out_shape, in_specs=[spec] * len(args),...]
    reduce_sum x3 -> x0, other arithmetic: 1.89 us -> none  [the longest x1 0.68 us: shards(): jnp.sum(map_residual * map_residual)]
  transfers between devices with their start and end apart: 17 -> 15, of which waited for: 12 -> 13; matrix products, arithmetic and copies ran while one was open for 9% -> 0% of each run, Pallas kernels for 0% -> 5%
where the time goes in v1:
time: 52.4 us; the launch traced here: 52.1 us
  waiting for transfers between devices  19.7 us (38%)
  starting transfers between devices  15.9 us (30%)
  Pallas kernels  12 us (23%)
  local copies, waits for them, and re-layouts  3.52 us (7%)
  between operations  0.76 us (1%)
    pallas_call x3, Pallas kernels, vmem_call(): pl.pallas_call(kernel, out_shape=out_shape, in_specs=[spec] * len(args),...  9.65 us
    ppermute x3, waiting for transfers between devices, summed(): value = value + lax.ppermute(value, axis, partner_perm(axis, by))  8.42 us
    ppermute x6, starting transfers between devices, exchanged(): lax.ppermute(value, axis, partner_perm(axis, by))  7.04 us
    ppermute x2, starting transfers between devices, shards(): near = [lax.ppermute(own, 'det', tile_perm(e)) for e in range(2)]  5.56 us
    ppermute x2, waiting for transfers between devices, shards(): pixels = pixels + lax.ppermute(half[1 + e], 'det', tile_perm(e))  4.56 us
    ppermute x6, waiting for transfers between devices, exchanged(): lax.ppermute(value, axis, partner_perm(axis, by))  3.88 us
    unnamed x14, local copies, waits for them, and re-layouts  3.48 us
    pallas_call x1, Pallas kernels, prepare(): pl.pallas_call(prep_kernel, out_shape=out_shape, in_specs=[spec, spec, sp...  2.25 us
  transfers between devices with their start and end apart: 15, of which 13 were waited for; matrix products, arithmetic and copies ran while one was open for 0% of the time, Pallas kernels for 5%

profile of v1, /device:TPU:0, one launch (start us, length us, event | category | flops | bytes accessed | tf_op | source)
XLA Modules:
  0.0 52.1 jit_solution(14664580774299724588)
XLA Ops:
  0.6 3.1 %collective-permute-start.1 = (f32[3,8,128]{2,1,0:T(8,128)}, f32[3,8,128]{2,1,0:T(8,128)S(1)}, u32[]{:S(2)}, u32[]{:S(2)}) collective-permute-start(f32[3,8,128]{2,1,0:T(8,128)} %bitcast.46), channel_id=1, source_target_pairs={{0,2},{2,0},{4,6},{6,4},{1,3},{3,1},{5,7},{7,5},{8,10},{10,8},{12,... | collective-permute-start | bytes 36872 | tf_op jit(solution)/shard_map/ppermute | solution.py:431
  3.7 2.5 %collective-permute-start = (f32[3,8,128]{2,1,0:T(8,128)}, f32[3,8,128]{2,1,0:T(8,128)S(1)}, u32[]{:S(2)}, u32[]{:S(2)}) collective-permute-start(f32[3,8,128]{2,1,0:T(8,128)} %bitcast.47), channel_id=1, source_target_pairs={{0,6},{2,4},{4,2},{6,0},{1,7},{3,5},{5,3},{7,1},{8,14},{10,12},{12... | collective-permute-start | bytes 36872 | tf_op jit(solution)/shard_map/ppermute | solution.py:431
  6.2 1.6 %copy-done = s32[2,16,16384]{2,1,0:T(8,128)S(1)} copy-done((s32[2,16,16384]{2,1,0:T(8,128)S(1)}, s32[2,16,16384]{2,1,0:T(8,128)}, u32[]{:S(2)}) %copy-start) | copy-done | bytes 2097176
  7.8 0.7 %copy-done.3 = s32[16,128]{1,0:T(8,128)S(1)} copy-done((s32[16,128]{1,0:T(8,128)S(1)}, s32[16,128]{1,0:T(8,128)}, u32[]{:S(2)}) %copy-start.3) | copy-done | bytes 8216
  8.5 0.7 %copy-done.4 = f32[3,1,8,128]{3,2,1,0:T(8,128)S(1)} copy-done((f32[3,1,8,128]{3,2,1,0:T(8,128)S(1)}, f32[3,1,8,128]{3,2,1,0:T(8,128)}, u32[]{:S(2)}) %copy-start.4) | copy-done | bytes 12312
  9.9 2.4 %collective-permute-start.4 = (f32[4,3,8,128]{3,2,1,0:T(8,128)S(1)}, f32[4,3,8,128]{3,2,1,0:T(8,128)S(1)}, u32[]{:S(2)}, u32[]{:S(2)}) collective-permute-start(f32[4,3,8,128]{3,2,1,0:T(8,128)S(1)} %pad_maximum_fusion.3.payload), channel_id=1, source_target_pairs={{0,24},{8,16},{16,8},{24,0},{1,25},{9,17},{17,9},{25,1},{2,26},{10... | collective-permute-start | bytes 147464 | tf_op jit(solution)/shard_map/ppermute | solution.py:406
  12.4 0.5 collective-permute-start.3
  12.9 0.5 %collective-permute-start.2 = (f32[4,3,8,128]{3,2,1,0:T(8,128)S(1)}, f32[4,3,8,128]{3,2,1,0:T(8,128)S(1)}, u32[]{:S(2)}, u32[]{:S(2)}) collective-permute-start(f32[4,3,8,128]{3,2,1,0:T(8,128)S(1)} %pad_maximum_fusion.3.payload), channel_id=1, source_target_pairs={{0,8},{8,0},{16,24},{24,16},{1,9},{9,1},{17,25},{25,17},{2,10},{10... | collective-permute-start | bytes 147464 | tf_op jit(solution)/shard_map/ppermute | solution.py:406
  13.4 2.2 %shard_map.95 = (f32[4,3,8,128]{3,2,1,0:T(8,128)S(1)}, f32[2,16,16384]{2,1,0:T(8,128)S(1)}, bf16[2048,256]{1,0:T(8,128)(2,1)S(1)}, f32[16,1024]{1,0:T(8,128)S(1)}, bf16[1536,512]{1,0:T(8,128)(2,1)S(1)}) custom-call(f32[4,3,8,128]{3,2,1,0:T(8,128)S(1)} %pad_maximum_fusion.3.payload, s32[16,128]{1,0:T(8,128)S(1)} %copy-done.3, f32[16,512]{1,0:T(8,128)S(1)} %copy-done.2, ...), custom_call_target="tpu_custom_call" | custom-call | bytes 12000000 | tf_op jit(solution)/shard_map/pallas_call | solution.py:390
  15.7 0.8 %collective-permute-done.3 = f32[4,3,8,128]{3,2,1,0:T(8,128)S(1)} collective-permute-done((f32[4,3,8,128]{3,2,1,0:T(8,128)S(1)}, f32[4,3,8,128]{3,2,1,0:T(8,128)S(1)}, u32[]{:S(2)}, u32[]{:S(2)}) %collective-permute-start.3) | collective-permute-done | bytes 49184 | tf_op jit(solution)/shard_map/ppermute | solution.py:406
  17.1 1.5 %collective-permute-done.5 = f32[66,8,128]{2,1,0:T(8,128)S(1)} collective-permute-done((f32[66,8,128]{2,1,0:T(8,128)S(1)}, f32[66,8,128]{2,1,0:T(8,128)S(1)}, u32[]{:S(2)}, u32[]{:S(2)}) %collective-permute-start.5) | collective-permute-done | bytes 270368 | tf_op jit(solution)/shard_map/ppermute | solution.py:439
  18.6 8.9 %shard_map.96 = f32[2,3,4,8,384]{4,3,2,1,0:T(8,128)S(1)} custom-call(f32[4,4,3,8,128]{4,3,2,1,0:T(8,128)S(1)} %pad_maximum_fusion.1.arrived, f32[1,4,4,3,8,128]{5,4,3,2,1,0:T(8,128)S(1)} %bitcast.34, f32[2,16,16384]{2,1,0:T(8,128)S(1)} %get-tuple-element.15.weights, bf16[2048,256]{1,0:T(8,128)(2,1)S(1)} %get-tuple-element.16.onehot, ...), custom_call_target="tpu_custom_call" | custom-call | tf_op jit(solution)/shard_map/pallas_call | solution.py:345
  27.8 1.2 %collective-permute-done.6 = f32[3,4,8,384]{3,2,1,0:T(8,128)S(1)} collective-permute-done((f32[3,4,8,384]{3,2,1,0:T(8,128)S(1)}, f32[3,4,8,384]{3,2,1,0:T(8,128)S(1)}, u32[]{:S(2)}, u32[]{:S(2)}) %collective-permute-start.6) | collective-permute-done | bytes 147488 | tf_op jit(solution)/shard_map/ppermute | solution.py:463
  29.0 2.1 %collective-permute-start.7 = (f32[4,8,384]{2,1,0:T(8,128)S(1)}, f32[4,8,384]{2,1,0:T(8,128)S(1)}, u32[]{:S(2)}, u32[]{:S(2)}) collective-permute-start(f32[4,8,384]{2,1,0:T(8,128)S(1)} %get-tuple-element.21), channel_id=1, source_target_pairs={{0,6},{2,4},{4,2},{6,0},{1,7},{3,5},{5,3},{7,1},{8,14},{10,12},{12... | collective-permute-start | bytes 147464 | tf_op jit(solution)/shard_map/ppermute | solution.py:466
  31.2 4.1 %collective-permute-done.7 = f32[4,8,384]{2,1,0:T(8,128)S(1)} collective-permute-done((f32[4,8,384]{2,1,0:T(8,128)S(1)}, f32[4,8,384]{2,1,0:T(8,128)S(1)}, u32[]{:S(2)}, u32[]{:S(2)}) %collective-permute-start.7) | collective-permute-done | bytes 49184 | tf_op jit(solution)/shard_map/ppermute | solution.py:466
  35.8 1.6 %collective-permute-start.11 = (f32[4,8,384]{2,1,0:T(8,128)S(1)}, f32[4,8,384]{2,1,0:T(8,128)S(1)}, u32[]{:S(2)}, u32[]{:S(2)}) collective-permute-start(f32[4,8,384]{2,1,0:T(8,128)S(1)} %fusion.2), channel_id=1, source_target_pairs={{0,24},{8,16},{16,8},{24,0},{1,25},{9,17},{17,9},{25,1},{2,26},{10... | collective-permute-start | bytes 147464 | tf_op jit(solution)/shard_map/ppermute | solution.py:406
  37.3 0.5 collective-permute-start.10
  37.8 1.5 %collective-permute-start.9 = (f32[4,8,384]{2,1,0:T(8,128)S(1)}, f32[4,8,384]{2,1,0:T(8,128)S(1)}, u32[]{:S(2)}, u32[]{:S(2)}) collective-permute-start(f32[4,8,384]{2,1,0:T(8,128)S(1)} %fusion.2), channel_id=1, source_target_pairs={{0,8},{8,0},{16,24},{24,16},{1,9},{9,1},{17,25},{25,17},{2,10},{10... | collective-permute-start | bytes 147464 | tf_op jit(solution)/shard_map/ppermute | solution.py:406
  39.3 1.8 %collective-permute-done.11 = f32[4,8,384]{2,1,0:T(8,128)S(1)} collective-permute-done((f32[4,8,384]{2,1,0:T(8,128)S(1)}, f32[4,8,384]{2,1,0:T(8,128)S(1)}, u32[]{:S(2)}, u32[]{:S(2)}) %collective-permute-start.11) | collective-permute-done | bytes 49184 | tf_op jit(solution)/shard_map/ppermute | solution.py:406
  42.1 1.2 %collective-permute-done.12 = f32[8,128]{1,0:T(8,128)S(1)} collective-permute-done((f32[8,128]{1,0:T(8,128)S(1)}, f32[8,128]{1,0:T(8,128)S(1)}, u32[]{:S(2)}, u32[]{:S(2)}) %collective-permute-start.12) | collective-permute-done | bytes 4128 | tf_op jit(solution)/shard_map/ppermute | solution.py:416
  43.5 3.3 %collective-permute-done.13 = f32[8,128]{1,0:T(8,128)S(1)} collective-permute-done((f32[8,128]{1,0:T(8,128)S(1)}, f32[8,128]{1,0:T(8,128)S(1)}, u32[]{:S(2)}, u32[]{:S(2)}) %collective-permute-start.13) | collective-permute-done | bytes 4128 | tf_op jit(solution)/shard_map/ppermute | solution.py:416
  46.9 0.6 %collective-permute-start.14 = (f32[8,128]{1,0:T(8,128)S(1)}, f32[8,128]{1,0:T(8,128)S(1)}, u32[]{:S(2)}, u32[]{:S(2)}) collective-permute-start(f32[8,128]{1,0:T(8,128)S(1)} %add.22), channel_id=1, source_target_pairs={{0,4},{2,6},{4,0},{6,2},{1,5},{3,7},{5,1},{7,3},{8,12},{10,14},{12... | collective-permute-start | bytes 12296 | tf_op jit(solution)/shard_map/ppermute | solution.py:416
  47.4 3.9 %collective-permute-done.14 = f32[8,128]{1,0:T(8,128)S(1)} collective-permute-done((f32[8,128]{1,0:T(8,128)S(1)}, f32[8,128]{1,0:T(8,128)S(1)}, u32[]{:S(2)}, u32[]{:S(2)}) %collective-permute-start.14) | collective-permute-done | bytes 4128 | tf_op jit(solution)/shard_map/ppermute | solution.py:416
  51.4 0.7 %shard_map.98 = (f32[3,1,8,128]{3,2,1,0:T(8,128)}, f32[3,1,8,128]{3,2,1,0:T(8,128)}, f32[3,1,8,128]{3,2,1,0:T(8,128)}) custom-call(f32[8,128]{1,0:T(8,128)S(1)} %add.23.sums, f32[3,8,128]{2,1,0:T(8,128)S(1)} %get-tuple-element.20.image, f32[4,4,3,8,128]{4,3,2,1,0:T(8,128)S(1)} %pad_maximum_fusion.1.arrived, f32[3,1,8,128]{3,2,1,0:T(8,128)S(1)} %copy-done.5), custom_call_target="tpu_custom_call" | custom-call | tf_op jit(solution)/shard_map/pallas_call | solution.py:345
  (38 shorter events, 3.3 us)
Async XLA Ops:
  0.6 8.7 %collective-permute-start.1 = (f32[3,8,128]{2,1,0:T(8,128)}, f32[3,8,128]{2,1,0:T(8,128)S(1)}, u32[]{:S(2)}, u32[]{:S(2)}) collective-permute-start(f32[3,8,128]{2,1,0:T(8,128)} %bitcast.46), channel_id=1, source_target_pairs={{0,2},{2,0},{4,6},{6,4},{1,3},{3,1},{5,7},{7,5},{8,10},{10,8},{12,... | collective-permute-start | bytes 36872 | tf_op jit(solution)/shard_map/ppermute | solution.py:431
  3.7 5.7 %collective-permute-start = (f32[3,8,128]{2,1,0:T(8,128)}, f32[3,8,128]{2,1,0:T(8,128)S(1)}, u32[]{:S(2)}, u32[]{:S(2)}) collective-permute-start(f32[3,8,128]{2,1,0:T(8,128)} %bitcast.47), channel_id=1, source_target_pairs={{0,6},{2,4},{4,2},{6,0},{1,7},{3,5},{5,3},{7,1},{8,14},{10,12},{12... | collective-permute-start | bytes 36872 | tf_op jit(solution)/shard_map/ppermute | solution.py:431
  6.2 1.6 %copy-start = (s32[2,16,16384]{2,1,0:T(8,128)S(1)}, s32[2,16,16384]{2,1,0:T(8,128)}, u32[]{:S(2)}) copy-start(s32[2,16,16384]{2,1,0:T(8,128)} %stokes.3) | copy-start | bytes 6291460
  7.8 0.7 %copy-start.3 = (s32[16,128]{1,0:T(8,128)S(1)}, s32[16,128]{1,0:T(8,128)}, u32[]{:S(2)}) copy-start(s32[16,128]{1,0:T(8,128)} %hits.3) | copy-start | bytes 24580
  8.5 0.7 %copy-start.4 = (f32[3,1,8,128]{3,2,1,0:T(8,128)S(1)}, f32[3,1,8,128]{3,2,1,0:T(8,128)}, u32[]{:S(2)}) copy-start(f32[3,1,8,128]{3,2,1,0:T(8,128)} %residual.1) | copy-start | bytes 36868
  9.2 0.7 %copy-start.6 = (f32[3,1,8,128]{3,2,1,0:T(8,128)S(1)}, f32[3,1,8,128]{3,2,1,0:T(8,128)}, u32[]{:S(2)}) copy-start(f32[3,1,8,128]{3,2,1,0:T(8,128)} %param.9) | copy-start | bytes 36868
  9.2 4.2 %copy-start.1 = (bf16[1536,512]{1,0:T(8,128)(2,1)S(1)}, bf16[1536,512]{1,0:T(8,128)(2,1)}, u32[]{:S(2)}) copy-start(bf16[1536,512]{1,0:T(8,128)(2,1)} %constant.2.clone.tables_in) | copy-start | bytes 4718596
  9.2 4.2 %copy-start.2 = (f32[16,512]{1,0:T(8,128)S(1)}, f32[16,512]{1,0:T(8,128)}, u32[]{:S(2)}) copy-start(f32[16,512]{1,0:T(8,128)} %inv_noise.1) | copy-start | bytes 98308
  9.9 5.8 %collective-permute-start.4 = (f32[4,3,8,128]{3,2,1,0:T(8,128)S(1)}, f32[4,3,8,128]{3,2,1,0:T(8,128)S(1)}, u32[]{:S(2)}, u32[]{:S(2)}) collective-permute-start(f32[4,3,8,128]{3,2,1,0:T(8,128)S(1)} %pad_maximum_fusion.3.payload), channel_id=1, source_target_pairs={{0,24},{8,16},{16,8},{24,0},{1,25},{9,17},{17,9},{25,1},{2,26},{10... | collective-permute-start | bytes 147464 | tf_op jit(solution)/shard_map/ppermute | solution.py:406
  12.4 4.1 %collective-permute-start.3 = (f32[4,3,8,128]{3,2,1,0:T(8,128)S(1)}, f32[4,3,8,128]{3,2,1,0:T(8,128)S(1)}, u32[]{:S(2)}, u32[]{:S(2)}) collective-permute-start(f32[4,3,8,128]{3,2,1,0:T(8,128)S(1)} %pad_maximum_fusion.3.payload), channel_id=1, source_target_pairs={{0,16},{8,24},{16,0},{24,8},{1,17},{9,25},{17,1},{25,9},{2,18},{10... | collective-permute-start | bytes 147464 | tf_op jit(solution)/shard_map/ppermute | solution.py:406
  12.9 4.1 %collective-permute-start.2 = (f32[4,3,8,128]{3,2,1,0:T(8,128)S(1)}, f32[4,3,8,128]{3,2,1,0:T(8,128)S(1)}, u32[]{:S(2)}, u32[]{:S(2)}) collective-permute-start(f32[4,3,8,128]{3,2,1,0:T(8,128)S(1)} %pad_maximum_fusion.3.payload), channel_id=1, source_target_pairs={{0,8},{8,0},{16,24},{24,16},{1,9},{9,1},{17,25},{25,17},{2,10},{10... | collective-permute-start | bytes 147464 | tf_op jit(solution)/shard_map/ppermute | solution.py:406
  17.0 1.6 %collective-permute-start.5 = (f32[66,8,128]{2,1,0:T(8,128)S(1)}, f32[66,8,128]{2,1,0:T(8,128)S(1)}, u32[]{:S(2)}, u32[]{:S(2)}) collective-permute-start(f32[66,8,128]{2,1,0:T(8,128)S(1)} %pad_maximum_fusion), channel_id=1, source_target_pairs={{0,1},{1,0},{2,3},{3,2},{4,5},{5,4},{6,7},{7,6},{8,9},{9,8},{10,11... | collective-permute-start | bytes 811016 | tf_op jit(solution)/shard_map/ppermute | solution.py:439
  18.6 32.7 %copy-start.5 = (f32[3,1,8,128]{3,2,1,0:T(8,128)S(1)}, f32[3,1,8,128]{3,2,1,0:T(8,128)}, u32[]{:S(2)}) copy-start(f32[3,1,8,128]{3,2,1,0:T(8,128)} %solution_in.1) | copy-start | bytes 36868
  27.6 1.4 %collective-permute-start.6 = (f32[3,4,8,384]{3,2,1,0:T(8,128)S(1)}, f32[3,4,8,384]{3,2,1,0:T(8,128)S(1)}, u32[]{:S(2)}, u32[]{:S(2)}) collective-permute-start(f32[3,4,8,384]{3,2,1,0:T(8,128)S(1)} %slice_bitcast_fusion), channel_id=1, source_target_pairs={{0,1},{1,0},{2,3},{3,2},{4,5},{5,4},{6,7},{7,6},{8,9},{9,8},{10,11... | collective-permute-start | bytes 442376 | tf_op jit(solution)/shard_map/ppermute | solution.py:463
  29.0 6.2 %collective-permute-start.7 = (f32[4,8,384]{2,1,0:T(8,128)S(1)}, f32[4,8,384]{2,1,0:T(8,128)S(1)}, u32[]{:S(2)}, u32[]{:S(2)}) collective-permute-start(f32[4,8,384]{2,1,0:T(8,128)S(1)} %get-tuple-element.21), channel_id=1, source_target_pairs={{0,6},{2,4},{4,2},{6,0},{1,7},{3,5},{5,3},{7,1},{8,14},{10,12},{12... | collective-permute-start | bytes 147464 | tf_op jit(solution)/shard_map/ppermute | solution.py:466
  31.2 4.6 %collective-permute-start.8 = (f32[4,8,384]{2,1,0:T(8,128)S(1)}, f32[4,8,384]{2,1,0:T(8,128)S(1)}, u32[]{:S(2)}, u32[]{:S(2)}) collective-permute-start(f32[4,8,384]{2,1,0:T(8,128)S(1)} %get-tuple-element.22), channel_id=1, source_target_pairs={{0,2},{2,0},{4,6},{6,4},{1,3},{3,1},{5,7},{7,5},{8,10},{10,8},{12,... | collective-permute-start | bytes 147464 | tf_op jit(solution)/shard_map/ppermute | solution.py:466
  35.8 5.4 %collective-permute-start.11 = (f32[4,8,384]{2,1,0:T(8,128)S(1)}, f32[4,8,384]{2,1,0:T(8,128)S(1)}, u32[]{:S(2)}, u32[]{:S(2)}) collective-permute-start(f32[4,8,384]{2,1,0:T(8,128)S(1)} %fusion.2), channel_id=1, source_target_pairs={{0,24},{8,16},{16,8},{24,0},{1,25},{9,17},{17,9},{25,1},{2,26},{10... | collective-permute-start | bytes 147464 | tf_op jit(solution)/shard_map/ppermute | solution.py:406
  37.3 4.2 %collective-permute-start.10 = (f32[4,8,384]{2,1,0:T(8,128)S(1)}, f32[4,8,384]{2,1,0:T(8,128)S(1)}, u32[]{:S(2)}, u32[]{:S(2)}) collective-permute-start(f32[4,8,384]{2,1,0:T(8,128)S(1)} %fusion.2), channel_id=1, source_target_pairs={{0,16},{8,24},{16,0},{24,8},{1,17},{9,25},{17,1},{25,9},{2,18},{10... | collective-permute-start | bytes 147464 | tf_op jit(solution)/shard_map/ppermute | solution.py:406
  37.8 4.1 %collective-permute-start.9 = (f32[4,8,384]{2,1,0:T(8,128)S(1)}, f32[4,8,384]{2,1,0:T(8,128)S(1)}, u32[]{:S(2)}, u32[]{:S(2)}) collective-permute-start(f32[4,8,384]{2,1,0:T(8,128)S(1)} %fusion.2), channel_id=1, source_target_pairs={{0,8},{8,0},{16,24},{24,16},{1,9},{9,1},{17,25},{25,17},{2,10},{10... | collective-permute-start | bytes 147464 | tf_op jit(solution)/shard_map/ppermute | solution.py:406
  42.0 1.2 %collective-permute-start.12 = (f32[8,128]{1,0:T(8,128)S(1)}, f32[8,128]{1,0:T(8,128)S(1)}, u32[]{:S(2)}, u32[]{:S(2)}) collective-permute-start(f32[8,128]{1,0:T(8,128)S(1)} %get-tuple-element.19), channel_id=1, source_target_pairs={{0,1},{1,0},{2,3},{3,2},{4,5},{5,4},{6,7},{7,6},{8,9},{9,8},{10,11... | collective-permute-start | bytes 12296 | tf_op jit(solution)/shard_map/ppermute | solution.py:416
  43.2 3.6 %collective-permute-start.13 = (f32[8,128]{1,0:T(8,128)S(1)}, f32[8,128]{1,0:T(8,128)S(1)}, u32[]{:S(2)}, u32[]{:S(2)}) collective-permute-start(f32[8,128]{1,0:T(8,128)S(1)} %add.21), channel_id=1, source_target_pairs={{0,2},{2,0},{4,6},{6,4},{1,3},{3,1},{5,7},{7,5},{8,10},{10,8},{12,... | collective-permute-start | bytes 12296 | tf_op jit(solution)/shard_map/ppermute | solution.py:416
  46.9 4.5 %collective-permute-start.14 = (f32[8,128]{1,0:T(8,128)S(1)}, f32[8,128]{1,0:T(8,128)S(1)}, u32[]{:S(2)}, u32[]{:S(2)}) collective-permute-start(f32[8,128]{1,0:T(8,128)S(1)} %add.22), channel_id=1, source_target_pairs={{0,4},{2,6},{4,0},{6,2},{1,5},{3,7},{5,1},{7,3},{8,12},{10,14},{12... | collective-permute-start | bytes 12296 | tf_op jit(solution)/shard_map/ppermute | solution.py:416

commit v2 on v1

--- a/solution.py
+++ b/solution.py
@@ -42,11 +42,12 @@
     return np.concatenate([cos_t * scale, sin_t * math.sqrt(2.0 / samples)], axis=1)
 
 
-def tables():
+def table_rows():
     ee = trig_table(HALF, np.arange(0, SEG + 1, 4), WIN, True)
     eo = trig_table(HALF, np.arange(2, SEG, 4), WIN, False)
-    odd = trig_table(SEG, np.arange(1, SEG, 2), WIN, False)
-    return ee, eo, odd
+    angle = 2.0 * math.pi / WIN * np.arange(HALF)
+    turn = [np.tile(part(angle)[None], (16, 1)) for part in (np.cos, np.sin)]
+    return np.concatenate([np.concatenate(np_split(t), axis=1) for t in (ee, eo, *turn)], axis=0)
 
 
 def dot(a, b):
@@ -155,22 +156,28 @@
     lax.fori_loop(0, blocks // step, ones_of, 0)
 
     freqs = inv_noise.shape[1]
-    column = lax.broadcasted_iota(jnp.int32, (1, WIN), 1)
     quarter = HALF // 2
-    wanted = jnp.where(
-        column < HALF,
-        jnp.where(column <= quarter, 4 * column, 4 * (column - quarter)),
-        jnp.where(
-            column < SEG,
-            4 * lax.rem(column, quarter) + 2,
-            2 * lax.rem(column, HALF) + 1,
-        ),
-    )
-    wanted = jnp.broadcast_to(jnp.minimum(wanted, freqs - 1), (freqs, WIN))
-    held = lax.broadcasted_iota(jnp.int32, (freqs, WIN), 0)
+    column = lax.broadcasted_iota(jnp.int32, (1, 7 * quarter), 1)
+    place = lax.rem(column, quarter)
+    kind = column // quarter
+    wanted = 4 * place
+    wanted = jnp.where(kind == 1, jnp.where(place == 0, SEG, wanted), wanted)
+    wanted = jnp.where((kind == 2) | (kind == 3), wanted + 2, wanted)
+    wanted = jnp.where(kind == 4, wanted + 1, wanted)
+    wanted = jnp.where(kind == 5, jnp.maximum(wanted - 1, 1), wanted)
+    wanted = jnp.where(kind == 6, SEG, wanted)
+    wanted = jnp.broadcast_to(jnp.minimum(wanted, freqs - 1), (freqs, 7 * quarter))
+    held = lax.broadcasted_iota(jnp.int32, (freqs, 7 * quarter), 0)
     chosen = jnp.where(wanted == held, 1.0, 0.0).astype(BF)
     both = dot(jnp.concatenate(split(inv_noise[...]), axis=0), chosen)
-    scales[...] = both[:rows] + both[rows:]
+    half = 0.5 * (both[:rows] + both[rows:])
+    ahead, behind, last = [half[:, i * quarter:(i + 1) * quarter] for i in (4, 5, 6)]
+    mean = ahead + behind
+    lane = lax.broadcasted_iota(jnp.int32, (rows, quarter), 1)
+    scales[:, :SEG] = half[:, :SEG]
+    scales[:, SEG:SEG + quarter] = mean
+    scales[:, SEG + quarter:SEG + HALF] = jnp.where(lane == 0, 2.0 * last, mean)
+    scales[:, SEG + HALF:] = ahead - behind
 
     for i in range(parts):
         copies[i].wait()
@@ -182,19 +189,20 @@
 def main_kernel(
     arrived, others, weights, onehot, scales, tables_in, *refs,
 ):
-    sides, (out, window, mh, ml, x, f, total) = refs[:-7], refs[-7:]
+    sides, (out, window, mhl, x, f, total) = refs[:-6], refs[-6:]
     groups = lax.axis_size("group")
     times = lax.axis_size("tm")
     width = arrived.shape[3]
     rows = weights.shape[1]
     blocks = weights.shape[2] // LANES
     tile_blocks = groups * times * width
-    depth = mh.shape[0]
+    depth = mhl.shape[0]
+    local = 3 * tile_blocks
     segs = blocks // PER_SEG
-    chunk_segs = 4
+    chunk_segs = 32
     chunk_blocks = chunk_segs * PER_SEG
     chunk = chunk_blocks * rows
-    tiles = (1, tile_sides(0)[0], tile_sides(1)[0])
+    tiles = (1, tile_sides(1)[0], tile_sides(0)[0])
 
     window[...] = jnp.zeros(window.shape, F32)
     for k in range(times):
@@ -205,7 +213,7 @@
                 for c in range(3):
                     piece = arrived[j, s, c] if k == 0 else others[k - 1, j, s, c]
                     window[place, pl.ds(c * LANES, LANES)] = piece
-    mh[...], ml[...] = split(window[...])
+    mhl[:, :3 * LANES], mhl[:, 3 * LANES:] = split(window[...])
 
     ids = lax.broadcasted_iota(jnp.int32, (rows, depth), 1).astype(F32)
 
@@ -229,14 +237,16 @@
             ],
             axis=0,
         ).astype(BF)
-        picked = dot(ones, mh[...]) + dot(ones, ml[...])
+        picked = dot(ones, mhl[...])
+        picked = picked[:, :3 * LANES] + picked[:, 3 * LANES:]
         place = pl.ds(at if isinstance(at, int) else pl.multiple_of(at, rows), rows)
         for j in range(PER_SEG):
             x[place, pl.ds(j * LANES, LANES)] = scan(picked, j, side[j], side[PER_SEG + j])
 
     def scan_chunk(i, carry):
         ones = onehot[pl.ds(pl.multiple_of(i * chunk, chunk), chunk), :]
-        picked = dot(ones, mh[...]) + dot(ones, ml[...])
+        picked = dot(ones, mhl[...])
+        picked = picked[:, :3 * LANES] + picked[:, 3 * LANES:]
         for j in range(chunk_blocks):
             lanes = pl.ds(pl.multiple_of(i * chunk_blocks * LANES, LANES) + j * LANES, LANES)
             at = pl.multiple_of((i * chunk_segs + 1 + j // PER_SEG) * rows, rows)
@@ -247,33 +257,49 @@
 
     lax.fori_loop(0, segs // chunk_segs, scan_chunk, 0)
 
-    sh = tables_in[:SEG, :]
-    sl = tables_in[SEG:2 * SEG, :]
-    g1h, g1l = tables_in[2 * SEG:2 * SEG + HALF, :HALF], tables_in[2 * SEG:2 * SEG + HALF, HALF:]
-    g2h, g2l = tables_in[2 * SEG + HALF:, :HALF], tables_in[2 * SEG + HALF:, HALF:]
-    part_segs = 16
-    part = part_segs * rows
-
-    def weighted(coeffs, scale):
-        return (coeffs.reshape(part_segs, rows, -1) * scale[None]).reshape(part, -1)
-
-    def filter_part(i, carry):
-        at = pl.multiple_of(i * part, part)
-        middle = x[pl.ds(at + rows, part), :]
-        around = 0.5 * (x[pl.ds(at, part), :] + x[pl.ds(at + 2 * rows, part), :])
-        even = middle + around
-        odd = middle - around
-        coeffs = dot3(dot, even[:, :HALF] + even[:, HALF:], g1h, g1l)
-        first = dot3(dot_t, weighted(coeffs, 0.5 * scales[:, :HALF]), g1h, g1l)
-        coeffs = dot3(dot, even[:, :HALF] - even[:, HALF:], g2h, g2l)
-        second = dot3(dot_t, weighted(coeffs, 0.5 * scales[:, HALF:SEG]), g2h, g2l)
-        coeffs = dot3(dot, odd, sh, sl)
-        third = dot3(dot_t, weighted(coeffs, scales[:, SEG:]), sh, sl)
-        f[pl.ds(at, part), :HALF] = first + second + third[:, :HALF]
-        f[pl.ds(at, part), HALF:] = first - second + third[:, HALF:]
-        return carry
-
-    lax.fori_loop(0, segs // part_segs, filter_part, 0)
+    g1h, g1l = tables_in[:HALF, :HALF], tables_in[:HALF, HALF:]
+    g2h, g2l = tables_in[HALF:SEG, :HALF], tables_in[HALF:SEG, HALF:]
+    turn = tables_in[SEG:, :].astype(F32)
+    turn = turn[:, :HALF] + turn[:, HALF:]
+    cos, sin = turn[:1], turn[16:17]
+    quarter = HALF // 2
+    part = segs * rows
+
+    def weighted(coeffs, at, width):
+        scale = scales[:, at:at + width]
+        return (coeffs.reshape(segs, rows, width) * scale[None]).reshape(part, width)
+
+    middle = x[pl.ds(rows, part), :]
+    around = 0.5 * (x[pl.ds(0, part), :] + x[pl.ds(2 * rows, part), :])
+    even = middle + around
+    odd = middle - around
+    coeffs = dot3(dot, even[:, :HALF] - even[:, HALF:], g2h, g2l)
+    second = dot3(dot_t, weighted(coeffs, HALF, HALF), g2h, g2l)
+    real = cos * odd[:, :HALF] - sin * odd[:, HALF:]
+    imag = sin * odd[:, :HALF] + cos * odd[:, HALF:]
+    coeffs = dot3(
+        dot, jnp.concatenate([even[:, :HALF] + even[:, HALF:], real, imag], axis=0), g1h, g1l
+    )
+    real, imag = coeffs[part:2 * part], coeffs[2 * part:]
+    cross = SEG + HALF
+    mixed = [
+        weighted(real[:, :quarter], SEG, quarter) - weighted(imag[:, quarter:], cross, quarter),
+        weighted(real[:, quarter:], SEG + quarter, quarter) + weighted(imag[:, :quarter], cross, quarter),
+        weighted(imag[:, :quarter], SEG, quarter) + weighted(real[:, quarter:], cross, quarter),
+        weighted(imag[:, quarter:], SEG + quarter, quarter) - weighted(real[:, :quarter], cross, quarter),
+    ]
+    coeffs = jnp.concatenate(
+        [
+            weighted(coeffs[:part], 0, HALF),
+            jnp.concatenate(mixed[:2], axis=1),
+            jnp.concatenate(mixed[2:], axis=1),
+        ],
+        axis=0,
+    )
+    back = dot3(dot_t, coeffs, g1h, g1l)
+    first, real, imag = back[:part], back[part:2 * part], back[2 * part:]
+    f[:, :HALF] = first + second + cos * real + sin * imag
+    f[:, HALF:] = first - second - sin * real + cos * imag
 
     total[...] = jnp.zeros(total.shape, F32)
 
@@ -288,13 +314,14 @@
                     [value, weights[0, :, lanes] * value, weights[1, :, lanes] * value], axis=1
                 )
             )
-        vh, vl = split(jnp.concatenate(values, axis=0))
-        ones = onehot[pl.ds(pl.multiple_of(i * chunk, chunk), chunk), :]
-        over = (((0,), (0,)), ((), ()))
-        total[...] += (
-            lax.dot_general(ones, vh, over, preferred_element_type=F32)
-            + lax.dot_general(ones, vl, over, preferred_element_type=F32)
+        ones = onehot[pl.ds(pl.multiple_of(i * chunk, chunk), chunk), :local]
+        sums = lax.dot_general(
+            ones,
+            jnp.concatenate(split(jnp.concatenate(values, axis=0)), axis=1),
+            (((0,), (0,)), ((), ())),
+            preferred_element_type=F32,
         )
+        total[...] += sums[:, :3 * LANES] + sums[:, 3 * LANES:]
         return carry
 
     lax.fori_loop(0, segs // chunk_segs, bin_chunk, 0)
@@ -373,16 +400,13 @@
 def prepare(payload, hits, stokes_int, inv_noise, depth):
     rows, samples = stokes_int.shape[1:]
     blocks = samples // LANES
-    (g1h, g1l), (g2h, g2l), (sh, sl) = [np_split(table) for table in tables()]
-    fixed = np.concatenate(
-        [sh, sl, np.concatenate([g1h, g1l], 1), np.concatenate([g2h, g2l], 1)], axis=0
-    )
+    fixed = table_rows()
     parts = 4
     out_shape = [
         jax.ShapeDtypeStruct(payload.shape, F32),
         jax.ShapeDtypeStruct(stokes_int.shape, F32),
         jax.ShapeDtypeStruct((rows * blocks, depth), BF),
-        jax.ShapeDtypeStruct((rows, WIN), F32),
+        jax.ShapeDtypeStruct((rows, 3 * HALF + HALF // 2), F32),
         jax.ShapeDtypeStruct(fixed.shape, BF),
     ]
     spec = pl.BlockSpec(memory_space=pltpu.VMEM)
@@ -428,7 +452,7 @@
     segs = hits.shape[1] // PER_SEG
 
     own = map_direction[:, 0]
-    near = [lax.ppermute(own, "det", tile_perm(e)) for e in range(2)]
+    near = [lax.ppermute(own, "det", tile_perm(e)) for e in (1, 0)]
     *edge, residual = edges(hits, stokes_int, map_residual, 1 if times == 2 else 2)
     payload = jnp.stack([own] + near + [residual])
     from_group = exchanged(payload, "group")
@@ -451,11 +475,10 @@
         [arrived, others, weights, onehot, scales, fixed] + sides,
         [
             pltpu.VMEM((depth, 3 * LANES), F32),
-            pltpu.VMEM((depth, 3 * LANES), BF),
-            pltpu.VMEM((depth, 3 * LANES), BF),
+            pltpu.VMEM((depth, 6 * LANES), BF),
             pltpu.VMEM(((segs + 2) * rows, SEG), F32),
             pltpu.VMEM((segs * rows, SEG), F32),
-            pltpu.VMEM((depth, 3 * LANES), F32),
+            pltpu.VMEM((local, 3 * LANES), F32),
         ],
     )
     half = binned[0]
@@ -473,7 +496,7 @@
         ],
         [arrived, parts],
     )
-    sums = summed(summed(sums, "tm"), "det")
+    sums = sum(exchanged(summed(sums, "tm"), "det"))
     return vmem_call(
         step_kernel,
         [jax.ShapeDtypeStruct(map_solution.shape, F32)] * 3,

time: 52.4 us -> 46.3 us (0.88)
  waiting for transfers between devices: 19.7 us -> 15.2 us
  Pallas kernels: 12 us -> 8.06 us
  starting transfers between devices: 15.9 us -> 18.8 us
    ppermute x3 -> x1, waiting for transfers between devices: 8.42 us -> 1.15 us  [summed(): value = value + lax.ppermute(value, axis, partner_perm(axis, by))]
    ppermute x6 -> x9, starting transfers between devices: 7.04 us -> 11.5 us  [exchanged(): lax.ppermute(value, axis, partner_perm(axis, by))]
    pallas_call x3, Pallas kernels: 9.65 us -> 5.67 us  [vmem_call(): pl.pallas_call(kernel, out_shape=out_shape, in_specs=[spec] * len(args),...]
    ppermute x6 -> x9, waiting for transfers between devices: 3.88 us -> 5.93 us  [exchanged(): lax.ppermute(value, axis, partner_perm(axis, by))]
    ppermute x3 -> x1, starting transfers between devices: 0.92 us -> 0.07 us  [summed(): value = value + lax.ppermute(value, axis, partner_perm(axis, by))]
    ppermute x2, waiting for transfers between devices: 0.11 us -> 0.78 us  [shards(): near = [lax.ppermute(own, 'det', tile_perm(e)) for e in (1, 0)]]
  transfers between devices with their start and end apart: 15 -> 16, of which waited for: 13 -> 13; matrix products, arithmetic and copies ran while one was open for 0% -> 0% of each run, Pallas kernels for 5% -> 5%
where the time goes in v2:
time: 46.3 us; the launch traced here: 46 us
  starting transfers between devices  18.8 us (41%)
  waiting for transfers between devices  15.2 us (33%)
  Pallas kernels  8.06 us (17%)
  local copies, waits for them, and re-layouts  3.05 us (7%)
  between operations  0.77 us (2%)
    ppermute x9, starting transfers between devices, exchanged(): lax.ppermute(value, axis, partner_perm(axis, by))  11.5 us
    ppermute x9, waiting for transfers between devices, exchanged(): lax.ppermute(value, axis, partner_perm(axis, by))  5.93 us
    pallas_call x3, Pallas kernels, vmem_call(): pl.pallas_call(kernel, out_shape=out_shape, in_specs=[spec] * len(args),...  5.67 us
    ppermute x2, starting transfers between devices, shards(): near = [lax.ppermute(own, 'det', tile_perm(e)) for e in (1, 0)]  5.12 us
    ppermute x2, waiting for transfers between devices, shards(): pixels = pixels + lax.ppermute(half[1 + e], 'det', tile_perm(e))  4.59 us
    unnamed x14, local copies, waits for them, and re-layouts  3.01 us
    pallas_call x1, Pallas kernels, prepare(): pl.pallas_call(prep_kernel, out_shape=out_shape, in_specs=[spec, spec, sp...  2.29 us
    ppermute x2, starting transfers between devices, shards(): pixels = pixels + lax.ppermute(half[1 + e], 'det', tile_perm(e))  1.89 us
  transfers between devices with their start and end apart: 16, of which 13 were waited for; matrix products, arithmetic and copies ran while one was open for 0% of the time, Pallas kernels for 5%

profile of v2, /device:TPU:0, one launch (start us, length us, event | category | flops | bytes accessed | tf_op | source)
XLA Modules:
  0.0 46.0 jit_solution(7012974391555840616)
XLA Ops:
  0.6 5.1 %collective-permute-start.1 = (f32[3,8,128]{2,1,0:T(8,128)}, f32[3,8,128]{2,1,0:T(8,128)S(1)}, u32[]{:S(2)}, u32[]{:S(2)}) collective-permute-start(f32[3,8,128]{2,1,0:T(8,128)} %bitcast.46), channel_id=1, source_target_pairs={{0,6},{2,4},{4,2},{6,0},{1,7},{3,5},{5,3},{7,1},{8,14},{10,12},{12... | collective-permute-start | bytes 36872 | tf_op jit(solution)/shard_map/ppermute | solution.py:455
  5.8 1.6 %copy-done = s32[2,16,16384]{2,1,0:T(8,128)S(1)} copy-done((s32[2,16,16384]{2,1,0:T(8,128)S(1)}, s32[2,16,16384]{2,1,0:T(8,128)}, u32[]{:S(2)}) %copy-start) | copy-done | bytes 2097176
  7.3 0.7 %copy-done.3 = s32[16,128]{1,0:T(8,128)S(1)} copy-done((s32[16,128]{1,0:T(8,128)S(1)}, s32[16,128]{1,0:T(8,128)}, u32[]{:S(2)}) %copy-start.3) | copy-done | bytes 8216
  8.0 0.7 %copy-done.4 = f32[3,1,8,128]{3,2,1,0:T(8,128)S(1)} copy-done((f32[3,1,8,128]{3,2,1,0:T(8,128)S(1)}, f32[3,1,8,128]{3,2,1,0:T(8,128)}, u32[]{:S(2)}) %copy-start.4) | copy-done | bytes 12312
  8.9 0.8 %collective-permute-done = f32[3,8,128]{2,1,0:T(8,128)S(1)} collective-permute-done((f32[3,8,128]{2,1,0:T(8,128)}, f32[3,8,128]{2,1,0:T(8,128)S(1)}, u32[]{:S(2)}, u32[]{:S(2)}) %collective-permute-start) | collective-permute-done | bytes 12320 | tf_op jit(solution)/shard_map/ppermute | solution.py:455
  9.7 2.5 %collective-permute-start.4 = (f32[4,3,8,128]{3,2,1,0:T(8,128)S(1)}, f32[4,3,8,128]{3,2,1,0:T(8,128)S(1)}, u32[]{:S(2)}, u32[]{:S(2)}) collective-permute-start(f32[4,3,8,128]{3,2,1,0:T(8,128)S(1)} %pad_maximum_fusion.3.payload), channel_id=1, source_target_pairs={{0,24},{8,16},{16,8},{24,0},{1,25},{9,17},{17,9},{25,1},{2,26},{10... | collective-permute-start | bytes 147464 | tf_op jit(solution)/shard_map/ppermute | solution.py:430
  12.7 0.5 %collective-permute-start.2 = (f32[4,3,8,128]{3,2,1,0:T(8,128)S(1)}, f32[4,3,8,128]{3,2,1,0:T(8,128)S(1)}, u32[]{:S(2)}, u32[]{:S(2)}) collective-permute-start(f32[4,3,8,128]{3,2,1,0:T(8,128)S(1)} %pad_maximum_fusion.3.payload), channel_id=1, source_target_pairs={{0,8},{8,0},{16,24},{24,16},{1,9},{9,1},{17,25},{25,17},{2,10},{10... | collective-permute-start | bytes 147464 | tf_op jit(solution)/shard_map/ppermute | solution.py:430
  13.2 2.3 %shard_map.95 = (f32[4,3,8,128]{3,2,1,0:T(8,128)S(1)}, f32[2,16,16384]{2,1,0:T(8,128)S(1)}, bf16[2048,256]{1,0:T(8,128)(2,1)S(1)}, f32[16,896]{1,0:T(8,128)S(1)}, bf16[544,512]{1,0:T(8,128)(2,1)S(1)}) custom-call(f32[4,3,8,128]{3,2,1,0:T(8,128)S(1)} %pad_maximum_fusion.3.payload, s32[16,128]{1,0:T(8,128)S(1)} %copy-done.3, f32[16,512]{1,0:T(8,128)S(1)} %copy-done.2, ...), custom_call_target="tpu_custom_call" | custom-call | bytes 12000000 | tf_op jit(solution)/shard_map/pallas_call | solution.py:414
  15.5 0.7 %collective-permute-done.3 = f32[4,3,8,128]{3,2,1,0:T(8,128)S(1)} collective-permute-done((f32[4,3,8,128]{3,2,1,0:T(8,128)S(1)}, f32[4,3,8,128]{3,2,1,0:T(8,128)S(1)}, u32[]{:S(2)}, u32[]{:S(2)}) %collective-permute-start.3) | collective-permute-done | bytes 49184 | tf_op jit(solution)/shard_map/ppermute | solution.py:430
  16.9 1.5 %collective-permute-done.5 = f32[66,8,128]{2,1,0:T(8,128)S(1)} collective-permute-done((f32[66,8,128]{2,1,0:T(8,128)S(1)}, f32[66,8,128]{2,1,0:T(8,128)S(1)}, u32[]{:S(2)}, u32[]{:S(2)}) %collective-permute-start.5) | collective-permute-done | bytes 270368 | tf_op jit(solution)/shard_map/ppermute | solution.py:463
  18.5 4.9 %shard_map.96 = f32[2,3,4,8,384]{4,3,2,1,0:T(8,128)S(1)} custom-call(f32[4,4,3,8,128]{4,3,2,1,0:T(8,128)S(1)} %pad_maximum_fusion.1.arrived, f32[1,4,4,3,8,128]{5,4,3,2,1,0:T(8,128)S(1)} %bitcast.34, f32[2,16,16384]{2,1,0:T(8,128)S(1)} %get-tuple-element.15.weights, bf16[2048,256]{1,0:T(8,128)(2,1)S(1)} %get-tuple-element.16.onehot, ...), custom_call_target="tpu_custom_call" | custom-call | tf_op jit(solution)/shard_map/pallas_call | solution.py:372
  23.6 1.2 %collective-permute-done.6 = f32[3,4,8,384]{3,2,1,0:T(8,128)S(1)} collective-permute-done((f32[3,4,8,384]{3,2,1,0:T(8,128)S(1)}, f32[3,4,8,384]{3,2,1,0:T(8,128)S(1)}, u32[]{:S(2)}, u32[]{:S(2)}) %collective-permute-start.6) | collective-permute-done | bytes 147488 | tf_op jit(solution)/shard_map/ppermute | solution.py:486
  24.9 1.9 %collective-permute-start.7 = (f32[4,8,384]{2,1,0:T(8,128)S(1)}, f32[4,8,384]{2,1,0:T(8,128)S(1)}, u32[]{:S(2)}, u32[]{:S(2)}) collective-permute-start(f32[4,8,384]{2,1,0:T(8,128)S(1)} %get-tuple-element.21), channel_id=1, source_target_pairs={{0,6},{2,4},{4,2},{6,0},{1,7},{3,5},{5,3},{7,1},{8,14},{10,12},{12... | collective-permute-start | bytes 147464 | tf_op jit(solution)/shard_map/ppermute | solution.py:489
  26.8 4.4 %collective-permute-done.7 = f32[4,8,384]{2,1,0:T(8,128)S(1)} collective-permute-done((f32[4,8,384]{2,1,0:T(8,128)S(1)}, f32[4,8,384]{2,1,0:T(8,128)S(1)}, u32[]{:S(2)}, u32[]{:S(2)}) %collective-permute-start.7) | collective-permute-done | bytes 49184 | tf_op jit(solution)/shard_map/ppermute | solution.py:489
  31.4 1.6 %collective-permute-start.11 = (f32[4,8,384]{2,1,0:T(8,128)S(1)}, f32[4,8,384]{2,1,0:T(8,128)S(1)}, u32[]{:S(2)}, u32[]{:S(2)}) collective-permute-start(f32[4,8,384]{2,1,0:T(8,128)S(1)} %fusion.2), channel_id=1, source_target_pairs={{0,24},{8,16},{16,8},{24,0},{1,25},{9,17},{17,9},{25,1},{2,26},{10... | collective-permute-start | bytes 147464 | tf_op jit(solution)/shard_map/ppermute | solution.py:430
  33.4 1.5 %collective-permute-start.9 = (f32[4,8,384]{2,1,0:T(8,128)S(1)}, f32[4,8,384]{2,1,0:T(8,128)S(1)}, u32[]{:S(2)}, u32[]{:S(2)}) collective-permute-start(f32[4,8,384]{2,1,0:T(8,128)S(1)} %fusion.2), channel_id=1, source_target_pairs={{0,8},{8,0},{16,24},{24,16},{1,9},{9,1},{17,25},{25,17},{2,10},{10... | collective-permute-start | bytes 147464 | tf_op jit(solution)/shard_map/ppermute | solution.py:430
  34.9 1.6 %collective-permute-done.11 = f32[4,8,384]{2,1,0:T(8,128)S(1)} collective-permute-done((f32[4,8,384]{2,1,0:T(8,128)S(1)}, f32[4,8,384]{2,1,0:T(8,128)S(1)}, u32[]{:S(2)}, u32[]{:S(2)}) %collective-permute-start.11) | collective-permute-done | bytes 49184 | tf_op jit(solution)/shard_map/ppermute | solution.py:430
  36.5 0.5 %collective-permute-done.10 = f32[4,8,384]{2,1,0:T(8,128)S(1)} collective-permute-done((f32[4,8,384]{2,1,0:T(8,128)S(1)}, f32[4,8,384]{2,1,0:T(8,128)S(1)}, u32[]{:S(2)}, u32[]{:S(2)}) %collective-permute-start.10) | collective-permute-done | bytes 49184 | tf_op jit(solution)/shard_map/ppermute | solution.py:430
  37.7 1.2 %collective-permute-done.12 = f32[8,128]{1,0:T(8,128)S(1)} collective-permute-done((f32[8,128]{1,0:T(8,128)S(1)}, f32[8,128]{1,0:T(8,128)S(1)}, u32[]{:S(2)}, u32[]{:S(2)}) %collective-permute-start.12) | collective-permute-done | bytes 4128 | tf_op jit(solution)/shard_map/ppermute | solution.py:440
  38.8 2.0 %collective-permute-start.15 = (f32[8,128]{1,0:T(8,128)S(1)}, f32[8,128]{1,0:T(8,128)S(1)}, u32[]{:S(2)}, u32[]{:S(2)}) collective-permute-start(f32[8,128]{1,0:T(8,128)S(1)} %add.24), channel_id=1, source_target_pairs={{0,6},{2,4},{4,2},{6,0},{1,7},{3,5},{5,3},{7,1},{8,14},{10,12},{12... | collective-permute-start | bytes 12296 | tf_op jit(solution)/shard_map/ppermute | solution.py:430
  40.8 2.4 %collective-permute-start.13 = (f32[8,128]{1,0:T(8,128)S(1)}, f32[8,128]{1,0:T(8,128)S(1)}, u32[]{:S(2)}, u32[]{:S(2)}) collective-permute-start(f32[8,128]{1,0:T(8,128)S(1)} %add.24), channel_id=1, source_target_pairs={{0,2},{2,0},{4,6},{6,4},{1,3},{3,1},{5,7},{7,5},{8,10},{10,8},{12,... | collective-permute-start | bytes 12296 | tf_op jit(solution)/shard_map/ppermute | solution.py:430
  43.2 1.1 %collective-permute-done.15 = f32[8,128]{1,0:T(8,128)S(1)} collective-permute-done((f32[8,128]{1,0:T(8,128)S(1)}, f32[8,128]{1,0:T(8,128)S(1)}, u32[]{:S(2)}, u32[]{:S(2)}) %collective-permute-start.15) | collective-permute-done | bytes 4128 | tf_op jit(solution)/shard_map/ppermute | solution.py:430
  44.3 1.0 %collective-permute-done.14 = f32[8,128]{1,0:T(8,128)S(1)} collective-permute-done((f32[8,128]{1,0:T(8,128)S(1)}, f32[8,128]{1,0:T(8,128)S(1)}, u32[]{:S(2)}, u32[]{:S(2)}) %collective-permute-start.14) | collective-permute-done | bytes 4128 | tf_op jit(solution)/shard_map/ppermute | solution.py:430
  45.3 0.7 %shard_map.98 = (f32[3,1,8,128]{3,2,1,0:T(8,128)}, f32[3,1,8,128]{3,2,1,0:T(8,128)}, f32[3,1,8,128]{3,2,1,0:T(8,128)}) custom-call(f32[8,128]{1,0:T(8,128)S(1)} %add_add_fusion.sums, f32[3,8,128]{2,1,0:T(8,128)S(1)} %get-tuple-element.20.image, f32[4,4,3,8,128]{4,3,2,1,0:T(8,128)S(1)} %pad_maximum_fusion.1.arrived, f32[3,1,8,128]{3,2,1,0:T(8,128)S(1)} %copy-done.5), custom_call_target="tpu_custom_call" | custom-call | tf_op jit(solution)/shard_map/pallas_call | solution.py:372
  (39 shorter events, 2.9 us)
Async XLA Ops:
  0.6 8.2 %collective-permute-start.1 = (f32[3,8,128]{2,1,0:T(8,128)}, f32[3,8,128]{2,1,0:T(8,128)S(1)}, u32[]{:S(2)}, u32[]{:S(2)}) collective-permute-start(f32[3,8,128]{2,1,0:T(8,128)} %bitcast.46), channel_id=1, source_target_pairs={{0,6},{2,4},{4,2},{6,0},{1,7},{3,5},{5,3},{7,1},{8,14},{10,12},{12... | collective-permute-start | bytes 36872 | tf_op jit(solution)/shard_map/ppermute | solution.py:455
  5.7 3.9 %collective-permute-start = (f32[3,8,128]{2,1,0:T(8,128)}, f32[3,8,128]{2,1,0:T(8,128)S(1)}, u32[]{:S(2)}, u32[]{:S(2)}) collective-permute-start(f32[3,8,128]{2,1,0:T(8,128)} %bitcast.47), channel_id=1, source_target_pairs={{0,2},{2,0},{4,6},{6,4},{1,3},{3,1},{5,7},{7,5},{8,10},{10,8},{12,... | collective-permute-start | bytes 36872 | tf_op jit(solution)/shard_map/ppermute | solution.py:455
  5.7 1.6 %copy-start = (s32[2,16,16384]{2,1,0:T(8,128)S(1)}, s32[2,16,16384]{2,1,0:T(8,128)}, u32[]{:S(2)}) copy-start(s32[2,16,16384]{2,1,0:T(8,128)} %stokes.3) | copy-start | bytes 6291460
  7.3 0.7 %copy-start.3 = (s32[16,128]{1,0:T(8,128)S(1)}, s32[16,128]{1,0:T(8,128)}, u32[]{:S(2)}) copy-start(s32[16,128]{1,0:T(8,128)} %hits.3) | copy-start | bytes 24580
  8.0 0.7 %copy-start.4 = (f32[3,1,8,128]{3,2,1,0:T(8,128)S(1)}, f32[3,1,8,128]{3,2,1,0:T(8,128)}, u32[]{:S(2)}) copy-start(f32[3,1,8,128]{3,2,1,0:T(8,128)} %residual.1) | copy-start | bytes 36868
  8.7 0.9 %copy-start.6 = (f32[3,1,8,128]{3,2,1,0:T(8,128)S(1)}, f32[3,1,8,128]{3,2,1,0:T(8,128)}, u32[]{:S(2)}) copy-start(f32[3,1,8,128]{3,2,1,0:T(8,128)} %param.9) | copy-start | bytes 36868
  8.7 4.5 %copy-start.1 = (bf16[544,512]{1,0:T(8,128)(2,1)S(1)}, bf16[544,512]{1,0:T(8,128)(2,1)}, u32[]{:S(2)}) copy-start(bf16[544,512]{1,0:T(8,128)(2,1)} %constant.2.clone.tables_in) | copy-start | bytes 1671172
  8.8 4.5 %copy-start.2 = (f32[16,512]{1,0:T(8,128)S(1)}, f32[16,512]{1,0:T(8,128)}, u32[]{:S(2)}) copy-start(f32[16,512]{1,0:T(8,128)} %inv_noise.1) | copy-start | bytes 98308
  9.7 5.9 %collective-permute-start.4 = (f32[4,3,8,128]{3,2,1,0:T(8,128)S(1)}, f32[4,3,8,128]{3,2,1,0:T(8,128)S(1)}, u32[]{:S(2)}, u32[]{:S(2)}) collective-permute-start(f32[4,3,8,128]{3,2,1,0:T(8,128)S(1)} %pad_maximum_fusion.3.payload), channel_id=1, source_target_pairs={{0,24},{8,16},{16,8},{24,0},{1,25},{9,17},{17,9},{25,1},{2,26},{10... | collective-permute-start | bytes 147464 | tf_op jit(solution)/shard_map/ppermute | solution.py:430
  12.2 4.1 %collective-permute-start.3 = (f32[4,3,8,128]{3,2,1,0:T(8,128)S(1)}, f32[4,3,8,128]{3,2,1,0:T(8,128)S(1)}, u32[]{:S(2)}, u32[]{:S(2)}) collective-permute-start(f32[4,3,8,128]{3,2,1,0:T(8,128)S(1)} %pad_maximum_fusion.3.payload), channel_id=1, source_target_pairs={{0,16},{8,24},{16,0},{24,8},{1,17},{9,25},{17,1},{25,9},{2,18},{10... | collective-permute-start | bytes 147464 | tf_op jit(solution)/shard_map/ppermute | solution.py:430
  12.7 4.1 %collective-permute-start.2 = (f32[4,3,8,128]{3,2,1,0:T(8,128)S(1)}, f32[4,3,8,128]{3,2,1,0:T(8,128)S(1)}, u32[]{:S(2)}, u32[]{:S(2)}) collective-permute-start(f32[4,3,8,128]{3,2,1,0:T(8,128)S(1)} %pad_maximum_fusion.3.payload), channel_id=1, source_target_pairs={{0,8},{8,0},{16,24},{24,16},{1,9},{9,1},{17,25},{25,17},{2,10},{10... | collective-permute-start | bytes 147464 | tf_op jit(solution)/shard_map/ppermute | solution.py:430
  16.8 1.6 %collective-permute-start.5 = (f32[66,8,128]{2,1,0:T(8,128)S(1)}, f32[66,8,128]{2,1,0:T(8,128)S(1)}, u32[]{:S(2)}, u32[]{:S(2)}) collective-permute-start(f32[66,8,128]{2,1,0:T(8,128)S(1)} %pad_maximum_fusion), channel_id=1, source_target_pairs={{0,1},{1,0},{2,3},{3,2},{4,5},{5,4},{6,7},{7,6},{8,9},{9,8},{10,11... | collective-permute-start | bytes 811016 | tf_op jit(solution)/shard_map/ppermute | solution.py:463
  18.5 26.9 %copy-start.5 = (f32[3,1,8,128]{3,2,1,0:T(8,128)S(1)}, f32[3,1,8,128]{3,2,1,0:T(8,128)}, u32[]{:S(2)}) copy-start(f32[3,1,8,128]{3,2,1,0:T(8,128)} %solution_in.1) | copy-start | bytes 36868
  23.4 1.4 %collective-permute-start.6 = (f32[3,4,8,384]{3,2,1,0:T(8,128)S(1)}, f32[3,4,8,384]{3,2,1,0:T(8,128)S(1)}, u32[]{:S(2)}, u32[]{:S(2)}) collective-permute-start(f32[3,4,8,384]{3,2,1,0:T(8,128)S(1)} %slice_bitcast_fusion), channel_id=1, source_target_pairs={{0,1},{1,0},{2,3},{3,2},{4,5},{5,4},{6,7},{7,6},{8,9},{9,8},{10,11... | collective-permute-start | bytes 442376 | tf_op jit(solution)/shard_map/ppermute | solution.py:486
  24.9 6.2 %collective-permute-start.7 = (f32[4,8,384]{2,1,0:T(8,128)S(1)}, f32[4,8,384]{2,1,0:T(8,128)S(1)}, u32[]{:S(2)}, u32[]{:S(2)}) collective-permute-start(f32[4,8,384]{2,1,0:T(8,128)S(1)} %get-tuple-element.21), channel_id=1, source_target_pairs={{0,6},{2,4},{4,2},{6,0},{1,7},{3,5},{5,3},{7,1},{8,14},{10,12},{12... | collective-permute-start | bytes 147464 | tf_op jit(solution)/shard_map/ppermute | solution.py:489
  26.7 4.6 %collective-permute-start.8 = (f32[4,8,384]{2,1,0:T(8,128)S(1)}, f32[4,8,384]{2,1,0:T(8,128)S(1)}, u32[]{:S(2)}, u32[]{:S(2)}) collective-permute-start(f32[4,8,384]{2,1,0:T(8,128)S(1)} %get-tuple-element.22), channel_id=1, source_target_pairs={{0,2},{2,0},{4,6},{6,4},{1,3},{3,1},{5,7},{7,5},{8,10},{10,8},{12,... | collective-permute-start | bytes 147464 | tf_op jit(solution)/shard_map/ppermute | solution.py:489
  31.4 5.1 %collective-permute-start.11 = (f32[4,8,384]{2,1,0:T(8,128)S(1)}, f32[4,8,384]{2,1,0:T(8,128)S(1)}, u32[]{:S(2)}, u32[]{:S(2)}) collective-permute-start(f32[4,8,384]{2,1,0:T(8,128)S(1)} %fusion.2), channel_id=1, source_target_pairs={{0,24},{8,16},{16,8},{24,0},{1,25},{9,17},{17,9},{25,1},{2,26},{10... | collective-permute-start | bytes 147464 | tf_op jit(solution)/shard_map/ppermute | solution.py:430
  32.9 4.1 %collective-permute-start.10 = (f32[4,8,384]{2,1,0:T(8,128)S(1)}, f32[4,8,384]{2,1,0:T(8,128)S(1)}, u32[]{:S(2)}, u32[]{:S(2)}) collective-permute-start(f32[4,8,384]{2,1,0:T(8,128)S(1)} %fusion.2), channel_id=1, source_target_pairs={{0,16},{8,24},{16,0},{24,8},{1,17},{9,25},{17,1},{25,9},{2,18},{10... | collective-permute-start | bytes 147464 | tf_op jit(solution)/shard_map/ppermute | solution.py:430
  33.4 4.1 %collective-permute-start.9 = (f32[4,8,384]{2,1,0:T(8,128)S(1)}, f32[4,8,384]{2,1,0:T(8,128)S(1)}, u32[]{:S(2)}, u32[]{:S(2)}) collective-permute-start(f32[4,8,384]{2,1,0:T(8,128)S(1)} %fusion.2), channel_id=1, source_target_pairs={{0,8},{8,0},{16,24},{24,16},{1,9},{9,1},{17,25},{25,17},{2,10},{10... | collective-permute-start | bytes 147464 | tf_op jit(solution)/shard_map/ppermute | solution.py:430
  37.6 1.2 %collective-permute-start.12 = (f32[8,128]{1,0:T(8,128)S(1)}, f32[8,128]{1,0:T(8,128)S(1)}, u32[]{:S(2)}, u32[]{:S(2)}) collective-permute-start(f32[8,128]{1,0:T(8,128)S(1)} %get-tuple-element.19), channel_id=1, source_target_pairs={{0,1},{1,0},{2,3},{3,2},{4,5},{5,4},{6,7},{7,6},{8,9},{9,8},{10,11... | collective-permute-start | bytes 12296 | tf_op jit(solution)/shard_map/ppermute | solution.py:440
  38.8 5.4 %collective-permute-start.15 = (f32[8,128]{1,0:T(8,128)S(1)}, f32[8,128]{1,0:T(8,128)S(1)}, u32[]{:S(2)}, u32[]{:S(2)}) collective-permute-start(f32[8,128]{1,0:T(8,128)S(1)} %add.24), channel_id=1, source_target_pairs={{0,6},{2,4},{4,2},{6,0},{1,7},{3,5},{5,3},{7,1},{8,14},{10,12},{12... | collective-permute-start | bytes 12296 | tf_op jit(solution)/shard_map/ppermute | solution.py:430
  40.8 4.5 %collective-permute-start.14 = (f32[8,128]{1,0:T(8,128)S(1)}, f32[8,128]{1,0:T(8,128)S(1)}, u32[]{:S(2)}, u32[]{:S(2)}) collective-permute-start(f32[8,128]{1,0:T(8,128)S(1)} %add.24), channel_id=1, source_target_pairs={{0,4},{2,6},{4,0},{6,2},{1,5},{3,7},{5,1},{7,3},{8,12},{10,14},{12... | collective-permute-start | bytes 12296 | tf_op jit(solution)/shard_map/ppermute | solution.py:430
  40.8 4.5 %collective-permute-start.13 = (f32[8,128]{1,0:T(8,128)S(1)}, f32[8,128]{1,0:T(8,128)S(1)}, u32[]{:S(2)}, u32[]{:S(2)}) collective-permute-start(f32[8,128]{1,0:T(8,128)S(1)} %add.24), channel_id=1, source_target_pairs={{0,2},{2,0},{4,6},{6,4},{1,3},{3,1},{5,7},{7,5},{8,10},{10,8},{12,... | collective-permute-start | bytes 12296 | tf_op jit(solution)/shard_map/ppermute | solution.py:430

commit v3 on v2

--- a/solution.py
+++ b/solution.py
@@ -199,7 +199,8 @@
     depth = mhl.shape[0]
     local = 3 * tile_blocks
     segs = blocks // PER_SEG
-    chunk_segs = 32
+    halves = 2
+    chunk_segs = segs // halves
     chunk_blocks = chunk_segs * PER_SEG
     chunk = chunk_blocks * rows
     tiles = (1, tile_sides(1)[0], tile_sides(0)[0])
@@ -243,19 +244,16 @@
         for j in range(PER_SEG):
             x[place, pl.ds(j * LANES, LANES)] = scan(picked, j, side[j], side[PER_SEG + j])
 
-    def scan_chunk(i, carry):
-        ones = onehot[pl.ds(pl.multiple_of(i * chunk, chunk), chunk), :]
+    def scan_part(i):
+        ones = onehot[i * chunk:(i + 1) * chunk, :]
         picked = dot(ones, mhl[...])
         picked = picked[:, :3 * LANES] + picked[:, 3 * LANES:]
         for j in range(chunk_blocks):
-            lanes = pl.ds(pl.multiple_of(i * chunk_blocks * LANES, LANES) + j * LANES, LANES)
-            at = pl.multiple_of((i * chunk_segs + 1 + j // PER_SEG) * rows, rows)
+            lanes = pl.ds((i * chunk_blocks + j) * LANES, LANES)
+            at = (i * chunk_segs + 1 + j // PER_SEG) * rows
             x[pl.ds(at, rows), pl.ds((j % PER_SEG) * LANES, LANES)] = scan(
                 picked, j, weights[0, :, lanes], weights[1, :, lanes]
             )
-        return carry
-
-    lax.fori_loop(0, segs // chunk_segs, scan_chunk, 0)
 
     g1h, g1l = tables_in[:HALF, :HALF], tables_in[:HALF, HALF:]
     g2h, g2l = tables_in[HALF:SEG, :HALF], tables_in[HALF:SEG, HALF:]
@@ -263,68 +261,83 @@
     turn = turn[:, :HALF] + turn[:, HALF:]
     cos, sin = turn[:1], turn[16:17]
     quarter = HALF // 2
-    part = segs * rows
+    part = chunk_segs * rows
 
     def weighted(coeffs, at, width):
         scale = scales[:, at:at + width]
-        return (coeffs.reshape(segs, rows, width) * scale[None]).reshape(part, width)
-
-    middle = x[pl.ds(rows, part), :]
-    around = 0.5 * (x[pl.ds(0, part), :] + x[pl.ds(2 * rows, part), :])
-    even = middle + around
-    odd = middle - around
-    coeffs = dot3(dot, even[:, :HALF] - even[:, HALF:], g2h, g2l)
-    second = dot3(dot_t, weighted(coeffs, HALF, HALF), g2h, g2l)
-    real = cos * odd[:, :HALF] - sin * odd[:, HALF:]
-    imag = sin * odd[:, :HALF] + cos * odd[:, HALF:]
-    coeffs = dot3(
-        dot, jnp.concatenate([even[:, :HALF] + even[:, HALF:], real, imag], axis=0), g1h, g1l
-    )
-    real, imag = coeffs[part:2 * part], coeffs[2 * part:]
-    cross = SEG + HALF
-    mixed = [
-        weighted(real[:, :quarter], SEG, quarter) - weighted(imag[:, quarter:], cross, quarter),
-        weighted(real[:, quarter:], SEG + quarter, quarter) + weighted(imag[:, :quarter], cross, quarter),
-        weighted(imag[:, :quarter], SEG, quarter) + weighted(real[:, quarter:], cross, quarter),
-        weighted(imag[:, quarter:], SEG + quarter, quarter) - weighted(real[:, :quarter], cross, quarter),
-    ]
-    coeffs = jnp.concatenate(
-        [
-            weighted(coeffs[:part], 0, HALF),
-            jnp.concatenate(mixed[:2], axis=1),
-            jnp.concatenate(mixed[2:], axis=1),
-        ],
-        axis=0,
-    )
-    back = dot3(dot_t, coeffs, g1h, g1l)
-    first, real, imag = back[:part], back[part:2 * part], back[2 * part:]
-    f[:, :HALF] = first + second + cos * real + sin * imag
-    f[:, HALF:] = first - second - sin * real + cos * imag
-
-    total[...] = jnp.zeros(total.shape, F32)
-
-    def bin_chunk(i, carry):
+        return (coeffs.reshape(chunk_segs, rows, width) * scale[None]).reshape(part, width)
+
+    def forward(i):
+        base = i * part
+        middle = x[pl.ds(base + rows, part), :]
+        around = 0.5 * (x[pl.ds(base, part), :] + x[pl.ds(base + 2 * rows, part), :])
+        even = middle + around
+        odd = middle - around
+        real = cos * odd[:, :HALF] - sin * odd[:, HALF:]
+        imag = sin * odd[:, :HALF] + cos * odd[:, HALF:]
+        most = jnp.concatenate([even[:, :HALF] + even[:, HALF:], real, imag], axis=0)
+        return (
+            dot3(dot, even[:, :HALF] - even[:, HALF:], g2h, g2l),
+            dot3(dot, most, g1h, g1l),
+        )
+
+    def scaled(found):
+        second, coeffs = found
+        real, imag = coeffs[part:2 * part], coeffs[2 * part:]
+        near, far = slice(None, quarter), slice(quarter, None)
+        cross = SEG + HALF
+        turned_real = [
+            weighted(real[:, near], SEG, quarter) - weighted(imag[:, far], cross, quarter),
+            weighted(real[:, far], SEG + quarter, quarter) + weighted(imag[:, near], cross, quarter),
+        ]
+        turned_imag = [
+            weighted(imag[:, near], SEG, quarter) + weighted(real[:, far], cross, quarter),
+            weighted(imag[:, far], SEG + quarter, quarter) - weighted(real[:, near], cross, quarter),
+        ]
+        most = [weighted(coeffs[:part], 0, HALF)]
+        most += [jnp.concatenate(turned, axis=1) for turned in (turned_real, turned_imag)]
+        return weighted(second, HALF, HALF), jnp.concatenate(most, axis=0)
+
+    def backward(i, coeffs):
+        second = dot3(dot_t, coeffs[0], g2h, g2l)
+        back = dot3(dot_t, coeffs[1], g1h, g1l)
+        first, real, imag = back[:part], back[part:2 * part], back[2 * part:]
+        place = pl.ds(i * part, part)
+        f[place, :HALF] = first + second + cos * real + sin * imag
+        f[place, HALF:] = first - second - sin * real + cos * imag
+
+    def bin_part(i):
         values = []
         for j in range(chunk_blocks):
-            lanes = pl.ds(pl.multiple_of(i * chunk_blocks * LANES, LANES) + j * LANES, LANES)
-            at = pl.multiple_of((i * chunk_segs + j // PER_SEG) * rows, rows)
+            lanes = pl.ds((i * chunk_blocks + j) * LANES, LANES)
+            at = (i * chunk_segs + j // PER_SEG) * rows
             value = f[pl.ds(at, rows), pl.ds((j % PER_SEG) * LANES, LANES)]
             values.append(
                 jnp.concatenate(
                     [value, weights[0, :, lanes] * value, weights[1, :, lanes] * value], axis=1
                 )
             )
-        ones = onehot[pl.ds(pl.multiple_of(i * chunk, chunk), chunk), :local]
         sums = lax.dot_general(
-            ones,
+            onehot[i * chunk:(i + 1) * chunk, :local],
             jnp.concatenate(split(jnp.concatenate(values, axis=0)), axis=1),
             (((0,), (0,)), ((), ())),
             preferred_element_type=F32,
         )
-        total[...] += sums[:, :3 * LANES] + sums[:, 3 * LANES:]
-        return carry
-
-    lax.fori_loop(0, segs // chunk_segs, bin_chunk, 0)
+        return sums[:, :3 * LANES] + sums[:, 3 * LANES:]
+
+    scan_part(0)
+    found = []
+    for i in range(1, halves):
+        scan_part(i)
+        found.append(forward(i - 1))
+    found.append(forward(halves - 1))
+    sums = []
+    for i in range(halves):
+        backward(i, scaled(found[i]))
+        if i:
+            sums.append(bin_part(i - 1))
+    sums.append(bin_part(halves - 1))
+    total[...] = sum(sums)
     tiles = (1, tile_sides(0)[1], tile_sides(1)[1])
     for k in range(times):
         for s in range(3):

time: 46.3 us -> 45.6 us (0.985)
  Pallas kernels: 8.06 us -> 7.31 us
    pallas_call x3, Pallas kernels: 5.67 us -> 4.92 us  [vmem_call(): pl.pallas_call(kernel, out_shape=out_shape, in_specs=[spec] * len(args),...]
where the time goes in v3:
time: 45.6 us; the launch traced here: 45.3 us
  starting transfers between devices  18.9 us (41%)
  waiting for transfers between devices  15.2 us (33%)
  Pallas kernels  7.31 us (16%)
  local copies, waits for them, and re-layouts  3.05 us (7%)
  between operations  0.77 us (2%)
    ppermute x9, starting transfers between devices, exchanged(): lax.ppermute(value, axis, partner_perm(axis, by))  11.5 us
    ppermute x9, waiting for transfers between devices, exchanged(): lax.ppermute(value, axis, partner_perm(axis, by))  5.94 us
    ppermute x2, starting transfers between devices, shards(): near = [lax.ppermute(own, 'det', tile_perm(e)) for e in (1, 0)]  5.12 us
    pallas_call x3, Pallas kernels, vmem_call(): pl.pallas_call(kernel, out_shape=out_shape, in_specs=[spec] * len(args),...  4.92 us
    ppermute x2, waiting for transfers between devices, shards(): pixels = pixels + lax.ppermute(half[1 + e], 'det', tile_perm(e))  4.59 us
    unnamed x14, local copies, waits for them, and re-layouts  3.01 us
    pallas_call x1, Pallas kernels, prepare(): pl.pallas_call(prep_kernel, out_shape=out_shape, in_specs=[spec, spec, sp...  2.29 us
    ppermute x2, starting transfers between devices, shards(): pixels = pixels + lax.ppermute(half[1 + e], 'det', tile_perm(e))  1.9 us
  transfers between devices with their start and end apart: 16, of which 13 were waited for; matrix products, arithmetic and copies ran while one was open for 0% of the time, Pallas kernels for 5%

profile of v3, /device:TPU:0, one launch (start us, length us, event | category | flops | bytes accessed | tf_op | source)
XLA Modules:
  0.0 45.3 jit_solution(12827013473024110987)
XLA Ops:
  0.6 5.1 %collective-permute-start.1 = (f32[3,8,128]{2,1,0:T(8,128)}, f32[3,8,128]{2,1,0:T(8,128)S(1)}, u32[]{:S(2)}, u32[]{:S(2)}) collective-permute-start(f32[3,8,128]{2,1,0:T(8,128)} %bitcast.46), channel_id=1, source_target_pairs={{0,6},{2,4},{4,2},{6,0},{1,7},{3,5},{5,3},{7,1},{8,14},{10,12},{12... | collective-permute-start | bytes 36872 | tf_op jit(solution)/shard_map/ppermute | solution.py:468
  5.8 1.6 %copy-done = s32[2,16,16384]{2,1,0:T(8,128)S(1)} copy-done((s32[2,16,16384]{2,1,0:T(8,128)S(1)}, s32[2,16,16384]{2,1,0:T(8,128)}, u32[]{:S(2)}) %copy-start) | copy-done | bytes 2097176
  7.3 0.7 %copy-done.3 = s32[16,128]{1,0:T(8,128)S(1)} copy-done((s32[16,128]{1,0:T(8,128)S(1)}, s32[16,128]{1,0:T(8,128)}, u32[]{:S(2)}) %copy-start.3) | copy-done | bytes 8216
  8.0 0.7 %copy-done.4 = f32[3,1,8,128]{3,2,1,0:T(8,128)S(1)} copy-done((f32[3,1,8,128]{3,2,1,0:T(8,128)S(1)}, f32[3,1,8,128]{3,2,1,0:T(8,128)}, u32[]{:S(2)}) %copy-start.4) | copy-done | bytes 12312
  8.9 0.8 %collective-permute-done = f32[3,8,128]{2,1,0:T(8,128)S(1)} collective-permute-done((f32[3,8,128]{2,1,0:T(8,128)}, f32[3,8,128]{2,1,0:T(8,128)S(1)}, u32[]{:S(2)}, u32[]{:S(2)}) %collective-permute-start) | collective-permute-done | bytes 12320 | tf_op jit(solution)/shard_map/ppermute | solution.py:468
  9.7 2.5 %collective-permute-start.4 = (f32[4,3,8,128]{3,2,1,0:T(8,128)S(1)}, f32[4,3,8,128]{3,2,1,0:T(8,128)S(1)}, u32[]{:S(2)}, u32[]{:S(2)}) collective-permute-start(f32[4,3,8,128]{3,2,1,0:T(8,128)S(1)} %pad_maximum_fusion.3.payload), channel_id=1, source_target_pairs={{0,24},{8,16},{16,8},{24,0},{1,25},{9,17},{17,9},{25,1},{2,26},{10... | collective-permute-start | bytes 147464 | tf_op jit(solution)/shard_map/ppermute | solution.py:443
  12.7 0.5 %collective-permute-start.2 = (f32[4,3,8,128]{3,2,1,0:T(8,128)S(1)}, f32[4,3,8,128]{3,2,1,0:T(8,128)S(1)}, u32[]{:S(2)}, u32[]{:S(2)}) collective-permute-start(f32[4,3,8,128]{3,2,1,0:T(8,128)S(1)} %pad_maximum_fusion.3.payload), channel_id=1, source_target_pairs={{0,8},{8,0},{16,24},{24,16},{1,9},{9,1},{17,25},{25,17},{2,10},{10... | collective-permute-start | bytes 147464 | tf_op jit(solution)/shard_map/ppermute | solution.py:443
  13.2 2.3 %shard_map.95 = (f32[4,3,8,128]{3,2,1,0:T(8,128)S(1)}, f32[2,16,16384]{2,1,0:T(8,128)S(1)}, bf16[2048,256]{1,0:T(8,128)(2,1)S(1)}, f32[16,896]{1,0:T(8,128)S(1)}, bf16[544,512]{1,0:T(8,128)(2,1)S(1)}) custom-call(f32[4,3,8,128]{3,2,1,0:T(8,128)S(1)} %pad_maximum_fusion.3.payload, s32[16,128]{1,0:T(8,128)S(1)} %copy-done.3, f32[16,512]{1,0:T(8,128)S(1)} %copy-done.2, ...), custom_call_target="tpu_custom_call" | custom-call | bytes 12000000 | tf_op jit(solution)/shard_map/pallas_call | solution.py:427
  15.5 0.7 %collective-permute-done.3 = f32[4,3,8,128]{3,2,1,0:T(8,128)S(1)} collective-permute-done((f32[4,3,8,128]{3,2,1,0:T(8,128)S(1)}, f32[4,3,8,128]{3,2,1,0:T(8,128)S(1)}, u32[]{:S(2)}, u32[]{:S(2)}) %collective-permute-start.3) | collective-permute-done | bytes 49184 | tf_op jit(solution)/shard_map/ppermute | solution.py:443
  16.9 1.5 %collective-permute-done.5 = f32[66,8,128]{2,1,0:T(8,128)S(1)} collective-permute-done((f32[66,8,128]{2,1,0:T(8,128)S(1)}, f32[66,8,128]{2,1,0:T(8,128)S(1)}, u32[]{:S(2)}, u32[]{:S(2)}) %collective-permute-start.5) | collective-permute-done | bytes 270368 | tf_op jit(solution)/shard_map/ppermute | solution.py:476
  18.5 4.2 %shard_map.96 = f32[2,3,4,8,384]{4,3,2,1,0:T(8,128)S(1)} custom-call(f32[4,4,3,8,128]{4,3,2,1,0:T(8,128)S(1)} %pad_maximum_fusion.1.arrived, f32[1,4,4,3,8,128]{5,4,3,2,1,0:T(8,128)S(1)} %bitcast.34, f32[2,16,16384]{2,1,0:T(8,128)S(1)} %get-tuple-element.15.weights, bf16[2048,256]{1,0:T(8,128)(2,1)S(1)} %get-tuple-element.16.onehot, ...), custom_call_target="tpu_custom_call" | custom-call | tf_op jit(solution)/shard_map/pallas_call | solution.py:385
  22.9 1.2 %collective-permute-done.6 = f32[3,4,8,384]{3,2,1,0:T(8,128)S(1)} collective-permute-done((f32[3,4,8,384]{3,2,1,0:T(8,128)S(1)}, f32[3,4,8,384]{3,2,1,0:T(8,128)S(1)}, u32[]{:S(2)}, u32[]{:S(2)}) %collective-permute-start.6) | collective-permute-done | bytes 147488 | tf_op jit(solution)/shard_map/ppermute | solution.py:499
  24.1 1.9 %collective-permute-start.7 = (f32[4,8,384]{2,1,0:T(8,128)S(1)}, f32[4,8,384]{2,1,0:T(8,128)S(1)}, u32[]{:S(2)}, u32[]{:S(2)}) collective-permute-start(f32[4,8,384]{2,1,0:T(8,128)S(1)} %get-tuple-element.21), channel_id=1, source_target_pairs={{0,6},{2,4},{4,2},{6,0},{1,7},{3,5},{5,3},{7,1},{8,14},{10,12},{12... | collective-permute-start | bytes 147464 | tf_op jit(solution)/shard_map/ppermute | solution.py:502
  26.0 4.4 %collective-permute-done.7 = f32[4,8,384]{2,1,0:T(8,128)S(1)} collective-permute-done((f32[4,8,384]{2,1,0:T(8,128)S(1)}, f32[4,8,384]{2,1,0:T(8,128)S(1)}, u32[]{:S(2)}, u32[]{:S(2)}) %collective-permute-start.7) | collective-permute-done | bytes 49184 | tf_op jit(solution)/shard_map/ppermute | solution.py:502
  30.6 1.6 %collective-permute-start.11 = (f32[4,8,384]{2,1,0:T(8,128)S(1)}, f32[4,8,384]{2,1,0:T(8,128)S(1)}, u32[]{:S(2)}, u32[]{:S(2)}) collective-permute-start(f32[4,8,384]{2,1,0:T(8,128)S(1)} %fusion.2), channel_id=1, source_target_pairs={{0,24},{8,16},{16,8},{24,0},{1,25},{9,17},{17,9},{25,1},{2,26},{10... | collective-permute-start | bytes 147464 | tf_op jit(solution)/shard_map/ppermute | solution.py:443
  32.7 1.5 %collective-permute-start.9 = (f32[4,8,384]{2,1,0:T(8,128)S(1)}, f32[4,8,384]{2,1,0:T(8,128)S(1)}, u32[]{:S(2)}, u32[]{:S(2)}) collective-permute-start(f32[4,8,384]{2,1,0:T(8,128)S(1)} %fusion.2), channel_id=1, source_target_pairs={{0,8},{8,0},{16,24},{24,16},{1,9},{9,1},{17,25},{25,17},{2,10},{10... | collective-permute-start | bytes 147464 | tf_op jit(solution)/shard_map/ppermute | solution.py:443
  34.2 1.6 %collective-permute-done.11 = f32[4,8,384]{2,1,0:T(8,128)S(1)} collective-permute-done((f32[4,8,384]{2,1,0:T(8,128)S(1)}, f32[4,8,384]{2,1,0:T(8,128)S(1)}, u32[]{:S(2)}, u32[]{:S(2)}) %collective-permute-start.11) | collective-permute-done | bytes 49184 | tf_op jit(solution)/shard_map/ppermute | solution.py:443
  35.7 0.5 %collective-permute-done.10 = f32[4,8,384]{2,1,0:T(8,128)S(1)} collective-permute-done((f32[4,8,384]{2,1,0:T(8,128)S(1)}, f32[4,8,384]{2,1,0:T(8,128)S(1)}, u32[]{:S(2)}, u32[]{:S(2)}) %collective-permute-start.10) | collective-permute-done | bytes 49184 | tf_op jit(solution)/shard_map/ppermute | solution.py:443
  37.0 1.2 %collective-permute-done.12 = f32[8,128]{1,0:T(8,128)S(1)} collective-permute-done((f32[8,128]{1,0:T(8,128)S(1)}, f32[8,128]{1,0:T(8,128)S(1)}, u32[]{:S(2)}, u32[]{:S(2)}) %collective-permute-start.12) | collective-permute-done | bytes 4128 | tf_op jit(solution)/shard_map/ppermute | solution.py:453
  38.1 2.0 %collective-permute-start.15 = (f32[8,128]{1,0:T(8,128)S(1)}, f32[8,128]{1,0:T(8,128)S(1)}, u32[]{:S(2)}, u32[]{:S(2)}) collective-permute-start(f32[8,128]{1,0:T(8,128)S(1)} %add.24), channel_id=1, source_target_pairs={{0,6},{2,4},{4,2},{6,0},{1,7},{3,5},{5,3},{7,1},{8,14},{10,12},{12... | collective-permute-start | bytes 12296 | tf_op jit(solution)/shard_map/ppermute | solution.py:443
  40.1 2.4 %collective-permute-start.13 = (f32[8,128]{1,0:T(8,128)S(1)}, f32[8,128]{1,0:T(8,128)S(1)}, u32[]{:S(2)}, u32[]{:S(2)}) collective-permute-start(f32[8,128]{1,0:T(8,128)S(1)} %add.24), channel_id=1, source_target_pairs={{0,2},{2,0},{4,6},{6,4},{1,3},{3,1},{5,7},{7,5},{8,10},{10,8},{12,... | collective-permute-start | bytes 12296 | tf_op jit(solution)/shard_map/ppermute | solution.py:443
  42.5 1.1 %collective-permute-done.15 = f32[8,128]{1,0:T(8,128)S(1)} collective-permute-done((f32[8,128]{1,0:T(8,128)S(1)}, f32[8,128]{1,0:T(8,128)S(1)}, u32[]{:S(2)}, u32[]{:S(2)}) %collective-permute-start.15) | collective-permute-done | bytes 4128 | tf_op jit(solution)/shard_map/ppermute | solution.py:443
  43.5 1.0 %collective-permute-done.14 = f32[8,128]{1,0:T(8,128)S(1)} collective-permute-done((f32[8,128]{1,0:T(8,128)S(1)}, f32[8,128]{1,0:T(8,128)S(1)}, u32[]{:S(2)}, u32[]{:S(2)}) %collective-permute-start.14) | collective-permute-done | bytes 4128 | tf_op jit(solution)/shard_map/ppermute | solution.py:443
  44.6 0.7 %shard_map.98 = (f32[3,1,8,128]{3,2,1,0:T(8,128)}, f32[3,1,8,128]{3,2,1,0:T(8,128)}, f32[3,1,8,128]{3,2,1,0:T(8,128)}) custom-call(f32[8,128]{1,0:T(8,128)S(1)} %add_add_fusion.sums, f32[3,8,128]{2,1,0:T(8,128)S(1)} %get-tuple-element.20.image, f32[4,4,3,8,128]{4,3,2,1,0:T(8,128)S(1)} %pad_maximum_fusion.1.arrived, f32[3,1,8,128]{3,2,1,0:T(8,128)S(1)} %copy-done.5), custom_call_target="tpu_custom_call" | custom-call | tf_op jit(solution)/shard_map/pallas_call | solution.py:385
  (39 shorter events, 3.0 us)
Async XLA Ops:
  0.6 8.2 %collective-permute-start.1 = (f32[3,8,128]{2,1,0:T(8,128)}, f32[3,8,128]{2,1,0:T(8,128)S(1)}, u32[]{:S(2)}, u32[]{:S(2)}) collective-permute-start(f32[3,8,128]{2,1,0:T(8,128)} %bitcast.46), channel_id=1, source_target_pairs={{0,6},{2,4},{4,2},{6,0},{1,7},{3,5},{5,3},{7,1},{8,14},{10,12},{12... | collective-permute-start | bytes 36872 | tf_op jit(solution)/shard_map/ppermute | solution.py:468
  5.7 3.9 %collective-permute-start = (f32[3,8,128]{2,1,0:T(8,128)}, f32[3,8,128]{2,1,0:T(8,128)S(1)}, u32[]{:S(2)}, u32[]{:S(2)}) collective-permute-start(f32[3,8,128]{2,1,0:T(8,128)} %bitcast.47), channel_id=1, source_target_pairs={{0,2},{2,0},{4,6},{6,4},{1,3},{3,1},{5,7},{7,5},{8,10},{10,8},{12,... | collective-permute-start | bytes 36872 | tf_op jit(solution)/shard_map/ppermute | solution.py:468
  5.7 1.6 %copy-start = (s32[2,16,16384]{2,1,0:T(8,128)S(1)}, s32[2,16,16384]{2,1,0:T(8,128)}, u32[]{:S(2)}) copy-start(s32[2,16,16384]{2,1,0:T(8,128)} %stokes.3) | copy-start | bytes 6291460
  7.3 0.7 %copy-start.3 = (s32[16,128]{1,0:T(8,128)S(1)}, s32[16,128]{1,0:T(8,128)}, u32[]{:S(2)}) copy-start(s32[16,128]{1,0:T(8,128)} %hits.3) | copy-start | bytes 24580
  8.0 0.7 %copy-start.4 = (f32[3,1,8,128]{3,2,1,0:T(8,128)S(1)}, f32[3,1,8,128]{3,2,1,0:T(8,128)}, u32[]{:S(2)}) copy-start(f32[3,1,8,128]{3,2,1,0:T(8,128)} %residual.1) | copy-start | bytes 36868
  8.7 0.9 %copy-start.6 = (f32[3,1,8,128]{3,2,1,0:T(8,128)S(1)}, f32[3,1,8,128]{3,2,1,0:T(8,128)}, u32[]{:S(2)}) copy-start(f32[3,1,8,128]{3,2,1,0:T(8,128)} %param.9) | copy-start | bytes 36868
  8.7 4.5 %copy-start.1 = (bf16[544,512]{1,0:T(8,128)(2,1)S(1)}, bf16[544,512]{1,0:T(8,128)(2,1)}, u32[]{:S(2)}) copy-start(bf16[544,512]{1,0:T(8,128)(2,1)} %constant.2.clone.tables_in) | copy-start | bytes 1671172
  8.8 4.5 %copy-start.2 = (f32[16,512]{1,0:T(8,128)S(1)}, f32[16,512]{1,0:T(8,128)}, u32[]{:S(2)}) copy-start(f32[16,512]{1,0:T(8,128)} %inv_noise.1) | copy-start | bytes 98308
  9.7 5.9 %collective-permute-start.4 = (f32[4,3,8,128]{3,2,1,0:T(8,128)S(1)}, f32[4,3,8,128]{3,2,1,0:T(8,128)S(1)}, u32[]{:S(2)}, u32[]{:S(2)}) collective-permute-start(f32[4,3,8,128]{3,2,1,0:T(8,128)S(1)} %pad_maximum_fusion.3.payload), channel_id=1, source_target_pairs={{0,24},{8,16},{16,8},{24,0},{1,25},{9,17},{17,9},{25,1},{2,26},{10... | collective-permute-start | bytes 147464 | tf_op jit(solution)/shard_map/ppermute | solution.py:443
  12.2 4.1 %collective-permute-start.3 = (f32[4,3,8,128]{3,2,1,0:T(8,128)S(1)}, f32[4,3,8,128]{3,2,1,0:T(8,128)S(1)}, u32[]{:S(2)}, u32[]{:S(2)}) collective-permute-start(f32[4,3,8,128]{3,2,1,0:T(8,128)S(1)} %pad_maximum_fusion.3.payload), channel_id=1, source_target_pairs={{0,16},{8,24},{16,0},{24,8},{1,17},{9,25},{17,1},{25,9},{2,18},{10... | collective-permute-start | bytes 147464 | tf_op jit(solution)/shard_map/ppermute | solution.py:443
  12.7 4.1 %collective-permute-start.2 = (f32[4,3,8,128]{3,2,1,0:T(8,128)S(1)}, f32[4,3,8,128]{3,2,1,0:T(8,128)S(1)}, u32[]{:S(2)}, u32[]{:S(2)}) collective-permute-start(f32[4,3,8,128]{3,2,1,0:T(8,128)S(1)} %pad_maximum_fusion.3.payload), channel_id=1, source_target_pairs={{0,8},{8,0},{16,24},{24,16},{1,9},{9,1},{17,25},{25,17},{2,10},{10... | collective-permute-start | bytes 147464 | tf_op jit(solution)/shard_map/ppermute | solution.py:443
  16.8 1.6 %collective-permute-start.5 = (f32[66,8,128]{2,1,0:T(8,128)S(1)}, f32[66,8,128]{2,1,0:T(8,128)S(1)}, u32[]{:S(2)}, u32[]{:S(2)}) collective-permute-start(f32[66,8,128]{2,1,0:T(8,128)S(1)} %pad_maximum_fusion), channel_id=1, source_target_pairs={{0,1},{1,0},{2,3},{3,2},{4,5},{5,4},{6,7},{7,6},{8,9},{9,8},{10,11... | collective-permute-start | bytes 811016 | tf_op jit(solution)/shard_map/ppermute | solution.py:476
  18.5 26.1 %copy-start.5 = (f32[3,1,8,128]{3,2,1,0:T(8,128)S(1)}, f32[3,1,8,128]{3,2,1,0:T(8,128)}, u32[]{:S(2)}) copy-start(f32[3,1,8,128]{3,2,1,0:T(8,128)} %solution_in.1) | copy-start | bytes 36868
  22.6 1.4 %collective-permute-start.6 = (f32[3,4,8,384]{3,2,1,0:T(8,128)S(1)}, f32[3,4,8,384]{3,2,1,0:T(8,128)S(1)}, u32[]{:S(2)}, u32[]{:S(2)}) collective-permute-start(f32[3,4,8,384]{3,2,1,0:T(8,128)S(1)} %slice_bitcast_fusion), channel_id=1, source_target_pairs={{0,1},{1,0},{2,3},{3,2},{4,5},{5,4},{6,7},{7,6},{8,9},{9,8},{10,11... | collective-permute-start | bytes 442376 | tf_op jit(solution)/shard_map/ppermute | solution.py:499
  24.1 6.3 %collective-permute-start.7 = (f32[4,8,384]{2,1,0:T(8,128)S(1)}, f32[4,8,384]{2,1,0:T(8,128)S(1)}, u32[]{:S(2)}, u32[]{:S(2)}) collective-permute-start(f32[4,8,384]{2,1,0:T(8,128)S(1)} %get-tuple-element.21), channel_id=1, source_target_pairs={{0,6},{2,4},{4,2},{6,0},{1,7},{3,5},{5,3},{7,1},{8,14},{10,12},{12... | collective-permute-start | bytes 147464 | tf_op jit(solution)/shard_map/ppermute | solution.py:502
  26.0 4.6 %collective-permute-start.8 = (f32[4,8,384]{2,1,0:T(8,128)S(1)}, f32[4,8,384]{2,1,0:T(8,128)S(1)}, u32[]{:S(2)}, u32[]{:S(2)}) collective-permute-start(f32[4,8,384]{2,1,0:T(8,128)S(1)} %get-tuple-element.22), channel_id=1, source_target_pairs={{0,2},{2,0},{4,6},{6,4},{1,3},{3,1},{5,7},{7,5},{8,10},{10,8},{12,... | collective-permute-start | bytes 147464 | tf_op jit(solution)/shard_map/ppermute | solution.py:502
  30.6 5.1 %collective-permute-start.11 = (f32[4,8,384]{2,1,0:T(8,128)S(1)}, f32[4,8,384]{2,1,0:T(8,128)S(1)}, u32[]{:S(2)}, u32[]{:S(2)}) collective-permute-start(f32[4,8,384]{2,1,0:T(8,128)S(1)} %fusion.2), channel_id=1, source_target_pairs={{0,24},{8,16},{16,8},{24,0},{1,25},{9,17},{17,9},{25,1},{2,26},{10... | collective-permute-start | bytes 147464 | tf_op jit(solution)/shard_map/ppermute | solution.py:443
  32.2 4.1 %collective-permute-start.10 = (f32[4,8,384]{2,1,0:T(8,128)S(1)}, f32[4,8,384]{2,1,0:T(8,128)S(1)}, u32[]{:S(2)}, u32[]{:S(2)}) collective-permute-start(f32[4,8,384]{2,1,0:T(8,128)S(1)} %fusion.2), channel_id=1, source_target_pairs={{0,16},{8,24},{16,0},{24,8},{1,17},{9,25},{17,1},{25,9},{2,18},{10... | collective-permute-start | bytes 147464 | tf_op jit(solution)/shard_map/ppermute | solution.py:443
  32.7 4.1 %collective-permute-start.9 = (f32[4,8,384]{2,1,0:T(8,128)S(1)}, f32[4,8,384]{2,1,0:T(8,128)S(1)}, u32[]{:S(2)}, u32[]{:S(2)}) collective-permute-start(f32[4,8,384]{2,1,0:T(8,128)S(1)} %fusion.2), channel_id=1, source_target_pairs={{0,8},{8,0},{16,24},{24,16},{1,9},{9,1},{17,25},{25,17},{2,10},{10... | collective-permute-start | bytes 147464 | tf_op jit(solution)/shard_map/ppermute | solution.py:443
  36.9 1.2 %collective-permute-start.12 = (f32[8,128]{1,0:T(8,128)S(1)}, f32[8,128]{1,0:T(8,128)S(1)}, u32[]{:S(2)}, u32[]{:S(2)}) collective-permute-start(f32[8,128]{1,0:T(8,128)S(1)} %get-tuple-element.19), channel_id=1, source_target_pairs={{0,1},{1,0},{2,3},{3,2},{4,5},{5,4},{6,7},{7,6},{8,9},{9,8},{10,11... | collective-permute-start | bytes 12296 | tf_op jit(solution)/shard_map/ppermute | solution.py:453
  38.1 5.4 %collective-permute-start.15 = (f32[8,128]{1,0:T(8,128)S(1)}, f32[8,128]{1,0:T(8,128)S(1)}, u32[]{:S(2)}, u32[]{:S(2)}) collective-permute-start(f32[8,128]{1,0:T(8,128)S(1)} %add.24), channel_id=1, source_target_pairs={{0,6},{2,4},{4,2},{6,0},{1,7},{3,5},{5,3},{7,1},{8,14},{10,12},{12... | collective-permute-start | bytes 12296 | tf_op jit(solution)/shard_map/ppermute | solution.py:443
  40.1 4.5 %collective-permute-start.14 = (f32[8,128]{1,0:T(8,128)S(1)}, f32[8,128]{1,0:T(8,128)S(1)}, u32[]{:S(2)}, u32[]{:S(2)}) collective-permute-start(f32[8,128]{1,0:T(8,128)S(1)} %add.24), channel_id=1, source_target_pairs={{0,4},{2,6},{4,0},{6,2},{1,5},{3,7},{5,1},{7,3},{8,12},{10,14},{12... | collective-permute-start | bytes 12296 | tf_op jit(solution)/shard_map/ppermute | solution.py:443
  40.1 4.5 %collective-permute-start.13 = (f32[8,128]{1,0:T(8,128)S(1)}, f32[8,128]{1,0:T(8,128)S(1)}, u32[]{:S(2)}, u32[]{:S(2)}) collective-permute-start(f32[8,128]{1,0:T(8,128)S(1)} %add.24), channel_id=1, source_target_pairs={{0,2},{2,0},{4,6},{6,4},{1,3},{3,1},{5,7},{7,5},{8,10},{10,8},{12,... | collective-permute-start | bytes 12296 | tf_op jit(solution)/shard_map/ppermute | solution.py:443

commit v4 on v3

--- a/solution.py
+++ b/solution.py
@@ -453,6 +453,18 @@
         value = value + lax.ppermute(value, axis, partner_perm(axis, by))
         by *= 2
     return value
+
+
+def det_sum(value):
+    count = lax.axis_size("det")
+    if lax.axis_size("tm") != 2 or count < 4 or count & (count - 1):
+        return sum(exchanged(value, "det"))
+    fetched = 0.0
+    for by in range(1, count // 2):
+        mixed = [(2 * z + t, 2 * (z ^ (count - by if t else by)) + t) for z in range(count) for t in range(2)]
+        fetched = fetched + lax.ppermute(value, ("det", "tm"), mixed)
+    across = lax.ppermute(value, "det", partner_perm("det", count // 2))
+    return value + across + fetched + lax.ppermute(fetched, "tm", partner_perm("tm", 1))
 
 
 def shards(map_solution, map_residual, map_direction, hits, stokes_int, inv_noise):
@@ -509,7 +521,7 @@
         ],
         [arrived, parts],
     )
-    sums = sum(exchanged(summed(sums, "tm"), "det"))
+    sums = det_sum(summed(sums, "tm"))
     return vmem_call(
         step_kernel,
         [jax.ShapeDtypeStruct(map_solution.shape, F32)] * 3,

time: 45.6 us -> 44.4 us (0.974)
  starting transfers between devices: 18.9 us -> 17.8 us
    ppermute x9 -> x6, starting transfers between devices: 11.5 us -> 7.11 us  [exchanged(): lax.ppermute(value, axis, partner_perm(axis, by))]
    ppermute x0 -> x3, starting transfers between devices: none -> 3.35 us  [the longest x1 2.31 us: det_sum(): across = lax.ppermute(value, 'det', partner_perm('det', count // 2))]
    ppermute x9 -> x6, waiting for transfers between devices: 5.94 us -> 3.84 us  [exchanged(): lax.ppermute(value, axis, partner_perm(axis, by))]
    ppermute x0 -> x3, waiting for transfers between devices: none -> 1.89 us  [the longest x1 1.07 us: det_sum(): fetched = fetched + lax.ppermute(value, ('det', 'tm'), mixed)]
  transfers between devices with their start and end apart: 16 -> 16, of which waited for: 13 -> 14; matrix products, arithmetic and copies ran while one was open for 0% -> 0% of each run, Pallas kernels for 5% -> 5%
where the time goes in v4:
time: 44.4 us; the launch traced here: 44.1 us
  starting transfers between devices  17.8 us (40%)
  waiting for transfers between devices  15 us (34%)
  Pallas kernels  7.31 us (16%)
  local copies, waits for them, and re-layouts  3.05 us (7%)
  between operations  0.76 us (2%)
    ppermute x6, starting transfers between devices, exchanged(): lax.ppermute(value, axis, partner_perm(axis, by))  7.11 us
    ppermute x2, starting transfers between devices, shards(): near = [lax.ppermute(own, 'det', tile_perm(e)) for e in (1, 0)]  5.12 us
    pallas_call x3, Pallas kernels, vmem_call(): pl.pallas_call(kernel, out_shape=out_shape, in_specs=[spec] * len(args),...  4.92 us
    ppermute x2, waiting for transfers between devices, shards(): pixels = pixels + lax.ppermute(half[1 + e], 'det', tile_perm(e))  4.59 us
    ppermute x6, waiting for transfers between devices, exchanged(): lax.ppermute(value, axis, partner_perm(axis, by))  3.84 us
    unnamed x14, local copies, waits for them, and re-layouts  3.01 us
    ppermute x1, starting transfers between devices, det_sum(): across = lax.ppermute(value, 'det', partner_perm('det', count // 2))  2.31 us
    pallas_call x1, Pallas kernels, prepare(): pl.pallas_call(prep_kernel, out_shape=out_shape, in_specs=[spec, spec, sp...  2.29 us
  transfers between devices with their start and end apart: 16, of which 14 were waited for; matrix products, arithmetic and copies ran while one was open for 0% of the time, Pallas kernels for 5%

profile of v4, /device:TPU:0, one launch (start us, length us, event | category | flops | bytes accessed | tf_op | source)
XLA Modules:
  0.0 44.1 jit_solution(14759658281880153469)
XLA Ops:
  0.6 5.1 %collective-permute-start.1 = (f32[3,8,128]{2,1,0:T(8,128)}, f32[3,8,128]{2,1,0:T(8,128)S(1)}, u32[]{:S(2)}, u32[]{:S(2)}) collective-permute-start(f32[3,8,128]{2,1,0:T(8,128)} %bitcast.46), channel_id=1, source_target_pairs={{0,6},{2,4},{4,2},{6,0},{1,7},{3,5},{5,3},{7,1},{8,14},{10,12},{12... | collective-permute-start | bytes 36872 | tf_op jit(solution)/shard_map/ppermute | solution.py:480
  5.8 1.6 %copy-done = s32[2,16,16384]{2,1,0:T(8,128)S(1)} copy-done((s32[2,16,16384]{2,1,0:T(8,128)S(1)}, s32[2,16,16384]{2,1,0:T(8,128)}, u32[]{:S(2)}) %copy-start) | copy-done | bytes 2097176
  7.3 0.7 %copy-done.3 = s32[16,128]{1,0:T(8,128)S(1)} copy-done((s32[16,128]{1,0:T(8,128)S(1)}, s32[16,128]{1,0:T(8,128)}, u32[]{:S(2)}) %copy-start.3) | copy-done | bytes 8216
  8.0 0.7 %copy-done.4 = f32[3,1,8,128]{3,2,1,0:T(8,128)S(1)} copy-done((f32[3,1,8,128]{3,2,1,0:T(8,128)S(1)}, f32[3,1,8,128]{3,2,1,0:T(8,128)}, u32[]{:S(2)}) %copy-start.4) | copy-done | bytes 12312
  8.9 0.8 %collective-permute-done = f32[3,8,128]{2,1,0:T(8,128)S(1)} collective-permute-done((f32[3,8,128]{2,1,0:T(8,128)}, f32[3,8,128]{2,1,0:T(8,128)S(1)}, u32[]{:S(2)}, u32[]{:S(2)}) %collective-permute-start) | collective-permute-done | bytes 12320 | tf_op jit(solution)/shard_map/ppermute | solution.py:480
  9.7 2.5 %collective-permute-start.4 = (f32[4,3,8,128]{3,2,1,0:T(8,128)S(1)}, f32[4,3,8,128]{3,2,1,0:T(8,128)S(1)}, u32[]{:S(2)}, u32[]{:S(2)}) collective-permute-start(f32[4,3,8,128]{3,2,1,0:T(8,128)S(1)} %pad_maximum_fusion.3.payload), channel_id=1, source_target_pairs={{0,24},{8,16},{16,8},{24,0},{1,25},{9,17},{17,9},{25,1},{2,26},{10... | collective-permute-start | bytes 147464 | tf_op jit(solution)/shard_map/ppermute | solution.py:443
  12.7 0.5 %collective-permute-start.2 = (f32[4,3,8,128]{3,2,1,0:T(8,128)S(1)}, f32[4,3,8,128]{3,2,1,0:T(8,128)S(1)}, u32[]{:S(2)}, u32[]{:S(2)}) collective-permute-start(f32[4,3,8,128]{3,2,1,0:T(8,128)S(1)} %pad_maximum_fusion.3.payload), channel_id=1, source_target_pairs={{0,8},{8,0},{16,24},{24,16},{1,9},{9,1},{17,25},{25,17},{2,10},{10... | collective-permute-start | bytes 147464 | tf_op jit(solution)/shard_map/ppermute | solution.py:443
  13.2 2.3 %shard_map.95 = (f32[4,3,8,128]{3,2,1,0:T(8,128)S(1)}, f32[2,16,16384]{2,1,0:T(8,128)S(1)}, bf16[2048,256]{1,0:T(8,128)(2,1)S(1)}, f32[16,896]{1,0:T(8,128)S(1)}, bf16[544,512]{1,0:T(8,128)(2,1)S(1)}) custom-call(f32[4,3,8,128]{3,2,1,0:T(8,128)S(1)} %pad_maximum_fusion.3.payload, s32[16,128]{1,0:T(8,128)S(1)} %copy-done.3, f32[16,512]{1,0:T(8,128)S(1)} %copy-done.2, ...), custom_call_target="tpu_custom_call" | custom-call | bytes 12000000 | tf_op jit(solution)/shard_map/pallas_call | solution.py:427
  15.5 0.7 %collective-permute-done.3 = f32[4,3,8,128]{3,2,1,0:T(8,128)S(1)} collective-permute-done((f32[4,3,8,128]{3,2,1,0:T(8,128)S(1)}, f32[4,3,8,128]{3,2,1,0:T(8,128)S(1)}, u32[]{:S(2)}, u32[]{:S(2)}) %collective-permute-start.3) | collective-permute-done | bytes 49184 | tf_op jit(solution)/shard_map/ppermute | solution.py:443
  16.9 1.5 %collective-permute-done.5 = f32[66,8,128]{2,1,0:T(8,128)S(1)} collective-permute-done((f32[66,8,128]{2,1,0:T(8,128)S(1)}, f32[66,8,128]{2,1,0:T(8,128)S(1)}, u32[]{:S(2)}, u32[]{:S(2)}) %collective-permute-start.5) | collective-permute-done | bytes 270368 | tf_op jit(solution)/shard_map/ppermute | solution.py:488
  18.5 4.2 %shard_map.96 = f32[2,3,4,8,384]{4,3,2,1,0:T(8,128)S(1)} custom-call(f32[4,4,3,8,128]{4,3,2,1,0:T(8,128)S(1)} %pad_maximum_fusion.1.arrived, f32[1,4,4,3,8,128]{5,4,3,2,1,0:T(8,128)S(1)} %bitcast.34, f32[2,16,16384]{2,1,0:T(8,128)S(1)} %get-tuple-element.15.weights, bf16[2048,256]{1,0:T(8,128)(2,1)S(1)} %get-tuple-element.16.onehot, ...), custom_call_target="tpu_custom_call" | custom-call | tf_op jit(solution)/shard_map/pallas_call | solution.py:385
  22.9 1.2 %collective-permute-done.6 = f32[3,4,8,384]{3,2,1,0:T(8,128)S(1)} collective-permute-done((f32[3,4,8,384]{3,2,1,0:T(8,128)S(1)}, f32[3,4,8,384]{3,2,1,0:T(8,128)S(1)}, u32[]{:S(2)}, u32[]{:S(2)}) %collective-permute-start.6) | collective-permute-done | bytes 147488 | tf_op jit(solution)/shard_map/ppermute | solution.py:511
  24.1 1.9 %collective-permute-start.7 = (f32[4,8,384]{2,1,0:T(8,128)S(1)}, f32[4,8,384]{2,1,0:T(8,128)S(1)}, u32[]{:S(2)}, u32[]{:S(2)}) collective-permute-start(f32[4,8,384]{2,1,0:T(8,128)S(1)} %get-tuple-element.21), channel_id=1, source_target_pairs={{0,6},{2,4},{4,2},{6,0},{1,7},{3,5},{5,3},{7,1},{8,14},{10,12},{12... | collective-permute-start | bytes 147464 | tf_op jit(solution)/shard_map/ppermute | solution.py:514
  26.0 4.4 %collective-permute-done.7 = f32[4,8,384]{2,1,0:T(8,128)S(1)} collective-permute-done((f32[4,8,384]{2,1,0:T(8,128)S(1)}, f32[4,8,384]{2,1,0:T(8,128)S(1)}, u32[]{:S(2)}, u32[]{:S(2)}) %collective-permute-start.7) | collective-permute-done | bytes 49184 | tf_op jit(solution)/shard_map/ppermute | solution.py:514
  30.6 1.6 %collective-permute-start.11 = (f32[4,8,384]{2,1,0:T(8,128)S(1)}, f32[4,8,384]{2,1,0:T(8,128)S(1)}, u32[]{:S(2)}, u32[]{:S(2)}) collective-permute-start(f32[4,8,384]{2,1,0:T(8,128)S(1)} %fusion.2), channel_id=1, source_target_pairs={{0,24},{8,16},{16,8},{24,0},{1,25},{9,17},{17,9},{25,1},{2,26},{10... | collective-permute-start | bytes 147464 | tf_op jit(solution)/shard_map/ppermute | solution.py:443
  32.7 1.5 %collective-permute-start.9 = (f32[4,8,384]{2,1,0:T(8,128)S(1)}, f32[4,8,384]{2,1,0:T(8,128)S(1)}, u32[]{:S(2)}, u32[]{:S(2)}) collective-permute-start(f32[4,8,384]{2,1,0:T(8,128)S(1)} %fusion.2), channel_id=1, source_target_pairs={{0,8},{8,0},{16,24},{24,16},{1,9},{9,1},{17,25},{25,17},{2,10},{10... | collective-permute-start | bytes 147464 | tf_op jit(solution)/shard_map/ppermute | solution.py:443
  34.2 1.6 %collective-permute-done.11 = f32[4,8,384]{2,1,0:T(8,128)S(1)} collective-permute-done((f32[4,8,384]{2,1,0:T(8,128)S(1)}, f32[4,8,384]{2,1,0:T(8,128)S(1)}, u32[]{:S(2)}, u32[]{:S(2)}) %collective-permute-start.11) | collective-permute-done | bytes 49184 | tf_op jit(solution)/shard_map/ppermute | solution.py:443
  35.7 0.5 %collective-permute-done.10 = f32[4,8,384]{2,1,0:T(8,128)S(1)} collective-permute-done((f32[4,8,384]{2,1,0:T(8,128)S(1)}, f32[4,8,384]{2,1,0:T(8,128)S(1)}, u32[]{:S(2)}, u32[]{:S(2)}) %collective-permute-start.10) | collective-permute-done | bytes 49184 | tf_op jit(solution)/shard_map/ppermute | solution.py:443
  37.0 1.2 %collective-permute-done.12 = f32[8,128]{1,0:T(8,128)S(1)} collective-permute-done((f32[8,128]{1,0:T(8,128)S(1)}, f32[8,128]{1,0:T(8,128)S(1)}, u32[]{:S(2)}, u32[]{:S(2)}) %collective-permute-start.12) | collective-permute-done | bytes 4128 | tf_op jit(solution)/shard_map/ppermute | solution.py:453
  38.3 2.3 %collective-permute-start.13 = (f32[8,128]{1,0:T(8,128)S(1)}, f32[8,128]{1,0:T(8,128)S(1)}, u32[]{:S(2)}, u32[]{:S(2)}) collective-permute-start(f32[8,128]{1,0:T(8,128)S(1)} %add.24), channel_id=1, source_target_pairs={{0,4},{2,6},{4,0},{6,2},{1,5},{3,7},{5,1},{7,3},{8,12},{10,14},{12... | collective-permute-start | bytes 12296 | tf_op jit(solution)/shard_map/ppermute | solution.py:466
  40.6 1.1 %collective-permute-done.14 = f32[8,128]{1,0:T(8,128)S(1)} collective-permute-done((f32[8,128]{1,0:T(8,128)S(1)}, f32[8,128]{1,0:T(8,128)S(1)}, u32[]{:S(2)}, u32[]{:S(2)}) %collective-permute-start.14) | collective-permute-done | bytes 4128 | tf_op jit(solution)/shard_map/ppermute | solution.py:465
  41.7 0.8 %collective-permute-start.15 = (f32[8,128]{1,0:T(8,128)S(1)}, f32[8,128]{1,0:T(8,128)S(1)}, u32[]{:S(2)}, u32[]{:S(2)}) collective-permute-start(f32[8,128]{1,0:T(8,128)S(1)} %collective-permute-done.14), channel_id=1, source_target_pairs={{0,1},{1,0},{2,3},{3,2},{4,5},{5,4},{6,7},{7,6},{8,9},{9,8},{10,11... | collective-permute-start | bytes 12296 | tf_op jit(solution)/shard_map/ppermute | solution.py:467
  42.8 0.5 %collective-permute-done.15 = f32[8,128]{1,0:T(8,128)S(1)} collective-permute-done((f32[8,128]{1,0:T(8,128)S(1)}, f32[8,128]{1,0:T(8,128)S(1)}, u32[]{:S(2)}, u32[]{:S(2)}) %collective-permute-start.15) | collective-permute-done | bytes 4128 | tf_op jit(solution)/shard_map/ppermute | solution.py:467
  43.4 0.7 %shard_map.98 = (f32[3,1,8,128]{3,2,1,0:T(8,128)}, f32[3,1,8,128]{3,2,1,0:T(8,128)}, f32[3,1,8,128]{3,2,1,0:T(8,128)}) custom-call(f32[8,128]{1,0:T(8,128)S(1)} %add_add_fusion.sums, f32[3,8,128]{2,1,0:T(8,128)S(1)} %get-tuple-element.20.image, f32[4,4,3,8,128]{4,3,2,1,0:T(8,128)S(1)} %pad_maximum_fusion.1.arrived, f32[3,1,8,128]{3,2,1,0:T(8,128)S(1)} %copy-done.5), custom_call_target="tpu_custom_call" | custom-call | tf_op jit(solution)/shard_map/pallas_call | solution.py:385
  (39 shorter events, 3.5 us)
Async XLA Ops:
  0.6 8.2 %collective-permute-start.1 = (f32[3,8,128]{2,1,0:T(8,128)}, f32[3,8,128]{2,1,0:T(8,128)S(1)}, u32[]{:S(2)}, u32[]{:S(2)}) collective-permute-start(f32[3,8,128]{2,1,0:T(8,128)} %bitcast.46), channel_id=1, source_target_pairs={{0,6},{2,4},{4,2},{6,0},{1,7},{3,5},{5,3},{7,1},{8,14},{10,12},{12... | collective-permute-start | bytes 36872 | tf_op jit(solution)/shard_map/ppermute | solution.py:480
  5.7 3.9 %collective-permute-start = (f32[3,8,128]{2,1,0:T(8,128)}, f32[3,8,128]{2,1,0:T(8,128)S(1)}, u32[]{:S(2)}, u32[]{:S(2)}) collective-permute-start(f32[3,8,128]{2,1,0:T(8,128)} %bitcast.47), channel_id=1, source_target_pairs={{0,2},{2,0},{4,6},{6,4},{1,3},{3,1},{5,7},{7,5},{8,10},{10,8},{12,... | collective-permute-start | bytes 36872 | tf_op jit(solution)/shard_map/ppermute | solution.py:480
  5.7 1.6 %copy-start = (s32[2,16,16384]{2,1,0:T(8,128)S(1)}, s32[2,16,16384]{2,1,0:T(8,128)}, u32[]{:S(2)}) copy-start(s32[2,16,16384]{2,1,0:T(8,128)} %stokes.3) | copy-start | bytes 6291460
  7.3 0.7 %copy-start.3 = (s32[16,128]{1,0:T(8,128)S(1)}, s32[16,128]{1,0:T(8,128)}, u32[]{:S(2)}) copy-start(s32[16,128]{1,0:T(8,128)} %hits.3) | copy-start | bytes 24580
  8.0 0.7 %copy-start.4 = (f32[3,1,8,128]{3,2,1,0:T(8,128)S(1)}, f32[3,1,8,128]{3,2,1,0:T(8,128)}, u32[]{:S(2)}) copy-start(f32[3,1,8,128]{3,2,1,0:T(8,128)} %residual.1) | copy-start | bytes 36868
  8.7 0.9 %copy-start.6 = (f32[3,1,8,128]{3,2,1,0:T(8,128)S(1)}, f32[3,1,8,128]{3,2,1,0:T(8,128)}, u32[]{:S(2)}) copy-start(f32[3,1,8,128]{3,2,1,0:T(8,128)} %param.9) | copy-start | bytes 36868
  8.7 4.5 %copy-start.1 = (bf16[544,512]{1,0:T(8,128)(2,1)S(1)}, bf16[544,512]{1,0:T(8,128)(2,1)}, u32[]{:S(2)}) copy-start(bf16[544,512]{1,0:T(8,128)(2,1)} %constant.2.clone.tables_in) | copy-start | bytes 1671172
  8.8 4.5 %copy-start.2 = (f32[16,512]{1,0:T(8,128)S(1)}, f32[16,512]{1,0:T(8,128)}, u32[]{:S(2)}) copy-start(f32[16,512]{1,0:T(8,128)} %inv_noise.1) | copy-start | bytes 98308
  9.7 5.9 %collective-permute-start.4 = (f32[4,3,8,128]{3,2,1,0:T(8,128)S(1)}, f32[4,3,8,128]{3,2,1,0:T(8,128)S(1)}, u32[]{:S(2)}, u32[]{:S(2)}) collective-permute-start(f32[4,3,8,128]{3,2,1,0:T(8,128)S(1)} %pad_maximum_fusion.3.payload), channel_id=1, source_target_pairs={{0,24},{8,16},{16,8},{24,0},{1,25},{9,17},{17,9},{25,1},{2,26},{10... | collective-permute-start | bytes 147464 | tf_op jit(solution)/shard_map/ppermute | solution.py:443
  12.2 4.1 %collective-permute-start.3 = (f32[4,3,8,128]{3,2,1,0:T(8,128)S(1)}, f32[4,3,8,128]{3,2,1,0:T(8,128)S(1)}, u32[]{:S(2)}, u32[]{:S(2)}) collective-permute-start(f32[4,3,8,128]{3,2,1,0:T(8,128)S(1)} %pad_maximum_fusion.3.payload), channel_id=1, source_target_pairs={{0,16},{8,24},{16,0},{24,8},{1,17},{9,25},{17,1},{25,9},{2,18},{10... | collective-permute-start | bytes 147464 | tf_op jit(solution)/shard_map/ppermute | solution.py:443
  12.7 4.1 %collective-permute-start.2 = (f32[4,3,8,128]{3,2,1,0:T(8,128)S(1)}, f32[4,3,8,128]{3,2,1,0:T(8,128)S(1)}, u32[]{:S(2)}, u32[]{:S(2)}) collective-permute-start(f32[4,3,8,128]{3,2,1,0:T(8,128)S(1)} %pad_maximum_fusion.3.payload), channel_id=1, source_target_pairs={{0,8},{8,0},{16,24},{24,16},{1,9},{9,1},{17,25},{25,17},{2,10},{10... | collective-permute-start | bytes 147464 | tf_op jit(solution)/shard_map/ppermute | solution.py:443
  16.8 1.6 %collective-permute-start.5 = (f32[66,8,128]{2,1,0:T(8,128)S(1)}, f32[66,8,128]{2,1,0:T(8,128)S(1)}, u32[]{:S(2)}, u32[]{:S(2)}) collective-permute-start(f32[66,8,128]{2,1,0:T(8,128)S(1)} %pad_maximum_fusion), channel_id=1, source_target_pairs={{0,1},{1,0},{2,3},{3,2},{4,5},{5,4},{6,7},{7,6},{8,9},{9,8},{10,11... | collective-permute-start | bytes 811016 | tf_op jit(solution)/shard_map/ppermute | solution.py:488
  18.5 24.9 %copy-start.5 = (f32[3,1,8,128]{3,2,1,0:T(8,128)S(1)}, f32[3,1,8,128]{3,2,1,0:T(8,128)}, u32[]{:S(2)}) copy-start(f32[3,1,8,128]{3,2,1,0:T(8,128)} %solution_in.1) | copy-start | bytes 36868
  22.6 1.4 %collective-permute-start.6 = (f32[3,4,8,384]{3,2,1,0:T(8,128)S(1)}, f32[3,4,8,384]{3,2,1,0:T(8,128)S(1)}, u32[]{:S(2)}, u32[]{:S(2)}) collective-permute-start(f32[3,4,8,384]{3,2,1,0:T(8,128)S(1)} %slice_bitcast_fusion), channel_id=1, source_target_pairs={{0,1},{1,0},{2,3},{3,2},{4,5},{5,4},{6,7},{7,6},{8,9},{9,8},{10,11... | collective-permute-start | bytes 442376 | tf_op jit(solution)/shard_map/ppermute | solution.py:511
  24.1 6.3 %collective-permute-start.7 = (f32[4,8,384]{2,1,0:T(8,128)S(1)}, f32[4,8,384]{2,1,0:T(8,128)S(1)}, u32[]{:S(2)}, u32[]{:S(2)}) collective-permute-start(f32[4,8,384]{2,1,0:T(8,128)S(1)} %get-tuple-element.21), channel_id=1, source_target_pairs={{0,6},{2,4},{4,2},{6,0},{1,7},{3,5},{5,3},{7,1},{8,14},{10,12},{12... | collective-permute-start | bytes 147464 | tf_op jit(solution)/shard_map/ppermute | solution.py:514
  26.0 4.6 %collective-permute-start.8 = (f32[4,8,384]{2,1,0:T(8,128)S(1)}, f32[4,8,384]{2,1,0:T(8,128)S(1)}, u32[]{:S(2)}, u32[]{:S(2)}) collective-permute-start(f32[4,8,384]{2,1,0:T(8,128)S(1)} %get-tuple-element.22), channel_id=1, source_target_pairs={{0,2},{2,0},{4,6},{6,4},{1,3},{3,1},{5,7},{7,5},{8,10},{10,8},{12,... | collective-permute-start | bytes 147464 | tf_op jit(solution)/shard_map/ppermute | solution.py:514
  30.6 5.1 %collective-permute-start.11 = (f32[4,8,384]{2,1,0:T(8,128)S(1)}, f32[4,8,384]{2,1,0:T(8,128)S(1)}, u32[]{:S(2)}, u32[]{:S(2)}) collective-permute-start(f32[4,8,384]{2,1,0:T(8,128)S(1)} %fusion.2), channel_id=1, source_target_pairs={{0,24},{8,16},{16,8},{24,0},{1,25},{9,17},{17,9},{25,1},{2,26},{10... | collective-permute-start | bytes 147464 | tf_op jit(solution)/shard_map/ppermute | solution.py:443
  32.2 4.1 %collective-permute-start.10 = (f32[4,8,384]{2,1,0:T(8,128)S(1)}, f32[4,8,384]{2,1,0:T(8,128)S(1)}, u32[]{:S(2)}, u32[]{:S(2)}) collective-permute-start(f32[4,8,384]{2,1,0:T(8,128)S(1)} %fusion.2), channel_id=1, source_target_pairs={{0,16},{8,24},{16,0},{24,8},{1,17},{9,25},{17,1},{25,9},{2,18},{10... | collective-permute-start | bytes 147464 | tf_op jit(solution)/shard_map/ppermute | solution.py:443
  32.7 4.1 %collective-permute-start.9 = (f32[4,8,384]{2,1,0:T(8,128)S(1)}, f32[4,8,384]{2,1,0:T(8,128)S(1)}, u32[]{:S(2)}, u32[]{:S(2)}) collective-permute-start(f32[4,8,384]{2,1,0:T(8,128)S(1)} %fusion.2), channel_id=1, source_target_pairs={{0,8},{8,0},{16,24},{24,16},{1,9},{9,1},{17,25},{25,17},{2,10},{10... | collective-permute-start | bytes 147464 | tf_op jit(solution)/shard_map/ppermute | solution.py:443
  36.9 1.2 %collective-permute-start.12 = (f32[8,128]{1,0:T(8,128)S(1)}, f32[8,128]{1,0:T(8,128)S(1)}, u32[]{:S(2)}, u32[]{:S(2)}) collective-permute-start(f32[8,128]{1,0:T(8,128)S(1)} %get-tuple-element.19), channel_id=1, source_target_pairs={{0,1},{1,0},{2,3},{3,2},{4,5},{5,4},{6,7},{7,6},{8,9},{9,8},{10,11... | collective-permute-start | bytes 12296 | tf_op jit(solution)/shard_map/ppermute | solution.py:453
  38.1 3.6 %collective-permute-start.14 = (f32[8,128]{1,0:T(8,128)S(1)}, f32[8,128]{1,0:T(8,128)S(1)}, u32[]{:S(2)}, u32[]{:S(2)}) collective-permute-start(f32[8,128]{1,0:T(8,128)S(1)} %add.24), channel_id=1, source_target_pairs={{0,2},{1,7},{2,0},{3,5},{4,6},{5,3},{6,4},{7,1},{8,10},{9,15},{10,... | collective-permute-start | bytes 12296 | tf_op jit(solution)/shard_map/ppermute | solution.py:465
  38.3 4.5 %collective-permute-start.13 = (f32[8,128]{1,0:T(8,128)S(1)}, f32[8,128]{1,0:T(8,128)S(1)}, u32[]{:S(2)}, u32[]{:S(2)}) collective-permute-start(f32[8,128]{1,0:T(8,128)S(1)} %add.24), channel_id=1, source_target_pairs={{0,4},{2,6},{4,0},{6,2},{1,5},{3,7},{5,1},{7,3},{8,12},{10,14},{12... | collective-permute-start | bytes 12296 | tf_op jit(solution)/shard_map/ppermute | solution.py:466
  41.7 1.6 %collective-permute-start.15 = (f32[8,128]{1,0:T(8,128)S(1)}, f32[8,128]{1,0:T(8,128)S(1)}, u32[]{:S(2)}, u32[]{:S(2)}) collective-permute-start(f32[8,128]{1,0:T(8,128)S(1)} %collective-permute-done.14), channel_id=1, source_target_pairs={{0,1},{1,0},{2,3},{3,2},{4,5},{5,4},{6,7},{7,6},{8,9},{9,8},{10,11... | collective-permute-start | bytes 12296 | tf_op jit(solution)/shard_map/ppermute | solution.py:467

commit v5 on v4

--- a/solution.py
+++ b/solution.py
@@ -207,10 +207,16 @@
 
     window[...] = jnp.zeros(window.shape, F32)
     for k in range(times):
+        core = source_of("tm", k)
+        if times == 2:
+            near = jnp.where(core == 0, tile_sides(1)[0], tile_sides(0)[0])
+            spots = [(1, core), (near, core), (near, 1 - core)]
+        else:
+            spots = [(tile, core) for tile in tiles]
         for j in range(groups):
-            at = (source_of("group", j) * times + source_of("tm", k)) * width
-            for s in range(3):
-                place = pl.ds(pl.multiple_of(tiles[s] * tile_blocks + at, 8), width)
+            for s, (tile, share) in enumerate(spots):
+                at = tile * tile_blocks + (source_of("group", j) * times + share) * width
+                place = pl.ds(pl.multiple_of(at, 8), width)
                 for c in range(3):
                     piece = arrived[j, s, c] if k == 0 else others[k - 1, j, s, c]
                     window[place, pl.ds(c * LANES, LANES)] = piece
@@ -378,6 +384,10 @@
         new_solution[c, 0] = solution_in[c, 0] + step_size * d
         new_residual[c, 0] = residual
         new_direction[c, 0] = residual + ratio * d
+
+
+def copy_kernel(source, target):
+    target[...] = source[:, 0]
 
 
 def vmem_call(kernel, out_shape, args, scratch=(), limit=24):
@@ -477,7 +487,14 @@
     segs = hits.shape[1] // PER_SEG
 
     own = map_direction[:, 0]
-    near = [lax.ppermute(own, "det", tile_perm(e)) for e in (1, 0)]
+    if times == 2:
+        mixed = [(2 * a + t, 2 * b + t) for t in range(2) for a, b in tile_perm(1 - t)]
+        other = lax.ppermute(own, "tm", partner_perm("tm", 1))
+        own = vmem_call(copy_kernel, jax.ShapeDtypeStruct(own.shape, F32), [map_direction])
+        pair = jnp.stack([own, other])
+        near = list(lax.ppermute(pair, ("det", "tm"), mixed))
+    else:
+        near = [lax.ppermute(own, "det", tile_perm(e)) for e in (1, 0)]
     *edge, residual = edges(hits, stokes_int, map_residual, 1 if times == 2 else 2)
     payload = jnp.stack([own] + near + [residual])
     from_group = exchanged(payload, "group")

time: 44.4 us -> 43.9 us (0.989)
  local copies, waits for them, and re-layouts: 3.05 us -> 3.75 us
  starting transfers between devices: 17.8 us -> 17.2 us
  waiting for transfers between devices: 15 us -> 14.4 us
    ppermute x2, starting transfers between devices: 5.12 us -> 3.43 us  [the longest x1 2.92 us: shards(): near = list(lax.ppermute(pair, ('det', 'tm'), mixed))]
    ppermute x2, starting transfers between devices: 1.9 us -> 2.99 us  [shards(): pixels = pixels + lax.ppermute(half[1 + e], 'det', tile_perm(e))]
    ppermute x2, waiting for transfers between devices: 4.59 us -> 3.72 us  [shards(): pixels = pixels + lax.ppermute(half[1 + e], 'det', tile_perm(e))]
    unnamed x14, local copies, waits for them, and re-layouts: 3.01 us -> 3.71 us
    ppermute x6, waiting for transfers between devices: 3.84 us -> 4.52 us  [exchanged(): lax.ppermute(value, axis, partner_perm(axis, by))]
    ppermute x1, starting transfers between devices: 2.31 us -> 1.84 us  [det_sum(): across = lax.ppermute(value, 'det', partner_perm('det', count // 2))]
    pallas_call x3 -> x4, Pallas kernels: 4.92 us -> 4.92 us  [vmem_call(): pl.pallas_call(kernel, out_shape=out_shape, in_specs=[spec] * len(args),...]
where the time goes in v5:
time: 43.9 us; the launch traced here: 43.5 us
  starting transfers between devices  17.2 us (39%)
  waiting for transfers between devices  14.4 us (33%)
  Pallas kernels  7.3 us (17%)
  local copies, waits for them, and re-layouts  3.75 us (9%)
  between operations  0.76 us (2%)
    ppermute x6, starting transfers between devices, exchanged(): lax.ppermute(value, axis, partner_perm(axis, by))  7.11 us
    pallas_call x4, Pallas kernels, vmem_call(): pl.pallas_call(kernel, out_shape=out_shape, in_specs=[spec] * len(args),...  4.92 us
    ppermute x6, waiting for transfers between devices, exchanged(): lax.ppermute(value, axis, partner_perm(axis, by))  4.52 us
    ppermute x2, waiting for transfers between devices, shards(): pixels = pixels + lax.ppermute(half[1 + e], 'det', tile_perm(e))  3.72 us
    unnamed x14, local copies, waits for them, and re-layouts  3.71 us
    ppermute x2, starting transfers between devices, shards(): pixels = pixels + lax.ppermute(half[1 + e], 'det', tile_perm(e))  2.99 us
    ppermute x1, starting transfers between devices, shards(): near = list(lax.ppermute(pair, ('det', 'tm'), mixed))  2.92 us
    pallas_call x1, Pallas kernels, prepare(): pl.pallas_call(prep_kernel, out_shape=out_shape, in_specs=[spec, spec, sp...  2.28 us
  transfers between devices with their start and end apart: 16, of which 14 were waited for; matrix products, arithmetic and copies ran while one was open for 0% of the time, Pallas kernels for 5%

profile of v5, /device:TPU:0, one launch (start us, length us, event | category | flops | bytes accessed | tf_op | source)
XLA Modules:
  0.0 43.5 jit_solution(16510487599671044752)
XLA Ops:
  1.2 0.7 %copy-done.6 = f32[3,1,8,128]{3,2,1,0:T(8,128)S(1)} copy-done((f32[3,1,8,128]{3,2,1,0:T(8,128)S(1)}, f32[3,1,8,128]{3,2,1,0:T(8,128)}, u32[]{:S(2)}) %copy-start.6) | copy-done | bytes 12312
  2.2 2.9 %collective-permute-start.1 = (f32[2,3,8,128]{3,2,1,0:T(8,128)S(1)}, f32[2,3,8,128]{3,2,1,0:T(8,128)S(1)}, u32[]{:S(2)}, u32[]{:S(2)}) collective-permute-start(f32[2,3,8,128]{3,2,1,0:T(8,128)S(1)} %pad_maximum_fusion.4), channel_id=1, source_target_pairs={{0,2},{2,0},{4,6},{6,4},{1,7},{3,5},{5,3},{7,1},{8,10},{10,8},{12,... | collective-permute-start | bytes 73736 | tf_op jit(solution)/shard_map/ppermute | solution.py:495
  5.1 1.6 %copy-done = s32[2,16,16384]{2,1,0:T(8,128)S(1)} copy-done((s32[2,16,16384]{2,1,0:T(8,128)S(1)}, s32[2,16,16384]{2,1,0:T(8,128)}, u32[]{:S(2)}) %copy-start) | copy-done | bytes 2097176
  6.7 0.7 %copy-done.3 = s32[16,128]{1,0:T(8,128)S(1)} copy-done((s32[16,128]{1,0:T(8,128)S(1)}, s32[16,128]{1,0:T(8,128)}, u32[]{:S(2)}) %copy-start.3) | copy-done | bytes 8216
  7.4 0.7 %copy-done.4 = f32[3,1,8,128]{3,2,1,0:T(8,128)S(1)} copy-done((f32[3,1,8,128]{3,2,1,0:T(8,128)S(1)}, f32[3,1,8,128]{3,2,1,0:T(8,128)}, u32[]{:S(2)}) %copy-start.4) | copy-done | bytes 12312
  8.3 2.5 %collective-permute-start.4 = (f32[4,3,8,128]{3,2,1,0:T(8,128)S(1)}, f32[4,3,8,128]{3,2,1,0:T(8,128)S(1)}, u32[]{:S(2)}, u32[]{:S(2)}) collective-permute-start(f32[4,3,8,128]{3,2,1,0:T(8,128)S(1)} %pad_maximum_fusion.3.payload), channel_id=1, source_target_pairs={{0,24},{8,16},{16,8},{24,0},{1,25},{9,17},{17,9},{25,1},{2,26},{10... | collective-permute-start | bytes 147464 | tf_op jit(solution)/shard_map/ppermute | solution.py:453
  11.8 2.3 %shard_map.96 = (f32[4,3,8,128]{3,2,1,0:T(8,128)S(1)}, f32[2,16,16384]{2,1,0:T(8,128)S(1)}, bf16[2048,256]{1,0:T(8,128)(2,1)S(1)}, f32[16,896]{1,0:T(8,128)S(1)}, bf16[544,512]{1,0:T(8,128)(2,1)S(1)}) custom-call(f32[4,3,8,128]{3,2,1,0:T(8,128)S(1)} %pad_maximum_fusion.3.payload, s32[16,128]{1,0:T(8,128)S(1)} %copy-done.3, f32[16,512]{1,0:T(8,128)S(1)} %copy-done.2, ...), custom_call_target="tpu_custom_call" | custom-call | bytes 12000000 | tf_op jit(solution)/shard_map/pallas_call | solution.py:437
  14.1 0.7 %collective-permute-done.3 = f32[4,3,8,128]{3,2,1,0:T(8,128)S(1)} collective-permute-done((f32[4,3,8,128]{3,2,1,0:T(8,128)S(1)}, f32[4,3,8,128]{3,2,1,0:T(8,128)S(1)}, u32[]{:S(2)}, u32[]{:S(2)}) %collective-permute-start.3) | collective-permute-done | bytes 49184 | tf_op jit(solution)/shard_map/ppermute | solution.py:453
  14.9 0.7 %collective-permute-done.2 = f32[4,3,8,128]{3,2,1,0:T(8,128)S(1)} collective-permute-done((f32[4,3,8,128]{3,2,1,0:T(8,128)S(1)}, f32[4,3,8,128]{3,2,1,0:T(8,128)S(1)}, u32[]{:S(2)}, u32[]{:S(2)}) %collective-permute-start.2) | collective-permute-done | bytes 49184 | tf_op jit(solution)/shard_map/ppermute | solution.py:453
  15.8 1.4 %collective-permute-done.5 = f32[66,8,128]{2,1,0:T(8,128)S(1)} collective-permute-done((f32[66,8,128]{2,1,0:T(8,128)S(1)}, f32[66,8,128]{2,1,0:T(8,128)S(1)}, u32[]{:S(2)}, u32[]{:S(2)}) %collective-permute-start.5) | collective-permute-done | bytes 270368 | tf_op jit(solution)/shard_map/ppermute | solution.py:505
  17.3 4.2 %shard_map.97 = f32[2,3,4,8,384]{4,3,2,1,0:T(8,128)S(1)} custom-call(f32[4,4,3,8,128]{4,3,2,1,0:T(8,128)S(1)} %pad_maximum_fusion.1.arrived, f32[1,4,4,3,8,128]{5,4,3,2,1,0:T(8,128)S(1)} %bitcast.33, f32[2,16,16384]{2,1,0:T(8,128)S(1)} %get-tuple-element.15.weights, bf16[2048,256]{1,0:T(8,128)(2,1)S(1)} %get-tuple-element.16.onehot, ...), custom_call_target="tpu_custom_call" | custom-call | tf_op jit(solution)/shard_map/pallas_call | solution.py:395
  21.7 1.2 %collective-permute-done.6 = f32[3,4,8,384]{3,2,1,0:T(8,128)S(1)} collective-permute-done((f32[3,4,8,384]{3,2,1,0:T(8,128)S(1)}, f32[3,4,8,384]{3,2,1,0:T(8,128)S(1)}, u32[]{:S(2)}, u32[]{:S(2)}) %collective-permute-start.6) | collective-permute-done | bytes 147488 | tf_op jit(solution)/shard_map/ppermute | solution.py:528
  22.9 2.5 %collective-permute-start.7 = (f32[4,8,384]{2,1,0:T(8,128)S(1)}, f32[4,8,384]{2,1,0:T(8,128)S(1)}, u32[]{:S(2)}, u32[]{:S(2)}) collective-permute-start(f32[4,8,384]{2,1,0:T(8,128)S(1)} %get-tuple-element.21), channel_id=1, source_target_pairs={{0,6},{2,4},{4,2},{6,0},{1,7},{3,5},{5,3},{7,1},{8,14},{10,12},{12... | collective-permute-start | bytes 147464 | tf_op jit(solution)/shard_map/ppermute | solution.py:531
  25.9 3.2 %collective-permute-done.7 = f32[4,8,384]{2,1,0:T(8,128)S(1)} collective-permute-done((f32[4,8,384]{2,1,0:T(8,128)S(1)}, f32[4,8,384]{2,1,0:T(8,128)S(1)}, u32[]{:S(2)}, u32[]{:S(2)}) %collective-permute-start.7) | collective-permute-done | bytes 49184 | tf_op jit(solution)/shard_map/ppermute | solution.py:531
  29.7 1.9 %collective-permute-start.11 = (f32[4,8,384]{2,1,0:T(8,128)S(1)}, f32[4,8,384]{2,1,0:T(8,128)S(1)}, u32[]{:S(2)}, u32[]{:S(2)}) collective-permute-start(f32[4,8,384]{2,1,0:T(8,128)S(1)} %fusion.2), channel_id=1, source_target_pairs={{0,24},{8,16},{16,8},{24,0},{1,25},{9,17},{17,9},{25,1},{2,26},{10... | collective-permute-start | bytes 147464 | tf_op jit(solution)/shard_map/ppermute | solution.py:453
  32.2 1.1 %collective-permute-start.9 = (f32[4,8,384]{2,1,0:T(8,128)S(1)}, f32[4,8,384]{2,1,0:T(8,128)S(1)}, u32[]{:S(2)}, u32[]{:S(2)}) collective-permute-start(f32[4,8,384]{2,1,0:T(8,128)S(1)} %fusion.2), channel_id=1, source_target_pairs={{0,8},{8,0},{16,24},{24,16},{1,9},{9,1},{17,25},{25,17},{2,10},{10... | collective-permute-start | bytes 147464 | tf_op jit(solution)/shard_map/ppermute | solution.py:453
  33.2 1.5 %collective-permute-done.11 = f32[4,8,384]{2,1,0:T(8,128)S(1)} collective-permute-done((f32[4,8,384]{2,1,0:T(8,128)S(1)}, f32[4,8,384]{2,1,0:T(8,128)S(1)}, u32[]{:S(2)}, u32[]{:S(2)}) %collective-permute-start.11) | collective-permute-done | bytes 49184 | tf_op jit(solution)/shard_map/ppermute | solution.py:453
  34.7 1.0 %collective-permute-done.10 = f32[4,8,384]{2,1,0:T(8,128)S(1)} collective-permute-done((f32[4,8,384]{2,1,0:T(8,128)S(1)}, f32[4,8,384]{2,1,0:T(8,128)S(1)}, u32[]{:S(2)}, u32[]{:S(2)}) %collective-permute-start.10) | collective-permute-done | bytes 49184 | tf_op jit(solution)/shard_map/ppermute | solution.py:453
  36.4 1.2 %collective-permute-done.12 = f32[8,128]{1,0:T(8,128)S(1)} collective-permute-done((f32[8,128]{1,0:T(8,128)S(1)}, f32[8,128]{1,0:T(8,128)S(1)}, u32[]{:S(2)}, u32[]{:S(2)}) %collective-permute-start.12) | collective-permute-done | bytes 4128 | tf_op jit(solution)/shard_map/ppermute | solution.py:463
  38.2 1.8 %collective-permute-start.13 = (f32[8,128]{1,0:T(8,128)S(1)}, f32[8,128]{1,0:T(8,128)S(1)}, u32[]{:S(2)}, u32[]{:S(2)}) collective-permute-start(f32[8,128]{1,0:T(8,128)S(1)} %add.24), channel_id=1, source_target_pairs={{0,4},{2,6},{4,0},{6,2},{1,5},{3,7},{5,1},{7,3},{8,12},{10,14},{12... | collective-permute-start | bytes 12296 | tf_op jit(solution)/shard_map/ppermute | solution.py:476
  40.0 1.2 %collective-permute-done.14 = f32[8,128]{1,0:T(8,128)S(1)} collective-permute-done((f32[8,128]{1,0:T(8,128)S(1)}, f32[8,128]{1,0:T(8,128)S(1)}, u32[]{:S(2)}, u32[]{:S(2)}) %collective-permute-start.14) | collective-permute-done | bytes 4128 | tf_op jit(solution)/shard_map/ppermute | solution.py:475
  41.2 0.8 %collective-permute-start.15 = (f32[8,128]{1,0:T(8,128)S(1)}, f32[8,128]{1,0:T(8,128)S(1)}, u32[]{:S(2)}, u32[]{:S(2)}) collective-permute-start(f32[8,128]{1,0:T(8,128)S(1)} %collective-permute-done.14), channel_id=1, source_target_pairs={{0,1},{1,0},{2,3},{3,2},{4,5},{5,4},{6,7},{7,6},{8,9},{9,8},{10,11... | collective-permute-start | bytes 12296 | tf_op jit(solution)/shard_map/ppermute | solution.py:477
  42.0 0.7 %collective-permute-done.13 = f32[8,128]{1,0:T(8,128)S(1)} collective-permute-done((f32[8,128]{1,0:T(8,128)S(1)}, f32[8,128]{1,0:T(8,128)S(1)}, u32[]{:S(2)}, u32[]{:S(2)}) %collective-permute-start.13) | collective-permute-done | bytes 4128 | tf_op jit(solution)/shard_map/ppermute | solution.py:476
  42.8 0.7 %shard_map.99 = (f32[3,1,8,128]{3,2,1,0:T(8,128)}, f32[3,1,8,128]{3,2,1,0:T(8,128)}, f32[3,1,8,128]{3,2,1,0:T(8,128)}) custom-call(f32[8,128]{1,0:T(8,128)S(1)} %add_add_fusion.sums, f32[3,8,128]{2,1,0:T(8,128)S(1)} %get-tuple-element.20.image, f32[4,4,3,8,128]{4,3,2,1,0:T(8,128)S(1)} %pad_maximum_fusion.1.arrived, f32[3,1,8,128]{3,2,1,0:T(8,128)S(1)} %copy-done.5), custom_call_target="tpu_custom_call" | custom-call | tf_op jit(solution)/shard_map/pallas_call | solution.py:395
  (41 shorter events, 5.6 us)
Async XLA Ops:
  0.6 11.2 %copy-start.2 = (f32[16,512]{1,0:T(8,128)S(1)}, f32[16,512]{1,0:T(8,128)}, u32[]{:S(2)}) copy-start(f32[16,512]{1,0:T(8,128)} %inv_noise.1) | copy-start | bytes 98308
  0.6 1.6 %collective-permute-start = (f32[3,8,128]{2,1,0:T(8,128)}, f32[3,8,128]{2,1,0:T(8,128)S(1)}, u32[]{:S(2)}, u32[]{:S(2)}) collective-permute-start(f32[3,8,128]{2,1,0:T(8,128)} %bitcast.40), channel_id=1, source_target_pairs={{0,1},{1,0},{2,3},{3,2},{4,5},{5,4},{6,7},{7,6},{8,9},{9,8},{10,11... | collective-permute-start | bytes 36872 | tf_op jit(solution)/shard_map/ppermute | solution.py:492
  1.2 0.7 %copy-start.6 = (f32[3,1,8,128]{3,2,1,0:T(8,128)S(1)}, f32[3,1,8,128]{3,2,1,0:T(8,128)}, u32[]{:S(2)}) copy-start(f32[3,1,8,128]{3,2,1,0:T(8,128)} %source.1) | copy-start | bytes 36868
  2.2 6.0 %collective-permute-start.1 = (f32[2,3,8,128]{3,2,1,0:T(8,128)S(1)}, f32[2,3,8,128]{3,2,1,0:T(8,128)S(1)}, u32[]{:S(2)}, u32[]{:S(2)}) collective-permute-start(f32[2,3,8,128]{3,2,1,0:T(8,128)S(1)} %pad_maximum_fusion.4), channel_id=1, source_target_pairs={{0,2},{2,0},{4,6},{6,4},{1,7},{3,5},{5,3},{7,1},{8,10},{10,8},{12,... | collective-permute-start | bytes 73736 | tf_op jit(solution)/shard_map/ppermute | solution.py:495
  5.1 1.6 %copy-start = (s32[2,16,16384]{2,1,0:T(8,128)S(1)}, s32[2,16,16384]{2,1,0:T(8,128)}, u32[]{:S(2)}) copy-start(s32[2,16,16384]{2,1,0:T(8,128)} %stokes.3) | copy-start | bytes 6291460
  6.7 0.7 %copy-start.3 = (s32[16,128]{1,0:T(8,128)S(1)}, s32[16,128]{1,0:T(8,128)}, u32[]{:S(2)}) copy-start(s32[16,128]{1,0:T(8,128)} %hits.3) | copy-start | bytes 24580
  7.4 0.7 %copy-start.4 = (f32[3,1,8,128]{3,2,1,0:T(8,128)S(1)}, f32[3,1,8,128]{3,2,1,0:T(8,128)}, u32[]{:S(2)}) copy-start(f32[3,1,8,128]{3,2,1,0:T(8,128)} %residual.1) | copy-start | bytes 36868
  8.1 3.7 %copy-start.1 = (bf16[544,512]{1,0:T(8,128)(2,1)S(1)}, bf16[544,512]{1,0:T(8,128)(2,1)}, u32[]{:S(2)}) copy-start(bf16[544,512]{1,0:T(8,128)(2,1)} %constant.2.clone.tables_in) | copy-start | bytes 1671172
  8.3 5.9 %collective-permute-start.4 = (f32[4,3,8,128]{3,2,1,0:T(8,128)S(1)}, f32[4,3,8,128]{3,2,1,0:T(8,128)S(1)}, u32[]{:S(2)}, u32[]{:S(2)}) collective-permute-start(f32[4,3,8,128]{3,2,1,0:T(8,128)S(1)} %pad_maximum_fusion.3.payload), channel_id=1, source_target_pairs={{0,24},{8,16},{16,8},{24,0},{1,25},{9,17},{17,9},{25,1},{2,26},{10... | collective-permute-start | bytes 147464 | tf_op jit(solution)/shard_map/ppermute | solution.py:453
  10.8 4.1 %collective-permute-start.3 = (f32[4,3,8,128]{3,2,1,0:T(8,128)S(1)}, f32[4,3,8,128]{3,2,1,0:T(8,128)S(1)}, u32[]{:S(2)}, u32[]{:S(2)}) collective-permute-start(f32[4,3,8,128]{3,2,1,0:T(8,128)S(1)} %pad_maximum_fusion.3.payload), channel_id=1, source_target_pairs={{0,16},{8,24},{16,0},{24,8},{1,17},{9,25},{17,1},{25,9},{2,18},{10... | collective-permute-start | bytes 147464 | tf_op jit(solution)/shard_map/ppermute | solution.py:453
  11.3 4.3 %collective-permute-start.2 = (f32[4,3,8,128]{3,2,1,0:T(8,128)S(1)}, f32[4,3,8,128]{3,2,1,0:T(8,128)S(1)}, u32[]{:S(2)}, u32[]{:S(2)}) collective-permute-start(f32[4,3,8,128]{3,2,1,0:T(8,128)S(1)} %pad_maximum_fusion.3.payload), channel_id=1, source_target_pairs={{0,8},{8,0},{16,24},{24,16},{1,9},{9,1},{17,25},{25,17},{2,10},{10... | collective-permute-start | bytes 147464 | tf_op jit(solution)/shard_map/ppermute | solution.py:453
  15.6 1.6 %collective-permute-start.5 = (f32[66,8,128]{2,1,0:T(8,128)S(1)}, f32[66,8,128]{2,1,0:T(8,128)S(1)}, u32[]{:S(2)}, u32[]{:S(2)}) collective-permute-start(f32[66,8,128]{2,1,0:T(8,128)S(1)} %pad_maximum_fusion), channel_id=1, source_target_pairs={{0,1},{1,0},{2,3},{3,2},{4,5},{5,4},{6,7},{7,6},{8,9},{9,8},{10,11... | collective-permute-start | bytes 811016 | tf_op jit(solution)/shard_map/ppermute | solution.py:505
  17.3 25.6 %copy-start.5 = (f32[3,1,8,128]{3,2,1,0:T(8,128)S(1)}, f32[3,1,8,128]{3,2,1,0:T(8,128)}, u32[]{:S(2)}) copy-start(f32[3,1,8,128]{3,2,1,0:T(8,128)} %solution_in.1) | copy-start | bytes 36868
  21.5 1.4 %collective-permute-start.6 = (f32[3,4,8,384]{3,2,1,0:T(8,128)S(1)}, f32[3,4,8,384]{3,2,1,0:T(8,128)S(1)}, u32[]{:S(2)}, u32[]{:S(2)}) collective-permute-start(f32[3,4,8,384]{3,2,1,0:T(8,128)S(1)} %slice_bitcast_fusion), channel_id=1, source_target_pairs={{0,1},{1,0},{2,3},{3,2},{4,5},{5,4},{6,7},{7,6},{8,9},{9,8},{10,11... | collective-permute-start | bytes 442376 | tf_op jit(solution)/shard_map/ppermute | solution.py:528
  22.9 6.2 %collective-permute-start.7 = (f32[4,8,384]{2,1,0:T(8,128)S(1)}, f32[4,8,384]{2,1,0:T(8,128)S(1)}, u32[]{:S(2)}, u32[]{:S(2)}) collective-permute-start(f32[4,8,384]{2,1,0:T(8,128)S(1)} %get-tuple-element.21), channel_id=1, source_target_pairs={{0,6},{2,4},{4,2},{6,0},{1,7},{3,5},{5,3},{7,1},{8,14},{10,12},{12... | collective-permute-start | bytes 147464 | tf_op jit(solution)/shard_map/ppermute | solution.py:531
  25.4 4.2 %collective-permute-start.8 = (f32[4,8,384]{2,1,0:T(8,128)S(1)}, f32[4,8,384]{2,1,0:T(8,128)S(1)}, u32[]{:S(2)}, u32[]{:S(2)}) collective-permute-start(f32[4,8,384]{2,1,0:T(8,128)S(1)} %get-tuple-element.22), channel_id=1, source_target_pairs={{0,2},{2,0},{4,6},{6,4},{1,3},{3,1},{5,7},{7,5},{8,10},{10,8},{12,... | collective-permute-start | bytes 147464 | tf_op jit(solution)/shard_map/ppermute | solution.py:531
  29.7 5.1 %collective-permute-start.11 = (f32[4,8,384]{2,1,0:T(8,128)S(1)}, f32[4,8,384]{2,1,0:T(8,128)S(1)}, u32[]{:S(2)}, u32[]{:S(2)}) collective-permute-start(f32[4,8,384]{2,1,0:T(8,128)S(1)} %fusion.2), channel_id=1, source_target_pairs={{0,24},{8,16},{16,8},{24,0},{1,25},{9,17},{17,9},{25,1},{2,26},{10... | collective-permute-start | bytes 147464 | tf_op jit(solution)/shard_map/ppermute | solution.py:453
  31.6 4.1 %collective-permute-start.10 = (f32[4,8,384]{2,1,0:T(8,128)S(1)}, f32[4,8,384]{2,1,0:T(8,128)S(1)}, u32[]{:S(2)}, u32[]{:S(2)}) collective-permute-start(f32[4,8,384]{2,1,0:T(8,128)S(1)} %fusion.2), channel_id=1, source_target_pairs={{0,16},{8,24},{16,0},{24,8},{1,17},{9,25},{17,1},{25,9},{2,18},{10... | collective-permute-start | bytes 147464 | tf_op jit(solution)/shard_map/ppermute | solution.py:453
  32.2 4.1 %collective-permute-start.9 = (f32[4,8,384]{2,1,0:T(8,128)S(1)}, f32[4,8,384]{2,1,0:T(8,128)S(1)}, u32[]{:S(2)}, u32[]{:S(2)}) collective-permute-start(f32[4,8,384]{2,1,0:T(8,128)S(1)} %fusion.2), channel_id=1, source_target_pairs={{0,8},{8,0},{16,24},{24,16},{1,9},{9,1},{17,25},{25,17},{2,10},{10... | collective-permute-start | bytes 147464 | tf_op jit(solution)/shard_map/ppermute | solution.py:453
  36.4 1.2 %collective-permute-start.12 = (f32[8,128]{1,0:T(8,128)S(1)}, f32[8,128]{1,0:T(8,128)S(1)}, u32[]{:S(2)}, u32[]{:S(2)}) collective-permute-start(f32[8,128]{1,0:T(8,128)S(1)} %get-tuple-element.19), channel_id=1, source_target_pairs={{0,1},{1,0},{2,3},{3,2},{4,5},{5,4},{6,7},{7,6},{8,9},{9,8},{10,11... | collective-permute-start | bytes 12296 | tf_op jit(solution)/shard_map/ppermute | solution.py:463
  37.6 3.6 %collective-permute-start.14 = (f32[8,128]{1,0:T(8,128)S(1)}, f32[8,128]{1,0:T(8,128)S(1)}, u32[]{:S(2)}, u32[]{:S(2)}) collective-permute-start(f32[8,128]{1,0:T(8,128)S(1)} %add.24), channel_id=1, source_target_pairs={{0,2},{1,7},{2,0},{3,5},{4,6},{5,3},{6,4},{7,1},{8,10},{9,15},{10,... | collective-permute-start | bytes 12296 | tf_op jit(solution)/shard_map/ppermute | solution.py:475
  38.2 4.5 %collective-permute-start.13 = (f32[8,128]{1,0:T(8,128)S(1)}, f32[8,128]{1,0:T(8,128)S(1)}, u32[]{:S(2)}, u32[]{:S(2)}) collective-permute-start(f32[8,128]{1,0:T(8,128)S(1)} %add.24), channel_id=1, source_target_pairs={{0,4},{2,6},{4,0},{6,2},{1,5},{3,7},{5,1},{7,3},{8,12},{10,14},{12... | collective-permute-start | bytes 12296 | tf_op jit(solution)/shard_map/ppermute | solution.py:476
  41.2 1.6 %collective-permute-start.15 = (f32[8,128]{1,0:T(8,128)S(1)}, f32[8,128]{1,0:T(8,128)S(1)}, u32[]{:S(2)}, u32[]{:S(2)}) collective-permute-start(f32[8,128]{1,0:T(8,128)S(1)} %collective-permute-done.14), channel_id=1, source_target_pairs={{0,1},{1,0},{2,3},{3,2},{4,5},{5,4},{6,7},{7,6},{8,9},{9,8},{10,11... | collective-permute-start | bytes 12296 | tf_op jit(solution)/shard_map/ppermute | solution.py:477

commit v6 on v5

--- a/solution.py
+++ b/solution.py
@@ -99,7 +99,9 @@
 
 def dot3(op, value, high, low):
     vh, vl = split(value)
-    return op(vh, high) + (op(vl, high) + op(vh, low))
+    axis = 0 if op is dot else 1
+    small = jnp.concatenate([high, low], axis=axis)
+    return op(vh, high) + op(jnp.concatenate([vl, vh], axis=1), small)
 
 
 def edge_kernel(count, hits, stokes, residual, *refs):

time: 43.9 us -> 43.8 us (level)
  transfers between devices with their start and end apart: 16 -> 16, of which waited for: 14 -> 14; matrix products, arithmetic and copies ran while one was open for 0% -> 0% of each run, Pallas kernels for 5% -> 6%
where the time goes in v6:
time: 43.8 us; the launch traced here: 43.4 us
  starting transfers between devices  17.2 us (39%)
  waiting for transfers between devices  14.4 us (33%)
  Pallas kernels  7.17 us (16%)
  local copies, waits for them, and re-layouts  3.75 us (9%)
  between operations  0.77 us (2%)
    ppermute x6, starting transfers between devices, exchanged(): lax.ppermute(value, axis, partner_perm(axis, by))  7.11 us
    pallas_call x4, Pallas kernels, vmem_call(): pl.pallas_call(kernel, out_shape=out_shape, in_specs=[spec] * len(args),...  4.79 us
    ppermute x6, waiting for transfers between devices, exchanged(): lax.ppermute(value, axis, partner_perm(axis, by))  4.51 us
    ppermute x2, waiting for transfers between devices, shards(): pixels = pixels + lax.ppermute(half[1 + e], 'det', tile_perm(e))  3.72 us
    unnamed x14, local copies, waits for them, and re-layouts  3.71 us
    ppermute x2, starting transfers between devices, shards(): pixels = pixels + lax.ppermute(half[1 + e], 'det', tile_perm(e))  2.99 us
    ppermute x1, starting transfers between devices, shards(): near = list(lax.ppermute(pair, ('det', 'tm'), mixed))  2.92 us
    pallas_call x1, Pallas kernels, prepare(): pl.pallas_call(prep_kernel, out_shape=out_shape, in_specs=[spec, spec, sp...  2.28 us
  transfers between devices with their start and end apart: 16, of which 14 were waited for; matrix products, arithmetic and copies ran while one was open for 0% of the time, Pallas kernels for 6%

profile of v6, /device:TPU:0, one launch (start us, length us, event | category | flops | bytes accessed | tf_op | source)
XLA Modules:
  0.0 43.4 jit_solution(16002008491297546291)
XLA Ops:
  1.2 0.7 %copy-done.6 = f32[3,1,8,128]{3,2,1,0:T(8,128)S(1)} copy-done((f32[3,1,8,128]{3,2,1,0:T(8,128)S(1)}, f32[3,1,8,128]{3,2,1,0:T(8,128)}, u32[]{:S(2)}) %copy-start.6) | copy-done | bytes 12312
  2.2 2.9 %collective-permute-start.1 = (f32[2,3,8,128]{3,2,1,0:T(8,128)S(1)}, f32[2,3,8,128]{3,2,1,0:T(8,128)S(1)}, u32[]{:S(2)}, u32[]{:S(2)}) collective-permute-start(f32[2,3,8,128]{3,2,1,0:T(8,128)S(1)} %pad_maximum_fusion.4), channel_id=1, source_target_pairs={{0,2},{2,0},{4,6},{6,4},{1,7},{3,5},{5,3},{7,1},{8,10},{10,8},{12,... | collective-permute-start | bytes 73736 | tf_op jit(solution)/shard_map/ppermute | solution.py:497
  5.1 1.6 %copy-done = s32[2,16,16384]{2,1,0:T(8,128)S(1)} copy-done((s32[2,16,16384]{2,1,0:T(8,128)S(1)}, s32[2,16,16384]{2,1,0:T(8,128)}, u32[]{:S(2)}) %copy-start) | copy-done | bytes 2097176
  6.7 0.7 %copy-done.3 = s32[16,128]{1,0:T(8,128)S(1)} copy-done((s32[16,128]{1,0:T(8,128)S(1)}, s32[16,128]{1,0:T(8,128)}, u32[]{:S(2)}) %copy-start.3) | copy-done | bytes 8216
  7.4 0.7 %copy-done.4 = f32[3,1,8,128]{3,2,1,0:T(8,128)S(1)} copy-done((f32[3,1,8,128]{3,2,1,0:T(8,128)S(1)}, f32[3,1,8,128]{3,2,1,0:T(8,128)}, u32[]{:S(2)}) %copy-start.4) | copy-done | bytes 12312
  8.3 2.5 %collective-permute-start.4 = (f32[4,3,8,128]{3,2,1,0:T(8,128)S(1)}, f32[4,3,8,128]{3,2,1,0:T(8,128)S(1)}, u32[]{:S(2)}, u32[]{:S(2)}) collective-permute-start(f32[4,3,8,128]{3,2,1,0:T(8,128)S(1)} %pad_maximum_fusion.3.payload), channel_id=1, source_target_pairs={{0,24},{8,16},{16,8},{24,0},{1,25},{9,17},{17,9},{25,1},{2,26},{10... | collective-permute-start | bytes 147464 | tf_op jit(solution)/shard_map/ppermute | solution.py:455
  11.8 2.3 %shard_map.96 = (f32[4,3,8,128]{3,2,1,0:T(8,128)S(1)}, f32[2,16,16384]{2,1,0:T(8,128)S(1)}, bf16[2048,256]{1,0:T(8,128)(2,1)S(1)}, f32[16,896]{1,0:T(8,128)S(1)}, bf16[544,512]{1,0:T(8,128)(2,1)S(1)}) custom-call(f32[4,3,8,128]{3,2,1,0:T(8,128)S(1)} %pad_maximum_fusion.3.payload, s32[16,128]{1,0:T(8,128)S(1)} %copy-done.3, f32[16,512]{1,0:T(8,128)S(1)} %copy-done.2, ...), custom_call_target="tpu_custom_call" | custom-call | bytes 12000000 | tf_op jit(solution)/shard_map/pallas_call | solution.py:439
  14.1 0.7 %collective-permute-done.3 = f32[4,3,8,128]{3,2,1,0:T(8,128)S(1)} collective-permute-done((f32[4,3,8,128]{3,2,1,0:T(8,128)S(1)}, f32[4,3,8,128]{3,2,1,0:T(8,128)S(1)}, u32[]{:S(2)}, u32[]{:S(2)}) %collective-permute-start.3) | collective-permute-done | bytes 49184 | tf_op jit(solution)/shard_map/ppermute | solution.py:455
  14.9 0.7 %collective-permute-done.2 = f32[4,3,8,128]{3,2,1,0:T(8,128)S(1)} collective-permute-done((f32[4,3,8,128]{3,2,1,0:T(8,128)S(1)}, f32[4,3,8,128]{3,2,1,0:T(8,128)S(1)}, u32[]{:S(2)}, u32[]{:S(2)}) %collective-permute-start.2) | collective-permute-done | bytes 49184 | tf_op jit(solution)/shard_map/ppermute | solution.py:455
  15.8 1.4 %collective-permute-done.5 = f32[66,8,128]{2,1,0:T(8,128)S(1)} collective-permute-done((f32[66,8,128]{2,1,0:T(8,128)S(1)}, f32[66,8,128]{2,1,0:T(8,128)S(1)}, u32[]{:S(2)}, u32[]{:S(2)}) %collective-permute-start.5) | collective-permute-done | bytes 270368 | tf_op jit(solution)/shard_map/ppermute | solution.py:507
  17.3 4.0 %shard_map.97 = f32[2,3,4,8,384]{4,3,2,1,0:T(8,128)S(1)} custom-call(f32[4,4,3,8,128]{4,3,2,1,0:T(8,128)S(1)} %pad_maximum_fusion.1.arrived, f32[1,4,4,3,8,128]{5,4,3,2,1,0:T(8,128)S(1)} %bitcast.33, f32[2,16,16384]{2,1,0:T(8,128)S(1)} %get-tuple-element.15.weights, bf16[2048,256]{1,0:T(8,128)(2,1)S(1)} %get-tuple-element.16.onehot, ...), custom_call_target="tpu_custom_call" | custom-call | tf_op jit(solution)/shard_map/pallas_call | solution.py:397
  21.5 1.2 %collective-permute-done.6 = f32[3,4,8,384]{3,2,1,0:T(8,128)S(1)} collective-permute-done((f32[3,4,8,384]{3,2,1,0:T(8,128)S(1)}, f32[3,4,8,384]{3,2,1,0:T(8,128)S(1)}, u32[]{:S(2)}, u32[]{:S(2)}) %collective-permute-start.6) | collective-permute-done | bytes 147488 | tf_op jit(solution)/shard_map/ppermute | solution.py:530
  22.8 2.5 %collective-permute-start.7 = (f32[4,8,384]{2,1,0:T(8,128)S(1)}, f32[4,8,384]{2,1,0:T(8,128)S(1)}, u32[]{:S(2)}, u32[]{:S(2)}) collective-permute-start(f32[4,8,384]{2,1,0:T(8,128)S(1)} %get-tuple-element.21), channel_id=1, source_target_pairs={{0,6},{2,4},{4,2},{6,0},{1,7},{3,5},{5,3},{7,1},{8,14},{10,12},{12... | collective-permute-start | bytes 147464 | tf_op jit(solution)/shard_map/ppermute | solution.py:533
  25.8 3.2 %collective-permute-done.7 = f32[4,8,384]{2,1,0:T(8,128)S(1)} collective-permute-done((f32[4,8,384]{2,1,0:T(8,128)S(1)}, f32[4,8,384]{2,1,0:T(8,128)S(1)}, u32[]{:S(2)}, u32[]{:S(2)}) %collective-permute-start.7) | collective-permute-done | bytes 49184 | tf_op jit(solution)/shard_map/ppermute | solution.py:533
  29.5 1.9 %collective-permute-start.11 = (f32[4,8,384]{2,1,0:T(8,128)S(1)}, f32[4,8,384]{2,1,0:T(8,128)S(1)}, u32[]{:S(2)}, u32[]{:S(2)}) collective-permute-start(f32[4,8,384]{2,1,0:T(8,128)S(1)} %fusion.2), channel_id=1, source_target_pairs={{0,24},{8,16},{16,8},{24,0},{1,25},{9,17},{17,9},{25,1},{2,26},{10... | collective-permute-start | bytes 147464 | tf_op jit(solution)/shard_map/ppermute | solution.py:455
  32.0 1.1 %collective-permute-start.9 = (f32[4,8,384]{2,1,0:T(8,128)S(1)}, f32[4,8,384]{2,1,0:T(8,128)S(1)}, u32[]{:S(2)}, u32[]{:S(2)}) collective-permute-start(f32[4,8,384]{2,1,0:T(8,128)S(1)} %fusion.2), channel_id=1, source_target_pairs={{0,8},{8,0},{16,24},{24,16},{1,9},{9,1},{17,25},{25,17},{2,10},{10... | collective-permute-start | bytes 147464 | tf_op jit(solution)/shard_map/ppermute | solution.py:455
  33.1 1.5 %collective-permute-done.11 = f32[4,8,384]{2,1,0:T(8,128)S(1)} collective-permute-done((f32[4,8,384]{2,1,0:T(8,128)S(1)}, f32[4,8,384]{2,1,0:T(8,128)S(1)}, u32[]{:S(2)}, u32[]{:S(2)}) %collective-permute-start.11) | collective-permute-done | bytes 49184 | tf_op jit(solution)/shard_map/ppermute | solution.py:455
  34.6 1.0 %collective-permute-done.10 = f32[4,8,384]{2,1,0:T(8,128)S(1)} collective-permute-done((f32[4,8,384]{2,1,0:T(8,128)S(1)}, f32[4,8,384]{2,1,0:T(8,128)S(1)}, u32[]{:S(2)}, u32[]{:S(2)}) %collective-permute-start.10) | collective-permute-done | bytes 49184 | tf_op jit(solution)/shard_map/ppermute | solution.py:455
  36.3 1.2 %collective-permute-done.12 = f32[8,128]{1,0:T(8,128)S(1)} collective-permute-done((f32[8,128]{1,0:T(8,128)S(1)}, f32[8,128]{1,0:T(8,128)S(1)}, u32[]{:S(2)}, u32[]{:S(2)}) %collective-permute-start.12) | collective-permute-done | bytes 4128 | tf_op jit(solution)/shard_map/ppermute | solution.py:465
  38.0 1.8 %collective-permute-start.13 = (f32[8,128]{1,0:T(8,128)S(1)}, f32[8,128]{1,0:T(8,128)S(1)}, u32[]{:S(2)}, u32[]{:S(2)}) collective-permute-start(f32[8,128]{1,0:T(8,128)S(1)} %add.24), channel_id=1, source_target_pairs={{0,4},{2,6},{4,0},{6,2},{1,5},{3,7},{5,1},{7,3},{8,12},{10,14},{12... | collective-permute-start | bytes 12296 | tf_op jit(solution)/shard_map/ppermute | solution.py:478
  39.9 1.2 %collective-permute-done.14 = f32[8,128]{1,0:T(8,128)S(1)} collective-permute-done((f32[8,128]{1,0:T(8,128)S(1)}, f32[8,128]{1,0:T(8,128)S(1)}, u32[]{:S(2)}, u32[]{:S(2)}) %collective-permute-start.14) | collective-permute-done | bytes 4128 | tf_op jit(solution)/shard_map/ppermute | solution.py:477
  41.1 0.8 %collective-permute-start.15 = (f32[8,128]{1,0:T(8,128)S(1)}, f32[8,128]{1,0:T(8,128)S(1)}, u32[]{:S(2)}, u32[]{:S(2)}) collective-permute-start(f32[8,128]{1,0:T(8,128)S(1)} %collective-permute-done.14), channel_id=1, source_target_pairs={{0,1},{1,0},{2,3},{3,2},{4,5},{5,4},{6,7},{7,6},{8,9},{9,8},{10,11... | collective-permute-start | bytes 12296 | tf_op jit(solution)/shard_map/ppermute | solution.py:479
  41.9 0.7 %collective-permute-done.13 = f32[8,128]{1,0:T(8,128)S(1)} collective-permute-done((f32[8,128]{1,0:T(8,128)S(1)}, f32[8,128]{1,0:T(8,128)S(1)}, u32[]{:S(2)}, u32[]{:S(2)}) %collective-permute-start.13) | collective-permute-done | bytes 4128 | tf_op jit(solution)/shard_map/ppermute | solution.py:478
  42.7 0.7 %shard_map.99 = (f32[3,1,8,128]{3,2,1,0:T(8,128)}, f32[3,1,8,128]{3,2,1,0:T(8,128)}, f32[3,1,8,128]{3,2,1,0:T(8,128)}) custom-call(f32[8,128]{1,0:T(8,128)S(1)} %add_add_fusion.sums, f32[3,8,128]{2,1,0:T(8,128)S(1)} %get-tuple-element.20.image, f32[4,4,3,8,128]{4,3,2,1,0:T(8,128)S(1)} %pad_maximum_fusion.1.arrived, f32[3,1,8,128]{3,2,1,0:T(8,128)S(1)} %copy-done.5), custom_call_target="tpu_custom_call" | custom-call | tf_op jit(solution)/shard_map/pallas_call | solution.py:397
  (41 shorter events, 5.6 us)
Async XLA Ops:
  0.6 11.2 %copy-start.2 = (f32[16,512]{1,0:T(8,128)S(1)}, f32[16,512]{1,0:T(8,128)}, u32[]{:S(2)}) copy-start(f32[16,512]{1,0:T(8,128)} %inv_noise.1) | copy-start | bytes 98308
  0.6 1.6 %collective-permute-start = (f32[3,8,128]{2,1,0:T(8,128)}, f32[3,8,128]{2,1,0:T(8,128)S(1)}, u32[]{:S(2)}, u32[]{:S(2)}) collective-permute-start(f32[3,8,128]{2,1,0:T(8,128)} %bitcast.40), channel_id=1, source_target_pairs={{0,1},{1,0},{2,3},{3,2},{4,5},{5,4},{6,7},{7,6},{8,9},{9,8},{10,11... | collective-permute-start | bytes 36872 | tf_op jit(solution)/shard_map/ppermute | solution.py:494
  1.2 0.7 %copy-start.6 = (f32[3,1,8,128]{3,2,1,0:T(8,128)S(1)}, f32[3,1,8,128]{3,2,1,0:T(8,128)}, u32[]{:S(2)}) copy-start(f32[3,1,8,128]{3,2,1,0:T(8,128)} %source.1) | copy-start | bytes 36868
  2.2 6.0 %collective-permute-start.1 = (f32[2,3,8,128]{3,2,1,0:T(8,128)S(1)}, f32[2,3,8,128]{3,2,1,0:T(8,128)S(1)}, u32[]{:S(2)}, u32[]{:S(2)}) collective-permute-start(f32[2,3,8,128]{3,2,1,0:T(8,128)S(1)} %pad_maximum_fusion.4), channel_id=1, source_target_pairs={{0,2},{2,0},{4,6},{6,4},{1,7},{3,5},{5,3},{7,1},{8,10},{10,8},{12,... | collective-permute-start | bytes 73736 | tf_op jit(solution)/shard_map/ppermute | solution.py:497
  5.1 1.6 %copy-start = (s32[2,16,16384]{2,1,0:T(8,128)S(1)}, s32[2,16,16384]{2,1,0:T(8,128)}, u32[]{:S(2)}) copy-start(s32[2,16,16384]{2,1,0:T(8,128)} %stokes.3) | copy-start | bytes 6291460
  6.7 0.7 %copy-start.3 = (s32[16,128]{1,0:T(8,128)S(1)}, s32[16,128]{1,0:T(8,128)}, u32[]{:S(2)}) copy-start(s32[16,128]{1,0:T(8,128)} %hits.3) | copy-start | bytes 24580
  7.4 0.7 %copy-start.4 = (f32[3,1,8,128]{3,2,1,0:T(8,128)S(1)}, f32[3,1,8,128]{3,2,1,0:T(8,128)}, u32[]{:S(2)}) copy-start(f32[3,1,8,128]{3,2,1,0:T(8,128)} %residual.1) | copy-start | bytes 36868
  8.1 3.7 %copy-start.1 = (bf16[544,512]{1,0:T(8,128)(2,1)S(1)}, bf16[544,512]{1,0:T(8,128)(2,1)}, u32[]{:S(2)}) copy-start(bf16[544,512]{1,0:T(8,128)(2,1)} %constant.2.clone.tables_in) | copy-start | bytes 1671172
  8.3 5.9 %collective-permute-start.4 = (f32[4,3,8,128]{3,2,1,0:T(8,128)S(1)}, f32[4,3,8,128]{3,2,1,0:T(8,128)S(1)}, u32[]{:S(2)}, u32[]{:S(2)}) collective-permute-start(f32[4,3,8,128]{3,2,1,0:T(8,128)S(1)} %pad_maximum_fusion.3.payload), channel_id=1, source_target_pairs={{0,24},{8,16},{16,8},{24,0},{1,25},{9,17},{17,9},{25,1},{2,26},{10... | collective-permute-start | bytes 147464 | tf_op jit(solution)/shard_map/ppermute | solution.py:455
  10.8 4.1 %collective-permute-start.3 = (f32[4,3,8,128]{3,2,1,0:T(8,128)S(1)}, f32[4,3,8,128]{3,2,1,0:T(8,128)S(1)}, u32[]{:S(2)}, u32[]{:S(2)}) collective-permute-start(f32[4,3,8,128]{3,2,1,0:T(8,128)S(1)} %pad_maximum_fusion.3.payload), channel_id=1, source_target_pairs={{0,16},{8,24},{16,0},{24,8},{1,17},{9,25},{17,1},{25,9},{2,18},{10... | collective-permute-start | bytes 147464 | tf_op jit(solution)/shard_map/ppermute | solution.py:455
  11.3 4.3 %collective-permute-start.2 = (f32[4,3,8,128]{3,2,1,0:T(8,128)S(1)}, f32[4,3,8,128]{3,2,1,0:T(8,128)S(1)}, u32[]{:S(2)}, u32[]{:S(2)}) collective-permute-start(f32[4,3,8,128]{3,2,1,0:T(8,128)S(1)} %pad_maximum_fusion.3.payload), channel_id=1, source_target_pairs={{0,8},{8,0},{16,24},{24,16},{1,9},{9,1},{17,25},{25,17},{2,10},{10... | collective-permute-start | bytes 147464 | tf_op jit(solution)/shard_map/ppermute | solution.py:455
  15.6 1.6 %collective-permute-start.5 = (f32[66,8,128]{2,1,0:T(8,128)S(1)}, f32[66,8,128]{2,1,0:T(8,128)S(1)}, u32[]{:S(2)}, u32[]{:S(2)}) collective-permute-start(f32[66,8,128]{2,1,0:T(8,128)S(1)} %pad_maximum_fusion), channel_id=1, source_target_pairs={{0,1},{1,0},{2,3},{3,2},{4,5},{5,4},{6,7},{7,6},{8,9},{9,8},{10,11... | collective-permute-start | bytes 811016 | tf_op jit(solution)/shard_map/ppermute | solution.py:507
  17.3 25.4 %copy-start.5 = (f32[3,1,8,128]{3,2,1,0:T(8,128)S(1)}, f32[3,1,8,128]{3,2,1,0:T(8,128)}, u32[]{:S(2)}) copy-start(f32[3,1,8,128]{3,2,1,0:T(8,128)} %solution_in.1) | copy-start | bytes 36868
  21.3 1.4 %collective-permute-start.6 = (f32[3,4,8,384]{3,2,1,0:T(8,128)S(1)}, f32[3,4,8,384]{3,2,1,0:T(8,128)S(1)}, u32[]{:S(2)}, u32[]{:S(2)}) collective-permute-start(f32[3,4,8,384]{3,2,1,0:T(8,128)S(1)} %slice_bitcast_fusion), channel_id=1, source_target_pairs={{0,1},{1,0},{2,3},{3,2},{4,5},{5,4},{6,7},{7,6},{8,9},{9,8},{10,11... | collective-permute-start | bytes 442376 | tf_op jit(solution)/shard_map/ppermute | solution.py:530
  22.8 6.2 %collective-permute-start.7 = (f32[4,8,384]{2,1,0:T(8,128)S(1)}, f32[4,8,384]{2,1,0:T(8,128)S(1)}, u32[]{:S(2)}, u32[]{:S(2)}) collective-permute-start(f32[4,8,384]{2,1,0:T(8,128)S(1)} %get-tuple-element.21), channel_id=1, source_target_pairs={{0,6},{2,4},{4,2},{6,0},{1,7},{3,5},{5,3},{7,1},{8,14},{10,12},{12... | collective-permute-start | bytes 147464 | tf_op jit(solution)/shard_map/ppermute | solution.py:533
  25.3 4.2 %collective-permute-start.8 = (f32[4,8,384]{2,1,0:T(8,128)S(1)}, f32[4,8,384]{2,1,0:T(8,128)S(1)}, u32[]{:S(2)}, u32[]{:S(2)}) collective-permute-start(f32[4,8,384]{2,1,0:T(8,128)S(1)} %get-tuple-element.22), channel_id=1, source_target_pairs={{0,2},{2,0},{4,6},{6,4},{1,3},{3,1},{5,7},{7,5},{8,10},{10,8},{12,... | collective-permute-start | bytes 147464 | tf_op jit(solution)/shard_map/ppermute | solution.py:533
  29.5 5.1 %collective-permute-start.11 = (f32[4,8,384]{2,1,0:T(8,128)S(1)}, f32[4,8,384]{2,1,0:T(8,128)S(1)}, u32[]{:S(2)}, u32[]{:S(2)}) collective-permute-start(f32[4,8,384]{2,1,0:T(8,128)S(1)} %fusion.2), channel_id=1, source_target_pairs={{0,24},{8,16},{16,8},{24,0},{1,25},{9,17},{17,9},{25,1},{2,26},{10... | collective-permute-start | bytes 147464 | tf_op jit(solution)/shard_map/ppermute | solution.py:455
  31.5 4.1 %collective-permute-start.10 = (f32[4,8,384]{2,1,0:T(8,128)S(1)}, f32[4,8,384]{2,1,0:T(8,128)S(1)}, u32[]{:S(2)}, u32[]{:S(2)}) collective-permute-start(f32[4,8,384]{2,1,0:T(8,128)S(1)} %fusion.2), channel_id=1, source_target_pairs={{0,16},{8,24},{16,0},{24,8},{1,17},{9,25},{17,1},{25,9},{2,18},{10... | collective-permute-start | bytes 147464 | tf_op jit(solution)/shard_map/ppermute | solution.py:455
  32.0 4.1 %collective-permute-start.9 = (f32[4,8,384]{2,1,0:T(8,128)S(1)}, f32[4,8,384]{2,1,0:T(8,128)S(1)}, u32[]{:S(2)}, u32[]{:S(2)}) collective-permute-start(f32[4,8,384]{2,1,0:T(8,128)S(1)} %fusion.2), channel_id=1, source_target_pairs={{0,8},{8,0},{16,24},{24,16},{1,9},{9,1},{17,25},{25,17},{2,10},{10... | collective-permute-start | bytes 147464 | tf_op jit(solution)/shard_map/ppermute | solution.py:455
  36.2 1.2 %collective-permute-start.12 = (f32[8,128]{1,0:T(8,128)S(1)}, f32[8,128]{1,0:T(8,128)S(1)}, u32[]{:S(2)}, u32[]{:S(2)}) collective-permute-start(f32[8,128]{1,0:T(8,128)S(1)} %get-tuple-element.19), channel_id=1, source_target_pairs={{0,1},{1,0},{2,3},{3,2},{4,5},{5,4},{6,7},{7,6},{8,9},{9,8},{10,11... | collective-permute-start | bytes 12296 | tf_op jit(solution)/shard_map/ppermute | solution.py:465
  37.5 3.6 %collective-permute-start.14 = (f32[8,128]{1,0:T(8,128)S(1)}, f32[8,128]{1,0:T(8,128)S(1)}, u32[]{:S(2)}, u32[]{:S(2)}) collective-permute-start(f32[8,128]{1,0:T(8,128)S(1)} %add.24), channel_id=1, source_target_pairs={{0,2},{1,7},{2,0},{3,5},{4,6},{5,3},{6,4},{7,1},{8,10},{9,15},{10,... | collective-permute-start | bytes 12296 | tf_op jit(solution)/shard_map/ppermute | solution.py:477
  38.0 4.5 %collective-permute-start.13 = (f32[8,128]{1,0:T(8,128)S(1)}, f32[8,128]{1,0:T(8,128)S(1)}, u32[]{:S(2)}, u32[]{:S(2)}) collective-permute-start(f32[8,128]{1,0:T(8,128)S(1)} %add.24), channel_id=1, source_target_pairs={{0,4},{2,6},{4,0},{6,2},{1,5},{3,7},{5,1},{7,3},{8,12},{10,14},{12... | collective-permute-start | bytes 12296 | tf_op jit(solution)/shard_map/ppermute | solution.py:478
  41.1 1.6 %collective-permute-start.15 = (f32[8,128]{1,0:T(8,128)S(1)}, f32[8,128]{1,0:T(8,128)S(1)}, u32[]{:S(2)}, u32[]{:S(2)}) collective-permute-start(f32[8,128]{1,0:T(8,128)S(1)} %collective-permute-done.14), channel_id=1, source_target_pairs={{0,1},{1,0},{2,3},{3,2},{4,5},{5,4},{6,7},{7,6},{8,9},{9,8},{10,11... | collective-permute-start | bytes 12296 | tf_op jit(solution)/shard_map/ppermute | solution.py:479
